TPU v7x, 32 devices: a whole 2x2x4 slice. The times are simulated.
32 devices in a mesh: batch: 4 (over y, x), seq: 8 (over z, core).
Axes of the slice: x: 2, y: 2, z: 4, core: 2. Of those that a mesh axis runs over, the one named last changes fastest.
Arguments:
- inputs: bfloat16 [4, 2048, 1024], P('batch', 'seq'), may hold values from -6 to 6
- out_grad: bfloat16 [4, 2048, 1024], P('batch', 'seq'), may hold values from -6 to 6
- row_lengths: int32 [4, 5], P('batch'), may hold values from 32 to 1920, as said below
- norm_gain: bfloat16 [1024], P('seq'), may hold values from 0.5 to 1.5
- w_gate: bfloat16 [1024, 1536], P('seq'), may hold values from -0.1875 to 0.1875
- w_in: bfloat16 [1024, 1536], P('seq'), may hold values from -0.1875 to 0.1875
- conv_w: bfloat16 [4, 1536], P(None, 'seq'), may hold values from -3 to 3
- conv_b: bfloat16 [1536], P('seq'), may hold values from -2 to 2
- w_rgate: bfloat16 [1536, 128], P('seq'), may hold values from -0.5 to 0.5
- b_rgate: bfloat16 [1536], P('seq'), may hold values from -4 to 4
- w_igate: bfloat16 [1536, 128], P('seq'), may hold values from -0.5 to 0.5
- b_igate: bfloat16 [1536], P('seq'), may hold values from -4 to 4
- lam: bfloat16 [1536], P('seq'), may hold values from 4 to 16
- w_out: bfloat16 [1536, 1024], P('seq'), may hold values from -0.4375 to 0.4375
- mlp_gain: bfloat16 [1024], P('seq'), may hold values from 0.5 to 1.5
- w_mlp_gate: bfloat16 [1024, 3072], P('seq'), may hold values from -0.1875 to 0.1875
- w_mlp_up: bfloat16 [1024, 3072], P('seq'), may hold values from -0.1875 to 0.1875
- w_mlp_down: bfloat16 [3072, 1024], P('seq'), may hold values from -0.21875 to 0.21875
Outputs:
- block_out: bfloat16 [4, 2048, 1024], P('batch', 'seq')
- input_grad: float32 [4, 2048, 1024], P('batch', 'seq')
- grad_norm_gain: float32 [1024], P('seq')
- grad_w_gate: float32 [1024, 1536], P('seq')
- grad_w_in: float32 [1024, 1536], P('seq')
- grad_conv_w: float32 [4, 1536], P(None, 'seq')
- grad_conv_b: float32 [1536], P('seq')
- grad_w_rgate: float32 [1536, 128], P('seq')
- grad_b_rgate: float32 [1536], P('seq')
- grad_w_igate: float32 [1536, 128], P('seq')
- grad_b_igate: float32 [1536], P('seq')
- grad_lam: float32 [1536], P('seq')
- grad_w_out: float32 [1536, 1024], P('seq')
- grad_mlp_gain: float32 [1024], P('seq')
- grad_w_mlp_gate: float32 [1024, 3072], P('seq')
- grad_w_mlp_up: float32 [1024, 3072], P('seq')
- grad_w_mlp_down: float32 [3072, 1024], P('seq')
- gate_mean: float32 [4, 5, 1536], P('batch')
Inputs may be any that keep to these rules, and one draw needn't show every extreme that they name: `row_lengths`: in each bucket rows 0, 1, 3 and 4 hold 32 to 96 tokens each and row 2 holds the rest of the 2048 positions; in one bucket rows 0, 1, 3 and 4 hold exactly 32 tokens each.
All inputs are finite; a program needn't handle non-finite values.
Results may differ from a plain program's by a relative error of at most 0.015.
Values may be sent and summed in bfloat16 or wider, within the bound.
A program may use at most 256 MiB of HBM per device.

v0:
```python
import jax
import jax.numpy as jnp
from jax import lax
from jax.sharding import PartitionSpec as P

NORM_EPS = 1e-06
DECAY_SCALE = 8.0


def shifted(value, axis, by):
    count = lax.axis_size(axis)
    pairs = [(i, i + by) for i in range(count) if 0 <= i + by < count]
    return lax.ppermute(value, axis, pairs)


def entering(value, axis, combine, identity, reverse):
    count, place = (lax.axis_size(axis), lax.axis_index(axis))
    everything = jax.tree.map(lambda part: lax.all_gather(part, axis), value)
    start = jax.tree.map(
        lambda part, zero: jnp.broadcast_to(jnp.asarray(zero, part.dtype), part.shape),
        value,
        identity,
    )

    def step(k, before):
        at = count - 1 - k if reverse else k
        reached = at > place if reverse else at < place
        new = combine(before, jax.tree.map(lambda part: part[at], everything))
        return jax.tree.map(lambda a, b: jnp.where(reached, a, b), new, before)

    return lax.fori_loop(0, count, step, start)


def rms_scale(values):
    return values * lax.rsqrt(jnp.mean(values * values, axis=-1, keepdims=True) + NORM_EPS)


def gelu_tanh(values):
    return jax.nn.gelu(values, approximate=True)


def link(earlier, later):
    return (earlier[0] * later[0], later[0] * earlier[1] + later[1])


def block_product(values, weight):
    count, channels = values.shape
    block_size = weight.shape[1]
    shaped = values.reshape(count, channels // block_size, block_size)
    result = jnp.einsum(
        "lni,nij->lnj",
        shaped,
        weight.reshape(channels // block_size, block_size, block_size),
        preferred_element_type=jnp.float32,
    )
    return result.reshape(count, channels)


def block_back(grads, weight):
    count, channels = grads.shape
    block_size = weight.shape[1]
    shaped = grads.reshape(count, channels // block_size, block_size)
    result = jnp.einsum(
        "lnj,nij->lni",
        shaped,
        weight.reshape(channels // block_size, block_size, block_size),
        preferred_element_type=jnp.float32,
    )
    return result.reshape(count, channels)


def block_weight_grad(values, grads, block_size):
    count, channels = values.shape
    left = values.reshape(count, channels // block_size, block_size)
    right = grads.reshape(count, channels // block_size, block_size)
    return jnp.einsum("lni,lnj->nij", left, right, preferred_element_type=jnp.float32).reshape(
        channels, block_size
    )


def recurrence_terms(conv_in, r_in, i_in, lam_in, restart):
    log_a = -DECAY_SCALE * jax.nn.sigmoid(r_in) * jax.nn.softplus(-lam_in)
    decays = jnp.exp(log_a)
    factor = jnp.where(restart[:, None] > 0, 1.0, jnp.sqrt(-jnp.expm1(2.0 * log_a)))
    return (decays * (1.0 - restart[:, None]), factor * jax.nn.sigmoid(i_in) * conv_in, decays)


def shards(
    inputs,
    out_grad,
    row_lengths,
    norm_gain,
    w_gate,
    w_in,
    conv_w,
    conv_b,
    w_rgate,
    b_rgate,
    w_igate,
    b_igate,
    lam,
    w_out,
    mlp_gain,
    w_mlp_gate,
    w_mlp_up,
    w_mlp_down,
):
    gathered = (
        lax.all_gather(norm_gain, "seq", axis=0, tiled=True),
        lax.all_gather(w_gate, "seq", axis=0, tiled=True),
        lax.all_gather(w_in, "seq", axis=0, tiled=True),
        lax.all_gather(conv_w, "seq", axis=1, tiled=True),
        lax.all_gather(conv_b, "seq", axis=0, tiled=True),
        lax.all_gather(w_rgate, "seq", axis=0, tiled=True),
        lax.all_gather(b_rgate, "seq", axis=0, tiled=True),
        lax.all_gather(w_igate, "seq", axis=0, tiled=True),
        lax.all_gather(b_igate, "seq", axis=0, tiled=True),
        lax.all_gather(lam, "seq", axis=0, tiled=True),
        lax.all_gather(w_out, "seq", axis=0, tiled=True),
        lax.all_gather(mlp_gain, "seq", axis=0, tiled=True),
        lax.all_gather(w_mlp_gate, "seq", axis=0, tiled=True),
        lax.all_gather(w_mlp_up, "seq", axis=0, tiled=True),
        lax.all_gather(w_mlp_down, "seq", axis=0, tiled=True),
    )
    gain_first = gathered[0].astype(jnp.float32)
    conv_taps = gathered[3].astype(jnp.float32)
    conv_bias = gathered[4].astype(jnp.float32)
    lam_value = gathered[9].astype(jnp.float32)
    gain_second = gathered[11].astype(jnp.float32)
    tokens = inputs[0].astype(jnp.float32)
    local_len = tokens.shape[0]
    channels = gathered[2].shape[1]
    block_size = gathered[5].shape[1]
    kernel_taps = conv_taps.shape[0]
    lengths = row_lengths[0]
    row_ends = jnp.cumsum(lengths)
    row_starts = row_ends - lengths
    positions = lax.axis_index("seq") * local_len + jnp.arange(local_len, dtype=jnp.int32)
    started = positions[:, None] >= row_starts[None, :]
    row_index = jnp.sum(started.astype(jnp.int32), axis=1) - 1
    row_first = jnp.max(jnp.where(started, row_starts[None, :], 0), axis=1)
    offset = positions - row_first
    restart = (offset == 0).astype(jnp.float32)
    members = (row_index[:, None] == jnp.arange(lengths.shape[0], dtype=jnp.int32)[None, :]).astype(
        jnp.float32
    )
    tap_masks = [(offset >= tap).astype(jnp.float32)[:, None] for tap in range(kernel_taps)]
    scaled, norm_pull = jax.vjp(rms_scale, tokens)
    normed = (scaled * gain_first).astype(jnp.bfloat16)
    gate_pre = jnp.dot(normed, gathered[1], preferred_element_type=jnp.float32)
    gate_branch, gate_pull = jax.vjp(gelu_tanh, gate_pre)
    inner = jnp.dot(normed, gathered[2], preferred_element_type=jnp.float32).astype(jnp.bfloat16)
    edge_rows = shifted(inner[local_len - kernel_taps + 1 :], "seq", 1)
    extended = jnp.concatenate([edge_rows, inner], axis=0).astype(jnp.float32)
    conv_sum = conv_bias + jnp.zeros((local_len, channels), jnp.float32)
    for tap in range(kernel_taps):
        start_row = kernel_taps - 1 - tap
        conv_sum = (
            conv_sum + conv_taps[tap] * extended[start_row : start_row + local_len] * tap_masks[tap]
        )
    conv_low = conv_sum.astype(jnp.bfloat16)
    conv_value = conv_low.astype(jnp.float32)
    r_pre = block_product(conv_low, gathered[5]) + gathered[6].astype(jnp.float32)
    i_pre = block_product(conv_low, gathered[7]) + gathered[8].astype(jnp.float32)

    def local_terms(conv_in, r_in, i_in, lam_in):
        return recurrence_terms(conv_in, r_in, i_in, lam_in, restart)

    (carried, drive_term, decays), recur_pull = jax.vjp(
        local_terms, conv_value, r_pre, i_pre, lam_value
    )
    prefix_decay, local_state = lax.associative_scan(link, (carried, drive_term), axis=0)
    identity = (jnp.ones((channels,), jnp.float32), jnp.zeros((channels,), jnp.float32))
    incoming = entering((prefix_decay[-1], local_state[-1]), "seq", link, identity, False)[1]
    states = local_state + prefix_decay * incoming
    mixed_low = (states * gate_branch).astype(jnp.bfloat16)
    residual = tokens + jnp.dot(mixed_low, gathered[10], preferred_element_type=jnp.float32)
    scaled_two, norm_pull_two = jax.vjp(rms_scale, residual)
    normed_two = (scaled_two * gain_second).astype(jnp.bfloat16)
    up_gate = jnp.dot(normed_two, gathered[12], preferred_element_type=jnp.float32)
    up_lin = jnp.dot(normed_two, gathered[13], preferred_element_type=jnp.float32)
    gelu_up, up_pull = jax.vjp(gelu_tanh, up_gate)
    hidden = (gelu_up * up_lin).astype(jnp.bfloat16)
    block_out = (
        residual + jnp.dot(hidden, gathered[14], preferred_element_type=jnp.float32)
    ).astype(jnp.bfloat16)
    row_sums = lax.psum(jnp.dot(members.T, decays, precision=lax.Precision.HIGHEST), "seq")
    gate_mean = row_sums / lengths.astype(jnp.float32)[:, None]
    grad_top = out_grad[0]
    grad_mdown = jnp.einsum("tf,td->fd", hidden, grad_top, preferred_element_type=jnp.float32)
    d_hidden = jnp.einsum("td,fd->tf", grad_top, gathered[14], preferred_element_type=jnp.float32)
    d_upgate = up_pull(d_hidden * up_lin)[0].astype(jnp.bfloat16)
    d_uplin = (d_hidden * gelu_up).astype(jnp.bfloat16)
    grad_mgate = jnp.einsum("td,tf->df", normed_two, d_upgate, preferred_element_type=jnp.float32)
    grad_mup = jnp.einsum("td,tf->df", normed_two, d_uplin, preferred_element_type=jnp.float32)
    d_normed_two = jnp.einsum(
        "tf,df->td", d_upgate, gathered[12], preferred_element_type=jnp.float32
    )
    d_normed_two = d_normed_two + jnp.einsum(
        "tf,df->td", d_uplin, gathered[13], preferred_element_type=jnp.float32
    )
    grad_mgain = jnp.sum(d_normed_two * scaled_two, axis=0)
    d_residual = grad_top.astype(jnp.float32) + norm_pull_two(d_normed_two * gain_second)[0]
    d_outlow = d_residual.astype(jnp.bfloat16)
    grad_outw = jnp.einsum("tr,td->rd", mixed_low, d_outlow, preferred_element_type=jnp.float32)
    d_mixed = jnp.einsum("td,rd->tr", d_outlow, gathered[10], preferred_element_type=jnp.float32)
    direct = d_mixed * gate_branch
    d_gatelow = gate_pull(d_mixed * states)[0].astype(jnp.bfloat16)
    grad_gatew = jnp.einsum("td,tr->dr", normed, d_gatelow, preferred_element_type=jnp.float32)
    next_decay = jnp.concatenate([carried[1:], jnp.ones((1, channels), jnp.float32)], axis=0)
    suffix_decay, local_grad = lax.associative_scan(
        link, (next_decay, direct), axis=0, reverse=True
    )
    arriving = entering(
        (carried[0] * suffix_decay[0], carried[0] * local_grad[0]), "seq", link, identity, True
    )[1]
    d_states = local_grad + suffix_decay * arriving
    previous = jnp.concatenate([incoming[None, :], states[:-1]], axis=0)
    grad_convval, d_rpre, d_ipre, grad_lambda = recur_pull(
        (d_states * previous, d_states, jnp.zeros_like(decays))
    )
    d_rlow = d_rpre.astype(jnp.bfloat16)
    d_ilow = d_ipre.astype(jnp.bfloat16)
    grad_rw = block_weight_grad(conv_low, d_rlow, block_size)
    grad_rb = jnp.sum(d_rlow.astype(jnp.float32), axis=0)
    grad_iw = block_weight_grad(conv_low, d_ilow, block_size)
    grad_ib = jnp.sum(d_ilow.astype(jnp.float32), axis=0)
    grad_convsum = grad_convval + block_back(d_rlow, gathered[5]) + block_back(d_ilow, gathered[7])
    grad_cb = jnp.sum(grad_convsum, axis=0)
    conv_again = gathered[3].astype(jnp.float32)
    grad_extended = jnp.zeros((local_len + kernel_taps - 1, channels), jnp.float32)
    tap_grads = []
    for tap in range(kernel_taps):
        start_row = kernel_taps - 1 - tap
        masked = grad_convsum * tap_masks[tap]
        tap_grads.append(jnp.sum(masked * extended[start_row : start_row + local_len], axis=0))
        grad_extended = grad_extended + jnp.pad(
            masked * conv_again[tap], ((start_row, tap), (0, 0))
        )
    grad_cw = jnp.stack(tap_grads)
    edge_grads = shifted(grad_extended[: kernel_taps - 1], "seq", -1)
    d_inner = (
        grad_extended[kernel_taps - 1 :]
        + jnp.pad(edge_grads, ((local_len - kernel_taps + 1, 0), (0, 0)))
    ).astype(jnp.bfloat16)
    grad_inw = jnp.einsum("td,tr->dr", normed, d_inner, preferred_element_type=jnp.float32)
    d_normed = jnp.einsum("tr,dr->td", d_gatelow, gathered[1], preferred_element_type=jnp.float32)
    d_normed = d_normed + jnp.einsum(
        "tr,dr->td", d_inner, gathered[2], preferred_element_type=jnp.float32
    )
    grad_gain = jnp.sum(d_normed * scaled, axis=0)
    d_tokens = d_residual + norm_pull(d_normed * gain_first)[0]
    shares = (
        lax.psum_scatter(grad_gain, "seq", scatter_dimension=0, tiled=True),
        lax.psum_scatter(grad_gatew, "seq", scatter_dimension=0, tiled=True),
        lax.psum_scatter(grad_inw, "seq", scatter_dimension=0, tiled=True),
        lax.psum_scatter(grad_cw, "seq", scatter_dimension=1, tiled=True),
        lax.psum_scatter(grad_cb, "seq", scatter_dimension=0, tiled=True),
        lax.psum_scatter(grad_rw, "seq", scatter_dimension=0, tiled=True),
        lax.psum_scatter(grad_rb, "seq", scatter_dimension=0, tiled=True),
        lax.psum_scatter(grad_iw, "seq", scatter_dimension=0, tiled=True),
        lax.psum_scatter(grad_ib, "seq", scatter_dimension=0, tiled=True),
        lax.psum_scatter(grad_lambda, "seq", scatter_dimension=0, tiled=True),
        lax.psum_scatter(grad_outw, "seq", scatter_dimension=0, tiled=True),
        lax.psum_scatter(grad_mgain, "seq", scatter_dimension=0, tiled=True),
        lax.psum_scatter(grad_mgate, "seq", scatter_dimension=0, tiled=True),
        lax.psum_scatter(grad_mup, "seq", scatter_dimension=0, tiled=True),
        lax.psum_scatter(grad_mdown, "seq", scatter_dimension=0, tiled=True),
    )
    totals = (
        lax.psum(shares[0].astype(jnp.bfloat16), "batch").astype(jnp.float32),
        lax.psum(shares[1].astype(jnp.bfloat16), "batch").astype(jnp.float32),
        lax.psum(shares[2].astype(jnp.bfloat16), "batch").astype(jnp.float32),
        lax.psum(shares[3].astype(jnp.bfloat16), "batch").astype(jnp.float32),
        lax.psum(shares[4].astype(jnp.bfloat16), "batch").astype(jnp.float32),
        lax.psum(shares[5].astype(jnp.bfloat16), "batch").astype(jnp.float32),
        lax.psum(shares[6].astype(jnp.bfloat16), "batch").astype(jnp.float32),
        lax.psum(shares[7].astype(jnp.bfloat16), "batch").astype(jnp.float32),
        lax.psum(shares[8].astype(jnp.bfloat16), "batch").astype(jnp.float32),
        lax.psum(shares[9].astype(jnp.bfloat16), "batch").astype(jnp.float32),
        lax.psum(shares[10].astype(jnp.bfloat16), "batch").astype(jnp.float32),
        lax.psum(shares[11].astype(jnp.bfloat16), "batch").astype(jnp.float32),
        lax.psum(shares[12].astype(jnp.bfloat16), "batch").astype(jnp.float32),
        lax.psum(shares[13].astype(jnp.bfloat16), "batch").astype(jnp.float32),
        lax.psum(shares[14].astype(jnp.bfloat16), "batch").astype(jnp.float32),
    )
    return (
        block_out[None],
        d_tokens[None],
        totals[0],
        totals[1],
        totals[2],
        totals[3],
        totals[4],
        totals[5],
        totals[6],
        totals[7],
        totals[8],
        totals[9],
        totals[10],
        totals[11],
        totals[12],
        totals[13],
        totals[14],
        gate_mean[None],
    )


def solution(mesh):
    in_specs = (
        P("batch", "seq", None),
        P("batch", "seq", None),
        P("batch", None),
        P("seq"),
        P("seq", None),
        P("seq", None),
        P(None, "seq"),
        P("seq"),
        P("seq", None),
        P("seq"),
        P("seq", None),
        P("seq"),
        P("seq"),
        P("seq", None),
        P("seq"),
        P("seq", None),
        P("seq", None),
        P("seq", None),
    )
    out_specs = (
        P("batch", "seq", None),
        P("batch", "seq", None),
        P("seq"),
        P("seq", None),
        P("seq", None),
        P(None, "seq"),
        P("seq"),
        P("seq", None),
        P("seq"),
        P("seq", None),
        P("seq"),
        P("seq"),
        P("seq", None),
        P("seq"),
        P("seq", None),
        P("seq", None),
        P("seq", None),
        P("batch", None, None),
    )
    return jax.shard_map(shards, mesh=mesh, in_specs=in_specs, out_specs=out_specs, check_vma=False)
```

profile of v0, /device:TPU:19, one launch (start us, length us, event | category | flops | bytes accessed | tf_op | source)
XLA Modules:
  0.0 1609.2 jit_solution(10546854070348652779)
XLA Ops:
  13.0 9.5 all-gather.1
  22.5 14.1 all-gather
  36.7 15.8 all_gather.63
  52.5 16.7 %all_gather.66 = bf16[1536,128]{1,0:T(8,128)(2,1)} all-gather(bf16[192,128]{1,0:T(8,128)(2,1)S(1)} %copy-done.88), channel_id=1, replica_groups=mesh['batch'=4,'seq'=8] {'seq'}, dimensions={0}, use_global_device_ids=true | all-gather | bytes 442368 | tf_op jit(solution)/shard_map/all_gather | solution.py:116
  71.5 22.0 %all-reduce.82 = (bf16[1536]{0:T(1024)(128)(2,1)S(1)}, bf16[1536]{0:T(1024)(128)(2,1)S(1)}, bf16[1536]{0:T(1024)(128)(2,1)S(1)}, bf16[1536]{0:T(1024)(128)(2,1)S(1)}) all-reduce(bf16[1536]{0:T(1024)(128)(2,1)S(1)} %dynamic-update-slice.2, bf16[1536]{0:T(1024)(128)(2,1)S(1)} %dynamic-update-slice, ...), channel_id=1, replica_groups=mesh['batch'=4,'seq'=8] {'seq'}, use_global_device_ids=true, to_apply=%add.73 | all-reduce | flops 6144 | bytes 24576
  101.0 10.0 all-gather.4
  125.7 5.4 convert_multiply_fusion.5
  327.4 5.2 pad.232
  332.6 5.2 pad.233
  338.7 14.9 all-gather.3
  355.7 5.1 pad.248
  360.9 5.1 pad.249
  366.8 14.0 all-gather.2
  380.8 6.9 slice.631
  387.6 6.9 slice.638
  394.5 6.9 slice.629
  402.7 7.2 multiply_convert_fusion.2
  415.1 6.4 fusion.110
  421.6 6.5 fusion.111
  428.0 9.9 multiply_convert_fusion
  437.9 5.8 fusion.112
  461.3 6.9 slice.633
  468.2 6.8 slice.635
  608.6 5.1 pad.281
  623.6 5.1 pad.265
  628.8 6.9 slice.691
  640.3 5.1 pad.264
  647.5 5.1 pad.280
  658.2 14.0 all-gather.6
  672.2 14.0 all-gather.5
  687.1 12.8 rev.9
  700.1 12.9 rev.8
  713.1 6.1 multiply_reduce_fusion
  739.8 5.9 multiply_reduce_fusion.4
  751.9 5.0 fusion.48
  774.2 7.8 fusion.116
  782.1 7.8 fusion.117
  790.9 7.7 fusion.42
  806.6 24.5 %all-reduce.81 = (bf16[1024]{0:T(1024)(128)(2,1)S(1)}, bf16[1536]{0:T(1024)(128)(2,1)S(1)}, bf16[1536]{0:T(1024)(128)(2,1)S(1)}, bf16[1536]{0:T(1024)(128)(2,1)S...) all-reduce(f32[1024]{0:T(1024)S(1)} %get-tuple-element.379, ...), channel_id=2, replica_groups=mesh['batch'=4,'seq'=8] {'seq'}, use_global_device_ids=true, to_apply=%region_11.12.clone | all-reduce | flops 15872 | bytes 110592
  841.8 72.1 %reduce-scatter.20.cloned.1.call-done = f32[192,1024]{1,0:T(8,128)} async-done(((f32[1536,1024]{1,0:T(8,128)}), f32[192,1024]{1,0:T(8,128)}) %reduce-scatter.20.cloned.1.call-update) | async-done | bytes 786448 | tf_op jit(solution)/shard_map/reduce_scatter | solution.py:264
  915.8 68.7 %reduce-scatter.12.cloned.1.call-done = f32[128,1536]{1,0:T(8,128)} async-done(((f32[1024,1536]{1,0:T(8,128)}), f32[128,1536]{1,0:T(8,128)}) %reduce-scatter.12.cloned.1.call-update) | async-done | bytes 786448 | tf_op jit(solution)/shard_map/reduce_scatter | solution.py:255
  986.4 68.6 %reduce-scatter.14.cloned.1.call-done = f32[128,1536]{1,0:T(8,128)} async-done(((f32[1024,1536]{1,0:T(8,128)}), f32[128,1536]{1,0:T(8,128)}) %reduce-scatter.14.cloned.1.call-update) | async-done | bytes 786448 | tf_op jit(solution)/shard_map/reduce_scatter | solution.py:256
  1056.9 128.1 %reduce-scatter.22.cloned.1.call-done = f32[128,3072]{1,0:T(8,128)} async-done(((f32[1024,3072]{1,0:T(8,128)}), f32[128,3072]{1,0:T(8,128)}) %reduce-scatter.22.cloned.1.call-update) | async-done | bytes 1572880 | tf_op jit(solution)/shard_map/reduce_scatter | solution.py:266
  1187.4 127.5 %reduce-scatter.24.cloned.1.call-done = f32[128,3072]{1,0:T(8,128)} async-done(((f32[1024,3072]{1,0:T(8,128)}), f32[128,3072]{1,0:T(8,128)}) %reduce-scatter.24.cloned.1.call-update) | async-done | bytes 1572880 | tf_op jit(solution)/shard_map/reduce_scatter | solution.py:267
  1317.3 127.5 %reduce-scatter.26.cloned.1.call-done = f32[384,1024]{1,0:T(8,128)} async-done(((f32[3072,1024]{1,0:T(8,128)}), f32[384,1024]{1,0:T(8,128)}) %reduce-scatter.26.cloned.1.call-update) | async-done | bytes 1572880 | tf_op jit(solution)/shard_map/reduce_scatter | solution.py:268
  1448.4 6.0 fusion.29
  1456.4 36.7 %all-reduce.88.cloned.1.call-done = (bf16[128]{0:T(256)(128)(2,1)}, bf16[4,192]{1,0:T(4,128)(2,1)}, bf16[192]{0:T(256)(128)(2,1)}, bf16[192,128]{1,0:T(8,128)(2,...) async-done(((bf16[128]{0:T(256)(128)(2,1)}, bf16[4,192]{1,0:T(4,128)(2,1)}, ...) | async-done | bytes 101904 | tf_op jit(solution)/shard_map/psum | solution.py:271
  1504.3 90.2 %all-reduce.90.cloned.1.call-done = (bf16[128,1536]{1,0:T(8,128)(2,1)}, bf16[128,1536]{1,0:T(8,128)(2,1)}, bf16[192,1024]{1,0:T(8,128)(2,1)}, bf16[128,3072]{1,0...) async-done(((bf16[128,1536]{1,0:T(8,128)(2,1)}, bf16[128,1536]{1,0:T(8,128)(2,1)}, bf16[192,1024]{1,0:T(8,128)(2,1)}, bf16[128,3072]{1,0:T(8,128)(2,1)}, ...) | async-done | bytes 3538960 | tf_op jit(solution)/shard_map/psum | solution.py:272
  (702 shorter events, 508.1 us)
Async XLA Ops:
  7.2 86.4 %all-gather.14.cloned.1.call-start = ((), (), s32[]{:S(2)}) async-start(), calls=%async_computation.9 | async-start | bytes 3538944 | tf_op jit(solution)/shard_map/all_gather | solution.py:111
  7.9 394.7 %all-gather.16.cloned.1.call-start = ((), (), s32[]{:S(2)}) async-start(), calls=%async_computation.10 | async-start | bytes 3538944 | tf_op jit(solution)/shard_map/all_gather | solution.py:110
  8.7 401.2 %all-gather.18.cloned.1.call-start = ((), (), s32[]{:S(2)}) async-start(), calls=%async_computation.11 | async-start | bytes 3538944 | tf_op jit(solution)/shard_map/all_gather | solution.py:119
  9.5 27.2 %copy-start.87 = (bf16[192,128]{1,0:T(8,128)(2,1)S(1)}, bf16[192,128]{1,0:T(8,128)(2,1)}, u32[]{:S(2)}) copy-start(bf16[192,128]{1,0:T(8,128)(2,1)} %param.30) | copy-start | bytes 147460
  9.5 43.0 %copy-start.88 = (bf16[192,128]{1,0:T(8,128)(2,1)S(1)}, bf16[192,128]{1,0:T(8,128)(2,1)}, u32[]{:S(2)}) copy-start(bf16[192,128]{1,0:T(8,128)(2,1)} %param.32) | copy-start | bytes 147460
  9.5 405.7 %all-gather.20.cloned.1.call-start = ((), (), s32[]{:S(2)}) async-start(), calls=%async_computation.12 | async-start | bytes 7077888 | tf_op jit(solution)/shard_map/all_gather | solution.py:121
  10.0 59.2 %copy-start.124 = (u32[32]{0:T(128)S(1)}, u32[32]{0:T(128)}, u32[]{:S(2)}) copy-start(u32[32]{0:T(128)} %constant.280) | copy-start | bytes 388
  10.1 60.4 %copy-start.131 = (bf16[192]{0:T(256)(128)(2,1)S(1)}, bf16[192]{0:T(256)(128)(2,1)}, u32[]{:S(2)}) copy-start(bf16[192]{0:T(256)(128)(2,1)} %param.29) | copy-start | bytes 1156
  10.1 60.7 %copy-start.132 = (bf16[192]{0:T(256)(128)(2,1)S(1)}, bf16[192]{0:T(256)(128)(2,1)}, u32[]{:S(2)}) copy-start(bf16[192]{0:T(256)(128)(2,1)} %param.31) | copy-start | bytes 1156
  10.1 60.9 %copy-start.133 = (bf16[192]{0:T(256)(128)(2,1)S(1)}, bf16[192]{0:T(256)(128)(2,1)}, u32[]{:S(2)}) copy-start(bf16[192]{0:T(256)(128)(2,1)} %param.34) | copy-start | bytes 1156
  10.1 61.2 %copy-start.134 = (bf16[192]{0:T(256)(128)(2,1)S(1)}, bf16[192]{0:T(256)(128)(2,1)}, u32[]{:S(2)}) copy-start(bf16[192]{0:T(256)(128)(2,1)} %param.33) | copy-start | bytes 1156
  10.1 411.4 %all-gather.22.cloned.1.call-start = ((), (), s32[]{:S(2)}) async-start(), calls=%async_computation.13 | async-start | bytes 7077888 | tf_op jit(solution)/shard_map/all_gather | solution.py:122
  10.7 417.3 %all-gather.24.cloned.1.call-start = ((), (), s32[]{:S(2)}) async-start(), calls=%async_computation.14 | async-start | bytes 7077888 | tf_op jit(solution)/shard_map/all_gather | solution.py:123
  11.3 823.4 %reduce-scatter.28.cloned.1.call-start = ((), (), s32[]{:S(2)}) async-start(), calls=%async_computation.23 | async-start | bytes 884736
  12.7 112.9 %copy-start.114 = (pred[256]{0:T(512)(128)(4,1)}, pred[256]{0:T(512)(128)(4,1)S(1)}, u32[]{:S(2)}) copy-start(pred[256]{0:T(512)(128)(4,1)S(1)} %get-tuple-element.443) | copy-start | bytes 772
  12.7 112.9 %copy-start.79 = (f32[256]{0:T(256)}, f32[256]{0:T(256)S(1)}, u32[]{:S(2)}) copy-start(f32[256]{0:T(256)S(1)} %get-tuple-element.534) | copy-start | bytes 3076
  12.8 112.9 %copy-start.81 = (f32[256]{0:T(256)}, f32[256]{0:T(256)S(1)}, u32[]{:S(2)}) copy-start(f32[256]{0:T(256)S(1)} %get-tuple-element.535) | copy-start | bytes 3076
  12.8 112.9 %copy-start.83 = (f32[256]{0:T(256)}, f32[256]{0:T(256)S(1)}, u32[]{:S(2)}) copy-start(f32[256]{0:T(256)S(1)} %get-tuple-element.536) | copy-start | bytes 3076
  12.8 112.9 %copy-start.85 = (f32[256]{0:T(256)}, f32[256]{0:T(256)S(1)}, u32[]{:S(2)}) copy-start(f32[256]{0:T(256)S(1)} %get-tuple-element.537) | copy-start | bytes 3076
  12.8 112.8 %copy-start.116 = (f32[256]{0:T(256)}, f32[256]{0:T(256)S(1)}, u32[]{:S(2)}) copy-start(f32[256]{0:T(256)S(1)} %fusion.80) | copy-start | bytes 3076
  13.0 57.5 %copy-start.118 = (f32[256]{0:T(256)}, f32[256]{0:T(256)S(1)}, u32[]{:S(2)}) copy-start(f32[256]{0:T(256)S(1)} %fusion.35) | copy-start | bytes 3076
  52.5 63.8 %copy-start.31 = (bf16[1536,128]{1,0:T(8,128)(2,1)}, bf16[1536,128]{1,0:T(8,128)(2,1)S(1)}, u32[]{:S(2)}) copy-start(bf16[1536,128]{1,0:T(8,128)(2,1)S(1)} %all_gather.63) | copy-start | bytes 1179652
  93.6 32.1 %copy-start.64 = (f32[1536]{0:T(1024)}, f32[1536]{0:T(1024)S(1)}, u32[]{:S(2)}) copy-start(f32[1536]{0:T(1024)S(1)} %broadcast_multiply_fusion) | copy-start | bytes 18436
  96.6 15.0 copy-start.45
  96.6 15.0 collective-permute-start
  100.9 24.8 %copy-start.56 = (f32[1536]{0:T(1024)}, f32[1536]{0:T(1024)S(1)}, u32[]{:S(2)}) copy-start(f32[1536]{0:T(1024)S(1)} %get-tuple-element.381) | copy-start | bytes 18436
  100.9 24.8 %copy-start.58 = (f32[1536]{0:T(1024)}, f32[1536]{0:T(1024)S(1)}, u32[]{:S(2)}) copy-start(f32[1536]{0:T(1024)S(1)} %get-tuple-element.382) | copy-start | bytes 18436
  100.9 24.8 %copy-start.60 = (f32[1536]{0:T(1024)}, f32[1536]{0:T(1024)S(1)}, u32[]{:S(2)}) copy-start(f32[1536]{0:T(1024)S(1)} %get-tuple-element.383) | copy-start | bytes 18436
  100.9 24.8 %copy-start.62 = (f32[1536]{0:T(1024)}, f32[1536]{0:T(1024)S(1)}, u32[]{:S(2)}) copy-start(f32[1536]{0:T(1024)S(1)} %get-tuple-element.384) | copy-start | bytes 18436
  101.0 24.8 %copy-start.70 = (f32[1536]{0:T(1024)}, f32[1536]{0:T(1024)S(1)}, u32[]{:S(2)}) copy-start(f32[1536]{0:T(1024)S(1)} %convert_element_type.240) | copy-start | bytes 18436
  101.0 24.8 %copy-start.66 = (f32[1536]{0:T(1024)}, f32[1536]{0:T(1024)S(1)}, u32[]{:S(2)}) copy-start(f32[1536]{0:T(1024)S(1)} %convert_element_type.251) | copy-start | bytes 18436
  101.0 24.7 %copy-start.68 = (f32[1536]{0:T(1024)}, f32[1536]{0:T(1024)S(1)}, u32[]{:S(2)}) copy-start(f32[1536]{0:T(1024)S(1)} %convert_element_type.253) | copy-start | bytes 18436
  332.6 21.0 %copy-start.93 = (f32[1,1536]{1,0:T(1,128)S(1)}, f32[1,1536]{1,0:T(1,128)}, u32[]{:S(2)}) copy-start(f32[1,1536]{1,0:T(1,128)} %slice.746) | copy-start | bytes 18436
  544.3 14.3 copy-start.103
  544.3 14.9 copy-start.76
  544.4 14.9 copy-start.77
  656.9 29.3 %copy-start.55 = (f32[1536]{0:T(1024)S(1)}, f32[1536]{0:T(1024)}, u32[]{:S(2)}) copy-start(f32[1536]{0:T(1024)} %custom-call.1) | copy-start | bytes 18436
  746.9 89.2 %reduce-scatter.16.cloned.1.call-start = ((), (), s32[]{:S(2)}) async-start(), calls=%async_computation.17 | async-start | bytes 884736 | tf_op jit(solution)/shard_map/reduce_scatter | solution.py:259
  749.5 90.6 %reduce-scatter.18.cloned.1.call-start = ((), (), s32[]{:S(2)}) async-start(), calls=%async_computation.18 | async-start | bytes 884736 | tf_op jit(solution)/shard_map/reduce_scatter | solution.py:261
  750.8 163.1 %reduce-scatter.20.cloned.1.call-start = ((), (), s32[]{:S(2)}) async-start(), calls=%async_computation.19 | async-start | bytes 7077888 | tf_op jit(solution)/shard_map/reduce_scatter | solution.py:264
  756.9 227.6 %reduce-scatter.12.cloned.1.call-start = ((), (), s32[]{:S(2)}) async-start(), calls=%async_computation.15 | async-start | bytes 7077888 | tf_op jit(solution)/shard_map/reduce_scatter | solution.py:255
  761.9 293.1 %reduce-scatter.14.cloned.1.call-start = ((), (), s32[]{:S(2)}) async-start(), calls=%async_computation.16 | async-start | bytes 7077888 | tf_op jit(solution)/shard_map/reduce_scatter | solution.py:256
  764.0 5.4 collective-permute-start.1
  773.1 411.9 %reduce-scatter.22.cloned.1.call-start = ((), (), s32[]{:S(2)}) async-start(), calls=%async_computation.20 | async-start | bytes 14155776 | tf_op jit(solution)/shard_map/reduce_scatter | solution.py:266
  782.0 532.9 %reduce-scatter.24.cloned.1.call-start = ((), (), s32[]{:S(2)}) async-start(), calls=%async_computation.21 | async-start | bytes 14155776 | tf_op jit(solution)/shard_map/reduce_scatter | solution.py:267
  789.9 654.8 %reduce-scatter.26.cloned.1.call-start = ((), (), s32[]{:S(2)}) async-start(), calls=%async_computation.22 | async-start | bytes 14155776 | tf_op jit(solution)/shard_map/reduce_scatter | solution.py:268
  798.7 694.4 %all-reduce.88.cloned.1.call-start = ((), (), s32[]{:S(2)}) async-start(), calls=%async_computation.24 | async-start | bytes 206848 | tf_op jit(solution)/shard_map/psum | solution.py:271
  841.6 752.9 %all-reduce.90.cloned.1.call-start = ((), (), s32[]{:S(2)}) async-start(), calls=%async_computation.25 | async-start | bytes 7077888 | tf_op jit(solution)/shard_map/psum | solution.py:272
  (106 other events, 647.8 us)
Sparse Core Ops, SparseCore 0:
  9.7 41.2 all-gather.13
  52.6 38.7 all-gather.15
  93.0 37.2 all-gather.17
  131.9 63.4 all-gather.19
  196.8 63.3 all-gather.21
  261.7 63.3 all-gather.23
  747.1 27.1 reduce-scatter.27
  777.2 29.7 reduce-scatter.15
  809.9 30.1 reduce-scatter.17
  842.3 71.5 reduce-scatter.19
  916.3 68.1 reduce-scatter.11
  986.8 68.1 reduce-scatter.13
  1057.4 127.5 reduce-scatter.21
  1187.3 127.5 reduce-scatter.23
  1317.1 127.5 reduce-scatter.25
  1450.2 42.9 all-reduce.87
  1497.9 96.5 all-reduce.89
where the time goes:
time: 1630 us; the launch traced here: 1610 us
  waiting for transfers between devices  728 us (45%)
  local copies, waits for them, and re-layouts  402 us (25%)
  other arithmetic  175 us (11%)
  blocking collectives  169 us (10%)
  matrix products  108 us (7%)
  between operations  17.8 us (1%)
    slice x57, local copies, waits for them, and re-layouts, shards(): lax.associative_scan(link, (next_decay, direct), axis=0, reverse=True)  131 us
    reduce_scatter x1, waiting for transfers between devices, shards(): lax.psum_scatter(grad_mgate, 'seq', scatter_dimension=0, tiled=True)  128 us
    reduce_scatter x1, waiting for transfers between devices, shards(): lax.psum_scatter(grad_mup, 'seq', scatter_dimension=0, tiled=True)  127 us
    reduce_scatter x1, waiting for transfers between devices, shards(): lax.psum_scatter(grad_mdown, 'seq', scatter_dimension=0, tiled=True)  127 us
    slice x52, local copies, waits for them, and re-layouts, shards(): lax.associative_scan(link, (carried, drive_term), axis=0)  91 us
    psum x1, waiting for transfers between devices, shards(): lax.psum(shares[1].astype(jnp.bfloat16), 'batch').astype(jnp.float32)  90.2 us
    reduce_scatter x1, waiting for transfers between devices, shards(): lax.psum_scatter(grad_outw, 'seq', scatter_dimension=0, tiled=True)  72.1 us
    reduce_scatter x1, waiting for transfers between devices, shards(): lax.psum_scatter(grad_gatew, 'seq', scatter_dimension=0, tiled=True)  68.7 us
  transfers between devices with their start and end apart: 19, of which 10 were waited for; matrix products, arithmetic and copies ran while one was open for 23% of the time, Pallas kernels for 0%

commit v1 on v0

--- a/solution.py
+++ b/solution.py
@@ -1,10 +1,1182 @@
+import functools
+import types
+
 import jax
 import jax.numpy as jnp
 from jax import lax
+from jax.experimental import pallas as pl
+from jax.experimental.pallas import tpu as pltpu
 from jax.sharding import PartitionSpec as P
 
 NORM_EPS = 1e-06
 DECAY_SCALE = 8.0
+BF = jnp.bfloat16
+F32 = jnp.float32
+GELU_SCALE = 0.7978845608028654
+GELU_CUBE = 0.044715
+TILE = 64
+NN = (((1,), (0,)), ((), ()))
+NT = (((1,), (1,)), ((), ()))
+TN = (((0,), (0,)), ((), ()))
+
+
+def dot(left, right, dims=NN):
+    return lax.dot_general(left, right, dims, preferred_element_type=F32)
+
+
+def loop(count, body):
+    def step(i, carry):
+        body(i)
+        return carry
+
+    lax.fori_loop(0, count, step, 0)
+
+
+class Net:
+    def __init__(self, send, recv):
+        self.send, self.recv, self.count = send, recv, 0
+        self.pending = []
+        self.p = lax.axis_index("batch")
+        self.q = lax.axis_index("seq")
+        self.z = lax.div(self.q, 2)
+        self.c = lax.rem(self.q, 2)
+        self.o = 1 - self.c
+        p = self.p
+        self.near = (p, p + 1 - 2 * lax.rem(p, 2), lax.rem(p + 2, 4), 3 - p)
+
+    def plane(self, k, core):
+        return {"batch": self.near[k], "seq": self.z * 2 + core}
+
+    def line(self, z, core):
+        return {"batch": self.p, "seq": z * 2 + core}
+
+    def up(self, k):
+        return lax.rem(self.z + k, 4)
+
+    def down(self, k):
+        return lax.rem(self.z + 4 - k, 4)
+
+    def slot(self, k, core):
+        return self.near[k] * 2 + core
+
+    def greet(self):
+        barrier = pltpu.get_barrier_semaphore()
+        partners = [self.plane(k, core) for k in (1, 2, 3) for core in (0, 1)]
+        partners += [self.line(self.up(k), core) for k in (1, 2, 3) for core in (0, 1)]
+        partners += [self.line(self.z, self.o)]
+        for partner in partners:
+            pl.semaphore_signal(barrier, inc=1, device_id=partner, device_id_type=pl.DeviceIdType.MESH)
+        pl.semaphore_wait(barrier, len(partners))
+
+    def reserve(self, count):
+        first = self.count
+        self.count += count
+        return first
+
+    def describe(self, src, dst, device, send_at, recv_at):
+        return pltpu.make_async_remote_copy(
+            src_ref=src,
+            dst_ref=dst,
+            send_sem=self.send.at[send_at],
+            recv_sem=self.recv.at[recv_at],
+            device_id=device,
+            device_id_type=pl.DeviceIdType.MESH,
+        )
+
+    def copy(self, src, dst, device):
+        at = self.reserve(1)
+        made = self.describe(src, dst, device, at, at)
+        made.start()
+        self.pending.append(made)
+        return made
+
+    def drain(self):
+        for made in self.pending:
+            made.wait_send()
+        self.pending = []
+
+
+class Gather:
+    def __init__(self, net, own, everything):
+        self.net, self.own, self.all = net, own, everything
+        self.half = own.shape[0] // 2
+
+    def part(self, slot, h):
+        return self.all.at[slot, pl.ds(h * self.half, self.half)]
+
+    def start(self):
+        net = self.net
+        mine = net.slot(0, net.c)
+        low, high = self.own.at[pl.ds(0, self.half)], self.own.at[pl.ds(self.half, self.half)]
+        self.x0 = net.copy(low, self.part(mine, 0), net.plane(1, net.c))
+        self.y1 = net.copy(high, self.part(mine, 1), net.plane(2, net.c))
+        self.x1 = net.copy(high, self.part(mine, 1), net.plane(1, net.c))
+        self.y0 = net.copy(low, self.part(mine, 0), net.plane(2, net.c))
+        self.s = [net.copy(self.own, self.all.at[mine], net.plane(0, net.o))]
+
+    def forward(self):
+        net = self.net
+        self.x0.wait_recv()
+        mine = self.part(net.slot(1, net.c), 0)
+        self.d0 = net.copy(mine, mine, net.plane(2, net.c))
+        self.y1.wait_recv()
+        mine = self.part(net.slot(2, net.c), 1)
+        self.d1 = net.copy(mine, mine, net.plane(1, net.c))
+
+    def across(self, k):
+        net = self.net
+        mine = self.all.at[net.slot(k, net.c)]
+        self.s.append(net.copy(mine, mine, net.plane(0, net.o)))
+
+    def middle(self):
+        self.x1.wait_recv()
+        self.across(1)
+        self.y0.wait_recv()
+        self.across(2)
+
+    def last(self):
+        self.d0.wait_recv()
+        self.d1.wait_recv()
+        self.across(3)
+
+    def sibling(self, k):
+        self.s[k].wait_recv()
+
+
+class Reduce:
+    def __init__(self, net, r):
+        self.net = net
+        self.keep, self.out, self.into = r.rs_keep, r.rs_out, r.rs_in
+        self.xs, self.ys, self.xr, self.yr = r.rs_xs, r.rs_ys, r.rs_xr, r.rs_yr
+        self.rows = self.keep.shape[1]
+        self.half = self.rows // 2
+        self.cross = [None] * 4
+
+    def put_own(self, k, value):
+        self.keep[k] = value
+
+    def put_other(self, k, value):
+        net = self.net
+        self.out[k] = value.astype(BF)
+        self.cross[k] = net.copy(self.out.at[k], self.into.at[k], net.plane(0, net.o))
+
+    def merge(self, k):
+        self.cross[k].wait_recv()
+        step = 32
+
+        def body(i):
+            rows = pl.ds(pl.multiple_of(i * step, step), step)
+            self.keep[k, rows, :] = self.keep[k, rows, :] + self.into[k, rows, :].astype(F32)
+
+        loop(self.rows // step, body)
+
+    def low(self, dst, j, k, h, extra=None):
+        step = 32
+
+        def body(i):
+            rows = pl.ds(pl.multiple_of(i * step, step), step)
+            source = pl.ds(pl.multiple_of(h * self.half + i * step, step), step)
+            value = self.keep[k, source, :]
+            if extra is not None:
+                value = value + extra[0, rows, :].astype(F32)
+            dst[j, rows, :] = value.astype(BF)
+
+        loop(self.half // step, body)
+
+    def send(self, src, dst, j, k):
+        net = self.net
+        return net.copy(src.at[j], dst.at[j], net.plane(k, net.c))
+
+    def far(self):
+        self.merge(3)
+        self.low(self.xs, 0, 3, 0)
+        self.x0 = self.send(self.xs, self.xr, 0, 1)
+        self.low(self.ys, 0, 3, 1)
+        self.y0 = self.send(self.ys, self.yr, 0, 2)
+
+    def near_x(self):
+        self.merge(1)
+        self.low(self.xs, 1, 1, 0)
+        self.x1 = self.send(self.xs, self.xr, 1, 1)
+
+    def near_y(self):
+        self.merge(2)
+        self.low(self.ys, 1, 2, 1)
+        self.y1 = self.send(self.ys, self.yr, 1, 2)
+
+    def relay(self):
+        self.x0.wait_recv()
+        self.low(self.ys, 2, 2, 0, self.xr)
+        self.y2 = self.send(self.ys, self.yr, 2, 2)
+        self.y0.wait_recv()
+        self.low(self.xs, 2, 1, 1, self.yr)
+        self.x2 = self.send(self.xs, self.xr, 2, 1)
+
+    def finish(self):
+        self.merge(0)
+        for made in (self.x1, self.y1, self.x2, self.y2):
+            made.wait_recv()
+
+    def total(self, h, i, step):
+        rows = pl.ds(pl.multiple_of(i * step, step), step)
+        source = pl.ds(pl.multiple_of(h * self.half + i * step, step), step)
+        first, second = (self.xr, self.yr) if h == 0 else (self.yr, self.xr)
+        return (
+            self.keep[0, source, :] + first[1, rows, :].astype(F32) + second[2, rows, :].astype(F32)
+        )
+
+
+def reduce_scratch(rows, width):
+    half = rows // 2
+    return dict(
+        rs_keep=pltpu.VMEM((4, rows, width), F32),
+        rs_out=pltpu.VMEM((4, rows, width), BF),
+        rs_in=pltpu.VMEM((4, rows, width), BF),
+        rs_xs=pltpu.VMEM((3, half, width), BF),
+        rs_ys=pltpu.VMEM((3, half, width), BF),
+        rs_xr=pltpu.VMEM((3, half, width), BF),
+        rs_yr=pltpu.VMEM((3, half, width), BF),
+    )
+
+
+def kernel_call(body, ins, outs, scratch, copies, cid):
+    names = list(ins) + list(outs) + list(scratch)
+    spec = pl.BlockSpec(memory_space=pltpu.VMEM)
+    shapes = list(scratch.values())
+    remote = copies > 0
+    if remote:
+        names += ["send", "recv"]
+        shapes += [pltpu.SemaphoreType.DMA((copies,)), pltpu.SemaphoreType.DMA((copies,))]
+
+    def kernel(*refs):
+        body(types.SimpleNamespace(**dict(zip(names, refs))))
+
+    params = dict(vmem_limit_bytes=61 * 2**20)
+    if remote:
+        params.update(collective_id=cid, has_side_effects=True)
+    results = pl.pallas_call(
+        kernel,
+        out_shape=list(outs.values()),
+        in_specs=[spec] * len(ins),
+        out_specs=[spec] * len(outs),
+        scratch_shapes=shapes,
+        compiler_params=pltpu.CompilerParams(**params),
+        name=body.__name__,
+    )(*ins.values())
+    return dict(zip(outs, results))
+
+
+def array(*shape, dtype=F32):
+    return jax.ShapeDtypeStruct(shape, dtype)
+
+
+def gelu_parts(v):
+    square = v * v
+    t = jnp.tanh(GELU_SCALE * v * (1.0 + GELU_CUBE * square))
+    half = 0.5 + 0.5 * t
+    slope = half + 0.5 * v * (1.0 - t * t) * (GELU_SCALE * (1.0 + 3.0 * GELU_CUBE * square))
+    return v * half, slope
+
+
+def decay_parts(sr, rate):
+    log_a = -DECAY_SCALE * sr * rate
+    a = jnp.exp(log_a)
+    y = 2.0 * log_a
+    series = 1.0 + y * (1 / 6) * (1.0 + y * (1 / 7))
+    for n in (5, 4, 3, 2):
+        series = 1.0 + y * (1 / n) * series
+    m2 = jnp.where(y > -0.35, -y * series, 1.0 - a * a)
+    return a, jnp.maximum(m2, 1e-36)
+
+
+def offsets(r, b, first_position, rows):
+    starts = r.starts_all[b]
+    at = lax.convert_element_type(first_position, F32) + lax.broadcasted_iota(
+        jnp.int32, (rows, 128), 0
+    ).astype(F32)
+    first = jnp.zeros((rows, 128), F32)
+    for row in range(5):
+        start = starts[row : row + 1, :]
+        first = jnp.maximum(first, jnp.where(at >= start, start, 0.0))
+    return first, at - first
+
+
+def roll_rows(value, by):
+    return pltpu.roll(value, by, 0)
+
+
+def combine_segments(p_end, s_end, reverse):
+    row = lax.broadcasted_iota(jnp.int32, (8, 128), 0)
+    for d in (1, 2, 4):
+        by = 8 - d if reverse else d
+        valid = row < 8 - d if reverse else row >= d
+        p_sh, s_sh = roll_rows(p_end, by), roll_rows(s_end, by)
+        s_end = jnp.where(valid, p_end * s_sh + s_end, s_end)
+        p_end = jnp.where(valid, p_end * p_sh, p_end)
+    edge = row == (7 if reverse else 0)
+    by = 7 if reverse else 1
+    enter_p = jnp.where(edge, 1.0, roll_rows(p_end, by))
+    enter_s = jnp.where(edge, 0.0, roll_rows(s_end, by))
+    last = 0 if reverse else 7
+    return enter_p, enter_s, p_end[last : last + 1, :], s_end[last : last + 1, :]
+
+
+def column_sum(value):
+    return jnp.sum(value.reshape(-1, 8, 128), axis=0)
+
+
+def scan_segments(decay, value, reverse):
+    length = decay.shape[1] // 8
+
+    def step(i, carry):
+        j = length - 1 - i if reverse else i
+        at = pl.ds(j, 8, stride=length)
+        done = []
+        for s in range(8):
+            p, v = carry[s]
+            d = decay[s, at, :]
+            if reverse:
+                v = v + value[s, at, :]
+                value[s, at, :] = v
+                decay[s, at, :] = p
+                p, v = d * p, d * v
+            else:
+                p, v = d * p, d * v + value[s, at, :]
+                value[s, at, :] = v
+                decay[s, at, :] = p
+            done.append((p, v))
+        return tuple(done)
+
+    start = tuple((jnp.ones((8, 128), F32), jnp.zeros((8, 128), F32)) for _ in range(8))
+    return lax.fori_loop(0, length, step, start)
+
+
+def entering_states(r, net, ends, reverse):
+    z = net.z
+    for s in range(8):
+        ep, es, tp, ts = combine_segments(*ends[s], reverse)
+        r.ent_p[s] = ep
+        r.ent_s[s] = es
+        r.tot[z, 0, s : s + 1, :] = tp
+        r.tot[z, 1, s : s + 1, :] = ts
+    copies = [net.copy(r.tot.at[z], r.tot.at[z], net.line(net.up(k), net.c)) for k in (1, 2, 3)]
+    for made in copies:
+        made.wait_recv()
+    state = jnp.zeros((8, 128), F32)
+    for i in range(4):
+        at = 3 - i if reverse else i
+        new = r.tot[at, 0] * state + r.tot[at, 1]
+        state = jnp.where((at > z) if reverse else (at < z), new, state)
+    r.inc[...] = state
+    for s in range(8):
+        r.ent_s[s] = r.ent_s[s] + r.ent_p[s] * r.inc[s : s + 1, :]
+
+
+def tile_rows(i):
+    return pl.ds(pl.multiple_of(i * TILE, TILE), TILE)
+
+
+def recur_front(r):
+    net = Net(r.send, r.recv)
+    net.greet()
+    p, z, c, o, q = net.p, net.z, net.c, net.o, net.q
+    sibling = net.plane(0, o)
+    tokens = Gather(net, r.x, r.x_all)
+    tokens.start()
+    mine = net.slot(0, c)
+    r.small_all[q] = r.small[...]
+    r.starts_all[p] = r.starts[...]
+    small = [net.copy(r.small, r.small_all.at[q], net.line(net.up(k), core)) for k in (1, 2, 3) for core in (c, o)]
+    small.append(net.copy(r.small, r.small_all.at[q], sibling))
+    starts = [net.copy(r.starts, r.starts_all.at[p], net.plane(k, c)) for k in (1, 2, 3)]
+    width = r.wg3.shape[2]
+    first = pl.multiple_of(p * width, 128)
+    chip = pl.ds(first, width)
+    theirs = pl.ds(pl.multiple_of(o * 128, 128), 256)
+    theirs_in = pl.ds(pl.multiple_of(first + o * 128, 128), 256)
+    pairs = ((r.wg, r.wg3), (r.wi, r.wi3))
+    from_line = [
+        [net.copy(src.at[:, chip], dst.at[q], net.line(net.up(k), c)) for src, dst in pairs] for k in (1, 2, 3)
+    ]
+    across = [net.copy(src.at[:, theirs_in], dst.at[q, :, theirs], sibling) for src, dst in pairs]
+    spread = []
+
+    def spread_rows(src, dst):
+        at = net.reserve(4)
+
+        @pl.when(z == p)
+        def _():
+            dst[c] = src[...]
+            for k in (1, 2, 3):
+                net.describe(src, dst.at[c], net.line(net.up(k), c), at + k, at).start()
+
+        spread.append((src, dst, at))
+
+    def spread_over(entry):
+        src, dst, at = entry
+
+        @pl.when(z != p)
+        def _():
+            net.describe(src, dst.at[c], sibling, at, at).wait_recv()
+
+        across.append(net.copy(dst.at[c], dst.at[c], sibling))
+
+    def spread_end():
+        for src, dst, at in spread:
+
+            @pl.when(z == p)
+            def _(src=src, dst=dst, at=at):
+                for k in (1, 2, 3):
+                    net.describe(src, dst.at[c], sibling, at + k, at).wait_send()
+
+    spread_rows(r.wr, r.wr3)
+    spread_rows(r.wv, r.wv3)
+    for src, dst in pairs:
+        dst[q] = src[:, chip]
+    cols = r.wmg_out.shape[2]
+    piece = cols // 4
+    selects = []
+    k_at = lax.broadcasted_iota(jnp.int32, (cols, cols), 0)
+    j_at = lax.broadcasted_iota(jnp.int32, (cols, cols), 1)
+    for part in range(4):
+        inside = (j_at >= part * piece) & (j_at < (part + 1) * piece)
+        chosen = inside & (k_at == j_at + (p - part) * piece)
+        selects.append(jnp.where(chosen, 1.0, 0.0).astype(BF))
+    for src, out in ((r.wmg, r.wmg_out), (r.wmu, r.wmu_out)):
+        for core in (0, 1):
+            picked = None
+            for part in range(4):
+                stretch = src[:, (part * 2 + core) * cols : (part * 2 + core + 1) * cols]
+                term = dot(stretch, selects[part])
+                picked = term if picked is None else picked + term
+            out[core] = picked.astype(BF)
+    for made in small + starts:
+        made.wait_recv()
+    low, high = r.small_all[2 * p], r.small_all[2 * p + 1]
+    at_first = jnp.concatenate([low[:, :192], high[:, :64]], axis=1)
+    at_second = jnp.concatenate([low[:, 128:192], high[:, :192]], axis=1)
+    both = lax.select(c == 0, at_first, at_second)
+    for n in range(2):
+        r.chan[n] = both[:, n * 128 : (n + 1) * 128]
+    gain = jnp.concatenate([r.small_all[i, 10:11, 0:128] for i in range(8)], axis=1)
+    r.gain1[...] = gain
+    r.gain2[...] = jnp.concatenate([r.small_all[i, 10:11, 128:256] for i in range(8)], axis=1)
+
+    def normalise(slot):
+        def body(i):
+            rows = pl.ds(pl.multiple_of(i * 32, 32), 32)
+            v = r.x_all[slot, rows, :].astype(F32)
+            s = lax.rsqrt(jnp.mean(v * v, axis=-1, keepdims=True) + NORM_EPS)
+            r.normed[slot, rows, :] = (v * s * gain).astype(BF)
+
+        loop(8, body)
+
+    r.x_all[mine] = r.x[...]
+    normalise(mine)
+    tokens.sibling(0)
+    normalise(net.slot(0, o))
+    tokens.forward()
+    for k in (1, 2, 3):
+        for (src, dst), made in zip(pairs, from_line[k - 1]):
+            made.wait_recv()
+            here = dst.at[net.down(k) * 2 + c, :, theirs]
+            across.append(net.copy(here, here, sibling))
+    tokens.middle()
+    for k in (1, 2):
+        normalise(net.slot(k, c))
+    for k in (1, 2):
+        tokens.sibling(k)
+        normalise(net.slot(k, o))
+    tokens.last()
+    for entry in spread:
+        spread_over(entry)
+    for made in across:
+        made.wait_recv()
+    spread_rows(r.wout, r.wout3)
+    feed = []
+    for src, dst in ((r.wmg_out, r.wmg_all), (r.wmu_out, r.wmu_all)):
+        dst[q] = src[c]
+        for k in (1, 2, 3):
+            for core in (c, o):
+                feed.append(net.copy(src.at[core], dst.at[q], net.line(net.up(k), core)))
+        feed.append(net.copy(src.at[o], dst.at[q], sibling))
+    down = pl.ds(pl.multiple_of(p * piece, 16), piece)
+    r.wmd_all[z] = r.wmd[down, :]
+    for k in (1, 2, 3):
+        feed.append(net.copy(r.wmd.at[down], r.wmd_all.at[z], net.line(net.up(k), c)))
+    cots = Gather(net, r.g, r.g_all)
+    cots.start()
+    r.g_all[mine] = r.g[...]
+    own_cols = pl.ds(pl.multiple_of(c * 128, 128), 256)
+    for i in range(8):
+        r.w2[i * 128 : (i + 1) * 128, 0:256] = r.wg3[i, :, own_cols]
+        r.w2[i * 128 : (i + 1) * 128, 256:512] = r.wi3[i, :, own_cols]
+    rows_of = r.wr3.shape[1]
+    for n in range(2):
+        for part, src in enumerate((r.wr3, r.wv3)):
+            flat = jnp.concatenate([src[0], src[1]], axis=0)
+            pick = lax.select(c == 0, flat[n * 128 : (n + 1) * 128], flat[(n + 1) * 128 : (n + 2) * 128])
+            r.wri[n, :, part * 128 : (part + 1) * 128] = pick
+
+    def project(slot):
+        b, half = lax.div(slot, 2), lax.rem(slot, 2)
+        at = pl.multiple_of(half * 256, 256)
+        h = r.normed[slot]
+        gate = dot(h, r.w2[:, 0:256])
+        inner = dot(h, r.w2[:, 256:512]).astype(BF).astype(F32)
+        for n in range(2):
+            lanes = slice(n * 128, (n + 1) * 128)
+            r.gp[b * 2 + n, pl.ds(at, 256), :] = gate[:, lanes]
+            r.inner[b * 2 + n, pl.ds(at + 8, 256), :] = inner[:, lanes]
+
+    for k in (0, 1, 2):
+        project(net.slot(k, c))
+        project(net.slot(k, o))
+    normalise(net.slot(3, c))
+    project(net.slot(3, c))
+    tokens.sibling(3)
+    normalise(net.slot(3, o))
+    project(net.slot(3, o))
+    edge = net.reserve(1)
+
+    def edge_copy():
+        return net.describe(
+            r.inner.at[:, pl.ds(512, 8)], r.inner.at[:, pl.ds(0, 8)], net.line(net.up(1), c), edge, edge
+        )
+
+    @pl.when(z < 3)
+    def _():
+        edge_copy().start()
+
+    @pl.when(z == 0)
+    def _():
+        r.inner[:, 0:8, :] = jnp.zeros((8, 8, 128), F32)
+
+    cots.forward()
+
+    def gelu_tile(i):
+        s, rows = lax.div(i, 8), tile_rows(lax.rem(i, 8))
+        v = r.gp[s, rows, :]
+        t = jnp.tanh(GELU_SCALE * v * (1.0 + GELU_CUBE * v * v))
+        r.gb[s, rows, :] = 0.5 * v * (1.0 + t)
+
+    loop(64, gelu_tile)
+
+    @pl.when(z > 0)
+    def _():
+        edge_copy().wait_recv()
+
+    @pl.when(z < 3)
+    def _():
+        edge_copy().wait_send()
+
+    def conv_tile(i):
+        s, tile = lax.div(i, 8), lax.rem(i, 8)
+        b, n = lax.div(s, 2), lax.rem(s, 2)
+        rows = tile_rows(tile)
+        _, offset = offsets(r, b, z * 512 + tile * TILE, TILE)
+        window = r.inner[s, pl.ds(pl.multiple_of(tile * TILE, 8), TILE + 8), :]
+        chan = r.chan[n]
+        total = chan[4:5, :] + chan[0:1, :] * window[8:, :]
+        for k in (1, 2, 3):
+            total = total + chan[k : k + 1, :] * jnp.where(offset >= k, window[8 - k : TILE + 8 - k, :], 0.0)
+        r.conv[s, rows, :] = total.astype(BF)
+
+    loop(64, conv_tile)
+    cots.middle()
+
+    def gates(i):
+        s, half = lax.div(i, 2), lax.rem(i, 2)
+        n = lax.rem(s, 2)
+        rows = pl.ds(pl.multiple_of(half * 256, 256), 256)
+        pre = dot(r.conv[s, rows, :], r.wri[n])
+        r.sr[s, rows, :] = pre[:, :128]
+        r.si[s, rows, :] = pre[:, 128:]
+
+    loop(16, gates)
+
+    def terms(s):
+        b, n = lax.div(s, 2), lax.rem(s, 2)
+        chan = r.chan[n]
+        starts_b = r.starts_all[b]
+
+        def tile(i, sums):
+            rows = tile_rows(i)
+            first, offset = offsets(r, b, z * 512 + i * TILE, TILE)
+            sr = jax.nn.sigmoid(r.sr[s, rows, :] + chan[5:6, :])
+            si = jax.nn.sigmoid(r.si[s, rows, :] + chan[6:7, :])
+            r.sr[s, rows, :] = sr
+            r.si[s, rows, :] = si
+            a, m2 = decay_parts(sr, chan[7:8, :])
+            restart = offset == 0.0
+            r.dec[s, rows, :] = jnp.where(restart, 0.0, a)
+            m = jnp.where(restart, 1.0, jnp.sqrt(m2))
+            r.drv[s, rows, :] = m * si * r.conv[s, rows, :].astype(F32)
+            return tuple(
+                sums[row] + column_sum(jnp.where(first == starts_b[row : row + 1, :], a, 0.0)) for row in range(5)
+            )
+
+        sums = lax.fori_loop(0, 512 // TILE, tile, tuple(jnp.zeros((8, 128), F32) for _ in range(5)))
+        sums = [jnp.sum(part, axis=0, keepdims=True) for part in sums] + [jnp.zeros((3, 128), F32)]
+        r.rs_all[z, s] = jnp.concatenate(sums, axis=0)
+
+    loop(8, terms)
+    spread_over(spread[-1])
+    row_sums = [net.copy(r.rs_all.at[z], r.rs_all.at[z], net.line(net.up(k), c)) for k in (1, 2, 3)]
+    ends = scan_segments(r.dec, r.drv, False)
+    entering_states(r, net, ends, False)
+    cots.last()
+    across[-1].wait_recv()
+
+    def own_rows(i):
+        at = c * 128 + i * 64
+        rows = pl.ds(pl.multiple_of(lax.rem(at, 192), 64), 64)
+        value = r.wout3[lax.div(at, 192), rows, :]
+        to = pl.ds(pl.multiple_of(i * 64, 64), 64)
+        r.wo[to, :] = value
+        r.wom[to, :] = value
+
+    loop(4, own_rows)
+    r.wom[pl.ds(pl.multiple_of(o * 192, 64), 64), :] = jnp.zeros((64, r.wom.shape[1]), BF)
+
+    for n in range(2):
+        for b in range(4):
+            r.states[b * 2 + n, 7:8, :] = r.inc[b * 2 + n : b * 2 + n + 1, :]
+
+    def mix_tile(i):
+        s, tile = lax.div(i, 8), lax.rem(i, 8)
+        b, n = lax.div(s, 2), lax.rem(s, 2)
+        rows = tile_rows(tile)
+        enter = r.ent_s[s, pl.ds(tile, 1), :]
+        states = r.drv[s, rows, :] + r.dec[s, rows, :] * enter
+        r.states[s, pl.ds(pl.multiple_of(tile * TILE + 8, 8), TILE), :] = states
+        lanes = pl.ds(pl.multiple_of(n * 128, 128), 128)
+        r.mixed[b * 2 + lax.div(tile, 4), tile_rows(lax.rem(tile, 4)), lanes] = (states * r.gb[s, rows, :]).astype(BF)
+
+    loop(64, mix_tile)
+    total = Reduce(net, r)
+    for k in (3, 1, 2, 0):
+        total.put_other(k, dot(r.mixed[net.slot(k, o)], r.wom[...]))
+        total.put_own(k, dot(r.mixed[net.slot(k, c)], r.wom[...]))
+    total.far()
+    total.near_x()
+    total.near_y()
+    total.relay()
+    for k in (1, 2, 3):
+        cots.sibling(k)
+    cots.sibling(0)
+    total.finish()
+    gain2 = r.gain2[...]
+    for h in range(2):
+
+        def body(i, h=h):
+            rows = pl.ds(pl.multiple_of(h * 128 + i * 32, 32), 32)
+            v = r.x[rows, :].astype(F32) + total.total(h, i, 32)
+            r.residual[rows, :] = v
+            s = lax.rsqrt(jnp.mean(v * v, axis=-1, keepdims=True) + NORM_EPS)
+            r.n2[rows, :] = (v * s * gain2).astype(BF)
+
+        loop(4, body)
+    for made in feed + row_sums:
+        made.wait_recv()
+    r.rows_sum[...] = r.rs_all[0] + r.rs_all[1] + r.rs_all[2] + r.rs_all[3]
+    spread_end()
+    net.drain()
+
+
+def feed_forward(r):
+    net = Net(r.send, r.recv)
+    net.greet()
+    z, c, o = net.z, net.c, net.o
+    acts = Gather(net, r.n2, r.n2_all)
+    acts.start()
+    mine = net.slot(0, c)
+    r.n2_all[mine] = r.n2[...]
+    width = r.wmg.shape[2]
+    back = Reduce(net, r)
+
+    def gate_up():
+        return r.wmg[...].reshape(-1, width), r.wmu[...].reshape(-1, width)
+
+    def down():
+        return r.wmd[...].reshape(width, -1)
+
+    def part(k, core):
+        slot = net.slot(k, core)
+        h = r.n2_all[slot]
+        wmg, wmu = gate_up()
+        r.ug[...] = dot(h, wmg)
+        r.ul[...] = dot(h, wmu)
+        r.dh[...] = dot(r.g_all[slot], down(), NT)
+
+        def body(i):
+            rows = pl.ds(pl.multiple_of(i * 32, 32), 32)
+            gelu, slope = gelu_parts(r.ug[rows, :])
+            ul, dh = r.ul[rows, :], r.dh[rows, :]
+            r.hid[slot, rows, :] = (gelu * ul).astype(BF)
+            r.dgu[slot, rows, 0:width] = (dh * ul * slope).astype(BF)
+            r.dgu[slot, rows, width : 2 * width] = (dh * gelu).astype(BF)
+
+        loop(8, body)
+        wmg, wmu = gate_up()
+        grad = dot(r.dgu[slot, :, 0:width], wmg, NT) + dot(r.dgu[slot, :, width : 2 * width], wmu, NT)
+        if core is c:
+            back.put_own(k, grad)
+        else:
+            back.put_other(k, grad)
+
+    part(0, c)
+    acts.sibling(0)
+    part(0, o)
+    acts.forward()
+    acts.middle()
+    part(1, c)
+    part(2, c)
+    acts.sibling(1)
+    part(1, o)
+    acts.sibling(2)
+    part(2, o)
+    acts.last()
+    part(3, c)
+    acts.sibling(3)
+    part(3, o)
+    back.far()
+    back.near_x()
+    back.near_y()
+    back.relay()
+    flat = r.dgu[...].reshape(-1, 2 * width)
+    for i in range(4):
+        rows = r.n2_all[:, :, i * 256 : (i + 1) * 256].reshape(-1, 256)
+        r.gm[i] = dot(rows, flat, TN).astype(BF)
+    hid = r.hid[...].reshape(-1, width)
+    g_flat = r.g_all[...].reshape(hid.shape[0], -1)
+    piece = width // 4
+    for half in range(2):
+        cols = slice(half * 512, half * 512 + 512)
+        value = dot(hid, g_flat[:, cols], TN).astype(BF)
+        for i in range(4):
+            r.gd[i, :, cols] = value[i * piece : (i + 1) * piece, :]
+    back.finish()
+    gain2 = r.gain2[...]
+    sums = jnp.zeros((8, r.n2.shape[1]), F32)
+    for h in range(2):
+
+        def body(i, sums, h=h):
+            rows = pl.ds(pl.multiple_of(h * 128 + i * 32, 32), 32)
+            v = r.residual[rows, :]
+            dn = back.total(h, i, 32)
+            s = lax.rsqrt(jnp.mean(v * v, axis=-1, keepdims=True) + NORM_EPS)
+            u = dn * gain2
+            pulled = s * u - v * (s * s * s * jnp.mean(u * v, axis=-1, keepdims=True))
+            d_res = r.g[rows, :].astype(F32) + pulled
+            r.d_res[rows, :] = d_res
+            r.d_out[rows, :] = d_res.astype(BF)
+            return sums + jnp.sum((dn * v * s).reshape(4, 8, -1), axis=0)
+
+        sums = lax.fori_loop(0, 4, body, sums)
+    r.gain2_sum[...] = sums
+    for partner in (net.plane(0, o), net.plane(1, c), net.plane(2, c)):
+        pl.semaphore_signal(r.free, inc=1, device_id=partner, device_id_type=pl.DeviceIdType.MESH)
+    pl.semaphore_wait(r.free, 3)
+    net.drain()
+    out = Reduce(net, r)
+    for k in (3, 1, 2, 0):
+        out.put_other(k, dot(r.hid[net.slot(k, o)], down()))
+        out.put_own(k, dot(r.hid[net.slot(k, c)], down()))
+    out.far()
+    out.near_x()
+    out.near_y()
+    out.relay()
+    out.finish()
+    for h in range(2):
+
+        def body(i, h=h):
+            rows = pl.ds(pl.multiple_of(h * 128 + i * 32, 32), 32)
+            r.block_out[rows, :] = (r.residual[rows, :] + out.total(h, i, 32)).astype(BF)
+
+        loop(4, body)
+    net.drain()
+
+
+def recur_back(r):
+    net = Net(r.send, r.recv)
+    net.greet()
+    p, z, c, o, q = net.p, net.z, net.c, net.o, net.q
+    sibling = net.plane(0, o)
+    grads = Gather(net, r.d_out, r.do_all)
+    grads.start()
+    mine = net.slot(0, c)
+    r.do_all[mine] = r.d_out[...]
+
+    def line_sum_start(src, dst):
+        return [net.copy(src.at[net.up(k)], dst.at[k - 1], net.line(net.up(k), c)) for k in (1, 2, 3)]
+
+    def line_sum_end(copies, src, dst, out):
+        for made in copies:
+            made.wait_recv()
+        rows = out.shape[0]
+        step = 32
+
+        def body(i):
+            at = pl.ds(pl.multiple_of(i * step, step), step)
+            value = src[z, at, :].astype(F32)
+            for k in range(3):
+                value = value + dst[k, at, :].astype(F32)
+            out[at, :] = value.astype(BF)
+
+        loop(rows // step, body)
+
+    mlp_m = line_sum_start(r.gm, r.gm_in)
+    mlp_d = line_sum_start(r.gd, r.gd_in)
+
+    def back_out(slot):
+        b, half = lax.div(slot, 2), lax.rem(slot, 2)
+        dm = dot(r.do_all[slot], r.wo[...], NT)
+        for n in range(2):
+            r.dconv[b * 2 + n, pl.ds(pl.multiple_of(half * 256, 256), 256), :] = dm[:, n * 128 : (n + 1) * 128]
+
+    back_out(mine)
+    grads.sibling(0)
+    back_out(net.slot(0, o))
+    lane = lax.rem(lax.broadcasted_iota(jnp.int32, (32, 512), 1), 256)
+    counted = (lane >= 64 * c) & (lane < 192 + 64 * c)
+
+    def mask_rows(i):
+        rows = pl.ds(pl.multiple_of(i * 32, 32), 32)
+        r.w2m[rows, :] = jnp.where(counted, r.w2[rows, :].astype(F32), 0.0).astype(BF)
+
+    loop(r.w2.shape[0] // 32, mask_rows)
+    grads.forward()
+    grads.middle()
+    for k in (1, 2):
+        back_out(net.slot(k, c))
+    for k in (1, 2):
+        grads.sibling(k)
+        back_out(net.slot(k, o))
+    grads.last()
+    back_out(net.slot(3, c))
+    grads.sibling(3)
+    back_out(net.slot(3, o))
+
+    def first_pass(i):
+        s, tile = lax.div(i, 8), lax.rem(i, 8)
+        b, n = lax.div(s, 2), lax.rem(s, 2)
+        rows = tile_rows(tile)
+        _, offset = offsets(r, b, z * 512 + tile * TILE, TILE)
+        gelu, slope = gelu_parts(r.gp[s, rows, :])
+        dm = r.dconv[s, rows, :]
+        states = r.states[s, pl.ds(pl.multiple_of(tile * TILE + 8, 8), TILE), :]
+        lanes = pl.ds(pl.multiple_of(n * 128, 128), 128)
+        r.dgi[b * 2 + lax.div(tile, 4), tile_rows(lax.rem(tile, 4)), lanes] = (dm * states * slope).astype(BF)
+        r.drv[s, rows, :] = dm * gelu
+        a, _ = decay_parts(r.sr[s, rows, :], r.chan[n, 7:8, :])
+        r.dec[s, rows, :] = jnp.where(offset == 0.0, 0.0, a)
+
+    loop(64, first_pass)
+    ends = scan_segments(r.dec, r.drv, True)
+    entering_states(r, net, ends, True)
+    r.vec[...] = jnp.zeros((2, 8, 8, 128), F32)
+
+    def second_pass(s):
+        b, n = lax.div(s, 2), lax.rem(s, 2)
+        chan = r.chan[n]
+
+        def tile(i, sums):
+            rows = tile_rows(i)
+            _, offset = offsets(r, b, z * 512 + i * TILE, TILE)
+            live = offset != 0.0
+            enter = r.ent_s[s, pl.ds(i, 1), :]
+            ds = r.drv[s, rows, :] + r.dec[s, rows, :] * enter
+            window = r.states[s, pl.ds(pl.multiple_of(i * TILE, 8), TILE + 8), :]
+            before = window[7 : TILE + 7, :]
+            sr, si = r.sr[s, rows, :], r.si[s, rows, :]
+            cv = r.conv[s, rows, :].astype(F32)
+            a, m2 = decay_parts(sr, chan[7:8, :])
+            inv = lax.rsqrt(m2)
+            m = jnp.where(live, m2 * inv, 1.0)
+            dsi = ds * si
+            d_log = jnp.where(live, a * (ds * before - dsi * cv * a * inv), 0.0)
+            lam_term = d_log * sr
+            d_r = (-DECAY_SCALE) * chan[7:8, :] * lam_term * (1.0 - sr)
+            dm_i = dsi * m
+            d_i = dm_i * cv * (1.0 - si)
+            d_r, d_i = d_r.astype(BF), d_i.astype(BF)
+            r.dri[s, rows, 0:128] = d_r
+            r.dri[s, rows, 128:256] = d_i
+            r.dconv[s, rows, :] = dm_i
+            return (
+                sums[0] + column_sum(d_r.astype(F32)),
+                sums[1] + column_sum(d_i.astype(F32)),
+                sums[2] + column_sum(lam_term),
+            )
+
+        zero = jnp.zeros((8, 128), F32)
+        sums = lax.fori_loop(0, 512 // TILE, tile, (zero, zero, zero))
+        r.vec[n, 5] = r.vec[n, 5] + sums[0]
+        r.vec[n, 6] = r.vec[n, 6] + sums[1]
+        r.vec[n, 7] = r.vec[n, 7] + sums[2]
+
+    loop(8, second_pass)
+
+    def gate_back(i):
+        s, half = lax.div(i, 2), lax.rem(i, 2)
+        n = lax.rem(s, 2)
+        rows = pl.ds(pl.multiple_of(half * 256, 256), 256)
+        r.dconv[s, rows, :] = r.dconv[s, rows, :] + dot(r.dri[s, rows, :], r.wri[n], NT)
+
+    loop(16, gate_back)
+    edge = net.reserve(1)
+
+    def edge_copy():
+        return net.describe(
+            r.dconv.at[:, pl.ds(0, 8)], r.dconv.at[:, pl.ds(512, 8)], net.line(net.down(1), c), edge, edge
+        )
+
+    @pl.when(z > 0)
+    def _():
+        edge_copy().start()
+
+    @pl.when(z == 3)
+    def _():
+        r.dconv[:, 512:520, :] = jnp.zeros((8, 8, 128), F32)
+
+    for n in range(2):
+        total = None
+        for b in range(4):
+            term = dot(r.conv[b * 2 + n], r.dri[b * 2 + n], TN)
+            total = term if total is None else total + term
+        r.go[n * 128 : (n + 1) * 128, 1024:1280] = total.astype(BF)
+    mixed = r.mixed[...].reshape(-1, 256)
+    for half in range(2):
+        cols = slice(half * 512, half * 512 + 512)
+        r.go[:, cols] = dot(mixed, r.do_all[:, :, cols].reshape(-1, 512), TN).astype(BF)
+    go_rows = r.go_in.shape[1]
+    own_rows = pl.ds(pl.multiple_of(c * 64, 16), go_rows)
+    go_at = net.reserve(3)
+
+    def go_copy(k):
+        return net.describe(r.go.at[own_rows], r.go_in.at[k - 1], net.line(p, c), go_at + k - 1, go_at + k - 1)
+
+    for k in (1, 2, 3):
+
+        @pl.when(lax.rem(z + 4 - p, 4) == k)
+        def _(k=k):
+            go_copy(k).start()
+
+    line_sum_end(mlp_m, r.gm, r.gm_in, r.gm_sum)
+    line_sum_end(mlp_d, r.gd, r.gd_in, r.gd_sum)
+    owners = []
+    half_rows = r.gm_sum.shape[0] // 2
+    slot_mine = p * 2 + c
+
+    def to_owners(src, dst):
+        for k in (1, 2, 3):
+            for core in (c, o):
+                rows = pl.ds(pl.multiple_of(core * half_rows, 16), half_rows)
+                owners.append(net.copy(src.at[rows], dst.at[slot_mine], net.plane(k, core)))
+        theirs = src.at[pl.ds(pl.multiple_of(o * half_rows, 16), half_rows)]
+        owners.append(net.copy(theirs, dst.at[slot_mine], sibling))
+        dst[slot_mine] = src[pl.ds(pl.multiple_of(c * half_rows, 16), half_rows), :]
+
+    to_owners(r.gm_sum, r.fm)
+    r.fd[p] = r.gd_sum[...]
+    for k in (1, 2, 3):
+        owners.append(net.copy(r.gd_sum, r.fd.at[p], net.plane(k, c)))
+    for k in (1, 2, 3):
+        for core in (c, o):
+            owners.append(
+                net.copy(r.rows_sum.at[pl.ds(net.near[k] * 2, 2)], r.fr.at[slot_mine], net.plane(k, core))
+            )
+    owners.append(net.copy(r.rows_sum.at[pl.ds(p * 2, 2)], r.fr.at[slot_mine], sibling))
+    r.fr[slot_mine] = r.rows_sum[pl.ds(p * 2, 2)]
+
+    @pl.when(z < 3)
+    def _():
+        edge_copy().wait_recv()
+
+    @pl.when(z > 0)
+    def _():
+        edge_copy().wait_send()
+
+    def conv_back(s):
+        b, n = lax.div(s, 2), lax.rem(s, 2)
+        chan = r.chan[n]
+        lanes = pl.ds(pl.multiple_of(256 + n * 128, 128), 128)
+
+        def tile(i, sums):
+            _, offset = offsets(r, b, z * 512 + i * TILE, TILE + 8)
+            window = r.dconv[s, pl.ds(pl.multiple_of(i * TILE, 8), TILE + 8), :]
+            inner = r.inner[s, pl.ds(pl.multiple_of(i * TILE, 8), TILE + 8), :]
+            total = chan[0:1, :] * window[:TILE, :]
+            out = [sums[0] + column_sum(window[:TILE, :] * inner[8:, :])]
+            for k in (1, 2, 3):
+                masked = jnp.where(offset >= k, window, 0.0)
+                total = total + chan[k : k + 1, :] * masked[k : TILE + k, :]
+                out.append(sums[k] + column_sum(masked[:TILE, :] * inner[8 - k : TILE + 8 - k, :]))
+            out.append(sums[4] + column_sum(window[:TILE, :]))
+            r.dgi[b * 2 + lax.div(i, 4), tile_rows(lax.rem(i, 4)), lanes] = total.astype(BF)
+            return tuple(out)
+
+        sums = lax.fori_loop(0, 512 // TILE, tile, tuple(jnp.zeros((8, 128), F32) for _ in range(5)))
+        for j in range(5):
+            r.vec[n, j] = r.vec[n, j] + sums[j]
+
+    loop(8, conv_back)
+    back = Reduce(net, r)
+    for k in (3, 1, 2, 0):
+        back.put_other(k, dot(r.dgi[net.slot(k, o)], r.w2m[...], NT))
+        back.put_own(k, dot(r.dgi[net.slot(k, c)], r.w2m[...], NT))
+    back.far()
+    back.near_x()
+    back.near_y()
+    back.relay()
+    flat = r.dgi[...].reshape(-1, 512)
+    half_c = pl.ds(pl.multiple_of(c * 128, 128), 128)
+    for i in range(4):
+        value = dot(r.normed[:, :, i * 256 : (i + 1) * 256].reshape(-1, 256), flat, TN)
+        for j in range(2):
+            n0, n1 = value[:, j * 256 : j * 256 + 128], value[:, j * 256 + 128 : j * 256 + 256]
+            r.ga[i, :, j * 128 : (j + 1) * 128] = lax.select(c == 0, n0, n1).astype(BF)
+            shared = lax.select(c == 0, n1, n0)
+            mine_rows = lax.select(c == 0, shared[0:128], shared[128:256])
+            r.gb2[i, :, j * 128 : (j + 1) * 128] = mine_rows.astype(BF)
+    sum_a = line_sum_start(r.ga, r.ga_in)
+    sum_b = line_sum_start(r.gb2, r.gb2_in)
+    for n in range(2):
+        sums = [jnp.sum(r.vec[n, j], axis=0, keepdims=True) for j in range(8)]
+        sums[7] = sums[7] * (DECAY_SCALE * r.chan[n, 8:9, :])
+        r.vsum[z, :, n * 128 : (n + 1) * 128] = jnp.concatenate(sums, axis=0)
+    vec = [net.copy(r.vsum.at[z], r.vsum.at[z], net.line(net.up(k), c)) for k in (1, 2, 3)]
+    back.finish()
+    gain = r.gain1[...]
+    sums = jnp.zeros((8, r.x.shape[1]), F32)
+    for h in range(2):
+
+        def body(i, sums, h=h):
+            rows = pl.ds(pl.multiple_of(h * 128 + i * 32, 32), 32)
+            v = r.x[rows, :].astype(F32)
+            dn = back.total(h, i, 32)
+            s = lax.rsqrt(jnp.mean(v * v, axis=-1, keepdims=True) + NORM_EPS)
+            u = dn * gain
+            r.d_in[rows, :] = r.d_res[rows, :] + (
+                s * u - v * (s * s * s * jnp.mean(u * v, axis=-1, keepdims=True))
+            )
+            return sums + jnp.sum((dn * v * s).reshape(4, 8, -1), axis=0)
+
+        sums = lax.fori_loop(0, 4, body, sums)
+    gains = jnp.concatenate(
+        [
+            jnp.sum(sums, axis=0, keepdims=True),
+            jnp.sum(r.gain2_sum[...], axis=0, keepdims=True),
+            jnp.zeros((6, sums.shape[1]), F32),
+        ],
+        axis=0,
+    )
+    for i in range(8):
+        r.gsum[i] = gains[:, i * 128 : (i + 1) * 128]
+    r.gline[q] = r.gsum[q]
+    gain_line = [
+        net.copy(r.gsum.at[net.up(k) * 2 + core], r.gline.at[q], net.line(net.up(k), core))
+        for k in (1, 2, 3)
+        for core in (c, o)
+    ]
+    gain_line.append(net.copy(r.gsum.at[z * 2 + o], r.gline.at[q], sibling))
+    for made in vec:
+        made.wait_recv()
+    r.vout[p] = r.vsum[0] + r.vsum[1] + r.vsum[2] + r.vsum[3]
+    fo_at = net.reserve(6)
+
+    def owner_copies(partners):
+        made = []
+        for k in partners:
+            made.append(net.describe(r.vout.at[p], r.vout.at[p], net.plane(k, c), fo_at + k - 1, fo_at))
+            made.append(net.describe(r.fo.at[0], r.fo.at[0], net.plane(k, c), fo_at + 2 + k, fo_at + 3))
+        return made
+
+    @pl.when(z == p)
+    def _():
+        for k in (1, 2, 3):
+            go_copy(k).wait_recv()
+
+        def body(i):
+            at = pl.ds(pl.multiple_of(i * 16, 16), 16)
+            value = r.go[pl.ds(pl.multiple_of(c * 64 + i * 16, 16), 16), :].astype(F32)
+            for k in range(3):
+                value = value + r.go_in[k, at, :].astype(F32)
+            r.fo[0, at, :] = value.astype(BF)
+
+        loop(go_rows // 16, body)
+        for made in owner_copies((1, 2, 3)):
+            made.start()
+
+    for k in (1, 2, 3):
+
+        @pl.when(lax.rem(z + 4 - p, 4) == k)
+        def _(k=k):
+            go_copy(k).wait_send()
+
+    line_sum_end(sum_a, r.ga, r.ga_in, r.ga_sum)
+    to_owners(r.ga_sum, r.fa)
+    line_sum_end(sum_b, r.gb2, r.gb2_in, r.gb2_sum)
+    r.fb[p] = r.gb2_sum[...]
+    for k in (1, 2, 3):
+        owners.append(net.copy(r.gb2_sum, r.fb.at[p], net.plane(k, c)))
+    for made in gain_line:
+        made.wait_recv()
+    total = r.gline[0]
+    for i in range(1, 8):
+        total = total + r.gline[i]
+    r.gplane[p] = total
+    gain_plane = [net.copy(r.gplane.at[p], r.gplane.at[p], net.plane(k, c)) for k in (1, 2, 3)]
+
+    @pl.when(z != p)
+    def _():
+        for made in owner_copies((1,)):
+            made.wait_recv()
+
+    @pl.when(z == p)
+    def _():
+        for made in owner_copies((1, 2, 3)):
+            made.wait_send()
+
+    for made in owners + gain_plane:
+        made.wait_recv()
+    r.gain_out[...] = r.gplane[0] + r.gplane[1] + r.gplane[2] + r.gplane[3]
+    r.vec_out[...] = r.vout[z]
+    net.drain()
+
+
+def assemble(r):
+    c = lax.rem(lax.axis_index("seq"), 2)
+    for chip in range(4):
+        for j, out in enumerate((r.o_gate, r.o_in)):
+            lanes = slice(j * 128, (j + 1) * 128)
+            at = chip * 384
+            out[:, at : at + 128] = r.fa[chip * 2, :, lanes].astype(F32)
+            out[:, at + 128 : at + 256] = r.fb[chip, :, lanes].astype(F32)
+            out[:, at + 256 : at + 384] = r.fa[chip * 2 + 1, :, lanes].astype(F32)
+    cols = r.fm.shape[2] // 2
+    piece = cols // 4
+    for j, out in enumerate((r.o_mgate, r.o_mup)):
+        for part in range(4):
+            for core in range(2):
+                at = (part * 2 + core) * cols
+                lanes = slice(j * cols + part * piece, j * cols + (part + 1) * piece)
+                out[:, at : at + cols] = jnp.concatenate(
+                    [r.fm[chip * 2 + core, :, lanes].astype(F32) for chip in range(4)], axis=1
+                )
+    for chip in range(4):
+        r.o_mdown[chip * piece : (chip + 1) * piece, :] = r.fd[chip].astype(F32)
+    r.o_out[...] = r.fo[0, :, 0:1024].astype(F32)
+    r.o_r[...] = r.fo[0, :, 1024:1152].astype(F32)
+    r.o_i[...] = r.fo[0, :, 1152:1280].astype(F32)
+    vec = r.vec_in[...]
+    r.o_vec[...] = lax.select(c == 0, vec[:, 0:192], vec[:, 64:256])
+    counts = r.starts[...]
+    for chip in range(4):
+        for half, (slot, n) in enumerate(((chip * 2, 0), (chip * 2, 1), (chip * 2 + 1, 1))):
+            at = chip * 384 + half * 128
+            r.o_mean[:, at : at + 128] = r.fr[slot, n] / counts[8:16, :]
 
 
 def shifted(value, axis, by):
@@ -306,6 +1478,237 @@
     )
 
 
+def pack(row_lengths, norm_gain, conv_w, conv_b, b_rgate, b_igate, lam, mlp_gain):
+    lengths = row_lengths[0]
+    starts = jnp.cumsum(lengths) - lengths
+    column = jnp.concatenate(
+        [starts.astype(F32), jnp.zeros((3,), F32), lengths.astype(F32), jnp.ones((3,), F32)]
+    )
+    lam = lam.astype(F32)
+    rows = jnp.concatenate(
+        [
+            conv_w.astype(F32),
+            conv_b.astype(F32)[None],
+            b_rgate.astype(F32)[None],
+            b_igate.astype(F32)[None],
+            jax.nn.softplus(-lam)[None],
+            jax.nn.sigmoid(-lam)[None],
+        ],
+        axis=0,
+    )
+    rows = jnp.pad(rows, ((0, 1), (0, 64)))
+    gains = jnp.concatenate([norm_gain.astype(F32), mlp_gain.astype(F32)])[None]
+    small = jnp.concatenate([rows, gains, jnp.zeros((5, 256), F32)], axis=0)
+    return small, jnp.broadcast_to(column[:, None], (16, 128))
+
+
+def planes(
+    inputs,
+    out_grad,
+    row_lengths,
+    norm_gain,
+    w_gate,
+    w_in,
+    conv_w,
+    conv_b,
+    w_rgate,
+    b_rgate,
+    w_igate,
+    b_igate,
+    lam,
+    w_out,
+    mlp_gain,
+    w_mlp_gate,
+    w_mlp_up,
+    w_mlp_down,
+):
+    small, starts = pack(row_lengths, norm_gain, conv_w, conv_b, b_rgate, b_igate, lam, mlp_gain)
+    x, g = inputs[0], out_grad[0]
+    vmem = pltpu.VMEM
+    front = kernel_call(
+        recur_front,
+        dict(
+            x=x, g=g, small=small, starts=starts, wg=w_gate, wi=w_in, wr=w_rgate, wv=w_igate, wout=w_out,
+            wmg=w_mlp_gate, wmu=w_mlp_up, wmd=w_mlp_down,
+        ),
+        dict(
+            normed=array(8, 256, 1024, dtype=BF),
+            g_all=array(8, 256, 1024, dtype=BF),
+            w2=array(1024, 512, dtype=BF),
+            wo=array(256, 1024, dtype=BF),
+            wri=array(2, 128, 256, dtype=BF),
+            wmg_all=array(8, 128, 384, dtype=BF),
+            wmu_all=array(8, 128, 384, dtype=BF),
+            wmd_all=array(4, 96, 1024, dtype=BF),
+            gp=array(8, 512, 128),
+            inner=array(8, 520, 128),
+            conv=array(8, 512, 128, dtype=BF),
+            sr=array(8, 512, 128),
+            si=array(8, 512, 128),
+            states=array(8, 520, 128),
+            mixed=array(8, 256, 256, dtype=BF),
+            residual=array(256, 1024),
+            n2=array(256, 1024, dtype=BF),
+            chan=array(2, 16, 128),
+            starts_all=array(4, 16, 128),
+            rows_sum=array(8, 8, 128),
+            gain1=array(1, 1024),
+            gain2=array(1, 1024),
+        ),
+        dict(
+            x_all=vmem((8, 256, 1024), BF),
+            small_all=vmem((8, 16, 256), F32),
+            wg3=vmem((8, 128, 384), BF),
+            wi3=vmem((8, 128, 384), BF),
+            wr3=vmem((2, 192, 128), BF),
+            wv3=vmem((2, 192, 128), BF),
+            wout3=vmem((2, 192, 1024), BF),
+            wom=vmem((256, 1024), BF),
+            wmg_out=vmem((2, 128, 384), BF),
+            wmu_out=vmem((2, 128, 384), BF),
+            gb=vmem((8, 512, 128), F32),
+            dec=vmem((8, 512, 128), F32),
+            drv=vmem((8, 512, 128), F32),
+            ent_p=vmem((8, 8, 128), F32),
+            ent_s=vmem((8, 8, 128), F32),
+            tot=vmem((4, 2, 8, 128), F32),
+            inc=vmem((8, 128), F32),
+            rs_all=vmem((4, 8, 8, 128), F32),
+            **reduce_scratch(256, 1024),
+        ),
+        110,
+        0,
+    )
+    feed = kernel_call(
+        feed_forward,
+        dict(
+            n2=front["n2"], g=g, g_all=front["g_all"], residual=front["residual"], gain2=front["gain2"],
+            wmg=front["wmg_all"], wmu=front["wmu_all"], wmd=front["wmd_all"],
+        ),
+        dict(
+            block_out=array(256, 1024, dtype=BF),
+            d_res=array(256, 1024),
+            d_out=array(256, 1024, dtype=BF),
+            gain2_sum=array(8, 1024),
+            gm=array(4, 256, 768, dtype=BF),
+            gd=array(4, 96, 1024, dtype=BF),
+        ),
+        dict(
+            n2_all=vmem((8, 256, 1024), BF),
+            ug=vmem((256, 384), F32),
+            ul=vmem((256, 384), F32),
+            dh=vmem((256, 384), F32),
+            hid=vmem((8, 256, 384), BF),
+            dgu=vmem((8, 256, 768), BF),
+            free=pltpu.SemaphoreType.REGULAR,
+            **reduce_scratch(256, 1024),
+        ),
+        40,
+        1,
+    )
+    back = kernel_call(
+        recur_back,
+        dict(
+            x=x, d_out=feed["d_out"], d_res=feed["d_res"], gain2_sum=feed["gain2_sum"], gm=feed["gm"], gd=feed["gd"],
+            **{
+                name: front[name]
+                for name in (
+                    "normed", "w2", "wo", "wri", "gp", "inner", "conv", "sr", "si", "states", "mixed", "chan",
+                    "starts_all", "rows_sum", "gain1",
+                )
+            },
+        ),
+        dict(
+            d_in=array(256, 1024),
+            fm=array(8, 128, 768, dtype=BF),
+            fd=array(4, 96, 1024, dtype=BF),
+            fa=array(8, 128, 256, dtype=BF),
+            fb=array(4, 128, 256, dtype=BF),
+            fo=array(1, 192, 1280, dtype=BF),
+            fr=array(8, 2, 8, 128),
+            vec_out=array(8, 256),
+            gain_out=array(8, 128),
+        ),
+        dict(
+            do_all=vmem((8, 256, 1024), BF),
+            gm_in=vmem((3, 256, 768), BF),
+            gd_in=vmem((3, 96, 1024), BF),
+            gm_sum=vmem((256, 768), BF),
+            gd_sum=vmem((96, 1024), BF),
+            w2m=vmem((1024, 512), BF),
+            drv=vmem((8, 512, 128), F32),
+            dec=vmem((8, 512, 128), F32),
+            dri=vmem((8, 512, 256), BF),
+            dconv=vmem((8, 520, 128), F32),
+            dgi=vmem((8, 256, 512), BF),
+            vec=vmem((2, 8, 8, 128), F32),
+            vsum=vmem((4, 8, 256), F32),
+            vout=vmem((4, 8, 256), F32),
+            ent_p=vmem((8, 8, 128), F32),
+            ent_s=vmem((8, 8, 128), F32),
+            tot=vmem((4, 2, 8, 128), F32),
+            inc=vmem((8, 128), F32),
+            go=vmem((256, 1280), BF),
+            go_in=vmem((3, 192, 1280), BF),
+            ga=vmem((4, 256, 256), BF),
+            ga_in=vmem((3, 256, 256), BF),
+            ga_sum=vmem((256, 256), BF),
+            gb2=vmem((4, 128, 256), BF),
+            gb2_in=vmem((3, 128, 256), BF),
+            gb2_sum=vmem((128, 256), BF),
+            gsum=vmem((8, 8, 128), F32),
+            gline=vmem((8, 8, 128), F32),
+            gplane=vmem((4, 8, 128), F32),
+            **reduce_scratch(256, 1024),
+        ),
+        110,
+        2,
+    )
+    out = kernel_call(
+        assemble,
+        dict(
+            fm=back["fm"], fd=back["fd"], fa=back["fa"], fb=back["fb"], fo=back["fo"], fr=back["fr"],
+            vec_in=back["vec_out"], starts=starts,
+        ),
+        dict(
+            o_gate=array(128, 1536),
+            o_in=array(128, 1536),
+            o_mgate=array(128, 3072),
+            o_mup=array(128, 3072),
+            o_mdown=array(384, 1024),
+            o_out=array(192, 1024),
+            o_r=array(192, 128),
+            o_i=array(192, 128),
+            o_vec=array(8, 192),
+            o_mean=array(8, 1536),
+        ),
+        {},
+        0,
+        None,
+    )
+    vec, gains = out["o_vec"], back["gain_out"]
+    return (
+        feed["block_out"][None],
+        back["d_in"][None],
+        gains[0],
+        out["o_gate"],
+        out["o_in"],
+        vec[0:4],
+        vec[4],
+        out["o_r"],
+        vec[5],
+        out["o_i"],
+        vec[6],
+        vec[7],
+        out["o_out"],
+        gains[1],
+        out["o_mgate"],
+        out["o_mup"],
+        out["o_mdown"],
+        out["o_mean"][None, 0:5],
+    )
+
+
 def solution(mesh):
     in_specs = (
         P("batch", "seq", None),
@@ -347,4 +1750,6 @@
         P("seq", None),
         P("batch", None, None),
     )
-    return jax.shard_map(shards, mesh=mesh, in_specs=in_specs, out_specs=out_specs, check_vma=False)
+    in_planes = mesh.shape["batch"] == 4 and mesh.shape["seq"] == 8
+    body = planes if in_planes else shards
+    return jax.shard_map(body, mesh=mesh, in_specs=in_specs, out_specs=out_specs, check_vma=False)

time: 1630 us -> 428 us (0.26); the launches traced: 1610 us -> 425 us
  waiting for transfers between devices: 728 us -> 0 us
  Pallas kernels: 0 us -> 409 us
  local copies, waits for them, and re-layouts: 402 us -> 8.67 us
  blocking collectives: 169 us -> 0 us
  other arithmetic: 175 us -> 6.22 us
  matrix products: 108 us -> 0 us
  between operations: 17.8 us -> 0.7 us
    reduce_scatter x8 -> x0, waiting for transfers between devices: 595 us -> none  [the longest x1 128 us: shards(): lax.psum_scatter(grad_mgate, 'seq', scatter_dimension=0, tiled=True)]
    pallas_call x0 -> x4, Pallas kernels: none -> 409 us  [kernel_call(): pl.pallas_call(kernel, out_shape=list(outs.values()), in_specs=[spec] * l...]
    slice x112 -> x2, local copies, waits for them, and re-layouts: 223 us -> 2.71 us  [the longest x1 1.42 us: planes(): vec[7]]
    psum x2 -> x0, waiting for transfers between devices: 127 us -> none  [the longest x1 90.2 us: shards(): lax.psum(shares[1].astype(jnp.bfloat16), 'batch').astype(jnp.float32)]
    all_gather x9 -> x0, blocking collectives: 123 us -> none  [the longest x4 56.9 us: entering(): everything = jax.tree.map(lambda part: lax.all_gather(part, axis), value)]
    pad x56 -> x0, local copies, waits for them, and re-layouts: 111 us -> none  [the longest x28 59.4 us: shards(): lax.associative_scan(link, (carried, drive_term), axis=0)]
    dot_general x25 -> x0, matrix products: 108 us -> none  [the longest x1 9.87 us: shards(): jnp.einsum('td,fd->tf', grad_top, gathered[14], preferred_element_type=jn...]
    add x46 -> x0, other arithmetic: 60.9 us -> none  [the longest x16 22 us: shards(): lax.associative_scan(link, (next_decay, direct), axis=0, reverse=True)]
  transfers between devices with their start and end apart: 19 -> 0, of which waited for: 10 -> 0; matrix products, arithmetic and copies ran while one was open for 23% -> 0% of each run, Pallas kernels for 0% -> 0%
where the time goes in v1:
time: 428 us; the launch traced here: 425 us
  Pallas kernels  409 us (96%)
  local copies, waits for them, and re-layouts  8.67 us (2%)
  other arithmetic  6.22 us (1%)
    pallas_call x4, Pallas kernels, kernel_call(): pl.pallas_call(kernel, out_shape=list(outs.values()), in_specs=[spec] * l...  409 us

profile of v1, /device:TPU:19, one launch (start us, length us, event | category | flops | bytes accessed | tf_op | source)
XLA Modules:
  0.0 424.7 jit_solution(4594366953418264794)
XLA Ops:
  0.7 0.8 reduce-window.9
  1.5 0.7 fusion.9
  2.1 0.7 bitcast_convert_fusion
  2.8 0.1 pad.11.clone
  2.9 0.1 pad_maximum_fusion
  3.0 0.7 maximum_convert_fusion
  3.6 0.7 broadcast_in_dim.63
  4.3 0.7 broadcast_in_dim.64
  5.0 0.7 broadcast_in_dim.65
  5.6 0.7 fusion.8
  6.3 0.7 broadcast_in_dim.59.refs_3_.refs_7_
  7.0 0.7 concatenate.13
  7.7 0.7 fusion.refs_2_
  8.4 158.5 %recur_front.1 = (bf16[8,256,1024]{2,1,0:T(8,128)(2,1)}, bf16[8,256,1024]{2,1,0:T(8,128)(2,1)}, bf16[1024,512]{1,0:T(8,128)(2,1)}, bf16[256,1024]{1,0:T(8,128)(2...) custom-call(bf16[256,1024]{1,0:T(8,128)(2,1)} %bitcast.28, ...), custom_call_target="tpu_custom_call" | custom-call | tf_op jit(solution)/shard_map/recur_front/pallas_call | solution.py:257
  166.9 82.0 %feed_forward.1 = (bf16[256,1024]{1,0:T(8,128)(2,1)}, f32[256,1024]{1,0:T(8,128)}, bf16[256,1024]{1,0:T(8,128)(2,1)}, f32[8,1024]{1,0:T(8,128)}, bf16[4,256,768]...) custom-call(bf16[256,1024]{1,0:T(8,128)(2,1)} %get-tuple-element.65.refs_0_, bf16[256,1024]{1,0:T(8,128)(2,1)} %bitcast.31, ...), custom_call_target="tpu_custom_call" | custom-call | tf_op jit(solution)/shard_map/feed_forward/pallas_call | solution.py:257
  249.0 162.6 %recur_back.1 = (f32[256,1024]{1,0:T(8,128)}, bf16[8,128,768]{2,1,0:T(8,128)(2,1)}, bf16[4,96,1024]{2,1,0:T(8,128)(2,1)}, bf16[8,128,256]{2,1,0:T(8,128)(2,1)}, ...) custom-call(bf16[256,1024]{1,0:T(8,128)(2,1)} %bitcast.29, ...), custom_call_target="tpu_custom_call" | custom-call | tf_op jit(solution)/shard_map/recur_back/pallas_call | solution.py:257
  411.6 0.0 copy-start.1
  411.6 1.3 slice_bitcast_fusion.1
  412.9 0.0 copy-start
  412.9 5.9 %assemble.1 = (f32[128,1536]{1,0:T(8,128)}, f32[128,1536]{1,0:T(8,128)}, f32[128,3072]{1,0:T(8,128)}, f32[128,3072]{1,0:T(8,128)}, f32[384,1024]{1,0:T(8,128)}, ...) custom-call(bf16[8,128,768]{2,1,0:T(8,128)(2,1)} %get-tuple-element., ...), custom_call_target="tpu_custom_call" | custom-call | tf_op jit(solution)/shard_map/assemble/pallas_call | solution.py:257
  418.7 1.3 slice.25
  420.0 1.4 fusion.10
  421.5 0.8 slice_bitcast_fusion
  422.3 0.6 copy.36
  422.9 0.0 copy-done.1
  422.9 0.8 copy.39
  423.7 0.0 copy-done
  423.7 1.0 copy.40
  (3 shorter events, 0.0 us)
Async XLA Ops:
  411.6 11.3 %copy-start.1 = (bf16[256,1024]{1,0:T(8,128)(2,1)S(1)}, bf16[256,1024]{1,0:T(8,128)(2,1)}, u32[]{:S(2)}) copy-start(bf16[256,1024]{1,0:T(8,128)(2,1)} %get-tuple-element.72) | copy-start | bytes 1572868
  412.9 10.8 %copy-start = (f32[256,1024]{1,0:T(8,128)S(1)}, f32[256,1024]{1,0:T(8,128)}, u32[]{:S(2)}) copy-start(f32[256,1024]{1,0:T(8,128)} %get-tuple-element.93) | copy-start | bytes 3145732

commit v2 on v0

--- a/solution.py
+++ b/solution.py
@@ -1,10 +1,1345 @@
+import functools
+import types
+
 import jax
 import jax.numpy as jnp
 from jax import lax
+from jax.experimental import pallas as pl
+from jax.experimental.pallas import tpu as pltpu
 from jax.sharding import PartitionSpec as P
 
 NORM_EPS = 1e-06
 DECAY_SCALE = 8.0
+BF = jnp.bfloat16
+F32 = jnp.float32
+GELU_SCALE = 0.7978845608028654
+GELU_CUBE = 0.044715
+TILE = 64
+NN = (((1,), (0,)), ((), ()))
+NT = (((1,), (1,)), ((), ()))
+TN = (((0,), (0,)), ((), ()))
+
+
+def dot(left, right, dims=NN):
+    return lax.dot_general(left, right, dims, preferred_element_type=F32)
+
+
+def loop(count, body):
+    def step(i, carry):
+        body(i)
+        return carry
+
+    lax.fori_loop(0, count, step, 0)
+
+
+class Net:
+    def __init__(self, r):
+        self.send, self.recv, self.count = r.send, r.recv, 0
+        self.here, self.here_count = r.local, 0
+        self.pending = []
+        self.p = lax.axis_index("batch")
+        self.q = lax.axis_index("seq")
+        self.z = lax.div(self.q, 2)
+        self.c = lax.rem(self.q, 2)
+        self.o = 1 - self.c
+        p = self.p
+        self.near = (p, p + 1 - 2 * lax.rem(p, 2), lax.rem(p + 2, 4), 3 - p)
+
+    def plane(self, k, core):
+        return {"batch": self.near[k], "seq": self.z * 2 + core}
+
+    def line(self, z, core):
+        return {"batch": self.p, "seq": z * 2 + core}
+
+    def up(self, k):
+        return lax.rem(self.z + k, 4)
+
+    def down(self, k):
+        return lax.rem(self.z + 4 - k, 4)
+
+    def slot(self, k, core):
+        return self.near[k] * 2 + core
+
+    def greet(self):
+        barrier = pltpu.get_barrier_semaphore()
+        partners = [self.plane(k, core) for k in (1, 2, 3) for core in (0, 1)]
+        partners += [self.line(self.up(k), core) for k in (1, 2, 3) for core in (0, 1)]
+        partners += [self.line(self.z, self.o)]
+        for partner in partners:
+            pl.semaphore_signal(barrier, inc=1, device_id=partner, device_id_type=pl.DeviceIdType.MESH)
+        pl.semaphore_wait(barrier, len(partners))
+
+    def reserve(self, count):
+        first = self.count
+        self.count += count
+        return first
+
+    def describe(self, src, dst, device, send_at, recv_at):
+        return pltpu.make_async_remote_copy(
+            src_ref=src,
+            dst_ref=dst,
+            send_sem=self.send.at[send_at],
+            recv_sem=self.recv.at[recv_at],
+            device_id=device,
+            device_id_type=pl.DeviceIdType.MESH,
+        )
+
+    def copy(self, src, dst, device, sent=None):
+        at = self.reserve(1)
+        made = self.describe(src, dst, device, at, at)
+        made.start()
+        (self.pending if sent is None else sent).append(made)
+        return made
+
+    def local(self, src, dst):
+        made = pltpu.make_async_copy(src, dst, self.here.at[self.here_count])
+        self.here_count += 1
+        made.start()
+        return made
+
+    def drain(self):
+        assert (self.count, self.here_count) == (self.send.shape[0], self.here.shape[0]), (self.count, self.here_count)
+        for made in self.pending:
+            made.wait_send()
+        self.pending = []
+
+
+class Gather:
+    def __init__(self, net, own, everything):
+        self.net, self.own, self.all = net, own, everything
+        self.sent = []
+        self.half = everything.shape[1] // 2
+
+    def part(self, slot, h):
+        return self.all.at[slot, pl.ds(h * self.half, self.half)]
+
+    def start(self):
+        net = self.net
+        mine = net.slot(0, net.c)
+        low, high = self.own.at[pl.ds(0, self.half)], self.own.at[pl.ds(self.half, self.half)]
+        self.s = []
+        self.x0 = net.copy(low, self.part(mine, 0), net.plane(1, net.c), self.sent)
+        self.y1 = net.copy(high, self.part(mine, 1), net.plane(2, net.c), self.sent)
+        self.x1 = net.copy(high, self.part(mine, 1), net.plane(1, net.c), self.sent)
+        self.y0 = net.copy(low, self.part(mine, 0), net.plane(2, net.c), self.sent)
+        self.s.append(net.copy(self.own, self.all.at[mine], net.plane(0, net.o), self.sent))
+
+    def forward(self):
+        net = self.net
+        self.x0.wait_recv()
+        mine = self.part(net.slot(1, net.c), 0)
+        self.d0 = net.copy(mine, mine, net.plane(2, net.c), self.sent)
+        self.y1.wait_recv()
+        mine = self.part(net.slot(2, net.c), 1)
+        self.d1 = net.copy(mine, mine, net.plane(1, net.c), self.sent)
+
+    def across(self, k):
+        net = self.net
+        mine = self.all.at[net.slot(k, net.c)]
+        self.s.append(net.copy(mine, mine, net.plane(0, net.o), self.sent))
+
+    def middle(self):
+        self.x1.wait_recv()
+        self.across(1)
+        self.y0.wait_recv()
+        self.across(2)
+
+    def last(self):
+        self.d0.wait_recv()
+        self.d1.wait_recv()
+        self.across(3)
+
+    def sibling(self, k):
+        self.s[k].wait_recv()
+
+    def release(self):
+        for made in self.sent:
+            made.wait_send()
+        self.sent = []
+
+
+class LineGather:
+    def __init__(self, net, own, first, place):
+        self.net, self.own, self.first, self.place = net, own, first, place
+        self.at = net.reserve(4 * len(own))
+
+    def made(self, k, j):
+        net = self.net
+        src, core = self.own[j]
+        at = self.at + 4 * j + k - 1
+        return net.describe(src, self.first(j), net.line(net.up(k), core), at, at)
+
+    def handed(self, j):
+        net = self.net
+        far = 6 - 3 * net.z
+        here = self.place(j, far)
+        at = self.at + 4 * j
+        return net.describe(here, here, net.line(3 - far, net.c), at + 3, at + 2 * net.z - 2)
+
+    def direct(self, k, body):
+        z = self.net.z
+        if k == 2:
+            body()
+        else:
+            pl.when(z != (0 if k == 3 else 3))(body)
+
+    def start(self, k, items):
+        def send():
+            for j in items:
+                self.made(k, j).start()
+
+        self.direct(k, send)
+
+    def inside(self, body):
+        z = self.net.z
+        pl.when((z == 1) | (z == 2))(body)
+
+    def relay(self):
+        @self.inside
+        def _():
+            for j in range(len(self.own)):
+                self.made(2, j).wait_recv()
+                self.handed(j).start()
+
+    def end(self):
+        z = self.net.z
+        for k in (1, 3):
+            for j in range(len(self.own)):
+                self.made(k, j).wait_recv()
+
+        @pl.when((z == 0) | (z == 3))
+        def _():
+            for j in range(len(self.own)):
+                self.made(2, j).wait_recv()
+
+    def drain(self):
+        for k in (1, 2, 3):
+
+            def wait(k=k):
+                for j in range(len(self.own)):
+                    self.made(k, j).wait_send()
+
+            self.direct(k, wait)
+
+        @self.inside
+        def _():
+            for j in range(len(self.own)):
+                self.handed(j).wait_send()
+
+
+class LineSum:
+    def __init__(self, net, block, slot):
+        self.net, self.block, self.slot = net, block, slot
+        self.at = net.reserve(3)
+
+    def made(self, k):
+        net = self.net
+        at = self.at + k - 1
+        to = lax.rem(2 * net.z + 1, 5) if k == 2 else net.up(k)
+        return net.describe(self.block(net.up(k)), self.slot(k), net.line(to, net.c), at, at)
+
+    def start(self):
+        z = self.net.z
+        self.made(2).start()
+        pl.when(z != 1)(lambda: self.made(1).start())
+        pl.when(z != 2)(lambda: self.made(3).start())
+
+    def relay(self, step=16):
+        z = self.net.z
+
+        @pl.when((z == 1) | (z == 2))
+        def _():
+            self.made(2).wait_recv()
+            mine, extra = self.block(3 - z), self.slot(2)
+
+            def body(i):
+                rows = pl.ds(pl.multiple_of(i * step, step), step)
+                mine[rows, :] = (mine[rows, :].astype(F32) + extra[rows, :].astype(F32)).astype(BF)
+
+            loop(mine.shape[0] // step, body)
+
+        pl.when(z == 1)(lambda: self.made(1).start())
+        pl.when(z == 2)(lambda: self.made(3).start())
+
+    def end(self, dst, step=16):
+        z = self.net.z
+        self.made(1).wait_recv()
+        self.made(3).wait_recv()
+        edge = (z == 0) | (z == 3)
+        pl.when(edge)(lambda: self.made(2).wait_recv())
+        share = jnp.where(edge, 1.0, 0.0)
+        own = self.block(z)
+
+        def body(i):
+            rows = pl.ds(pl.multiple_of(i * step, step), step)
+            value = own[rows, :].astype(F32) + share * self.slot(2)[rows, :].astype(F32)
+            value = value + self.slot(1)[rows, :].astype(F32) + self.slot(3)[rows, :].astype(F32)
+            dst[rows, :] = value.astype(BF)
+
+        loop(dst.shape[0] // step, body)
+
+    def drain(self):
+        for k in (1, 2, 3):
+            self.made(k).wait_send()
+
+
+class Reduce:
+    def __init__(self, net, r, value):
+        self.net, self.value = net, value
+        self.keep, self.out, self.into = r.rs_keep, r.rs_out, r.rs_in
+        self.xs, self.ys, self.xr, self.yr = r.rs_xs, r.rs_ys, r.rs_xr, r.rs_yr
+        self.half = self.keep.shape[1]
+        self.cross = [None] * 4
+        self.sent = []
+
+    def other(self, k):
+        net = self.net
+        self.out[k] = self.value(k, net.o).astype(BF)
+        self.cross[k] = net.copy(self.out.at[k], self.into.at[k], net.plane(0, net.o), self.sent)
+
+    def mine(self, k):
+        self.cross[k].wait_recv()
+        value = self.value(k, self.net.c) + self.into[k].astype(F32)
+        return value[: self.half], value[self.half :]
+
+    def send(self, src, dst, j, k):
+        net = self.net
+        return net.copy(src.at[j], dst.at[j], net.plane(k, net.c), self.sent)
+
+    def far(self):
+        low, high = self.mine(3)
+        self.xs[0] = low.astype(BF)
+        self.x0 = self.send(self.xs, self.xr, 0, 1)
+        self.ys[0] = high.astype(BF)
+        self.y0 = self.send(self.ys, self.yr, 0, 2)
+
+    def near(self):
+        low, high = self.mine(1)
+        self.xs[1] = low.astype(BF)
+        self.x1 = self.send(self.xs, self.xr, 1, 1)
+        self.keep[2] = high
+        low, high = self.mine(2)
+        self.ys[1] = high.astype(BF)
+        self.y1 = self.send(self.ys, self.yr, 1, 2)
+        self.keep[3] = low
+
+    def relay(self):
+        self.x0.wait_recv()
+        self.ys[2] = (self.keep[3] + self.xr[0].astype(F32)).astype(BF)
+        self.y2 = self.send(self.ys, self.yr, 2, 2)
+        self.y0.wait_recv()
+        self.xs[2] = (self.keep[2] + self.yr[0].astype(F32)).astype(BF)
+        self.x2 = self.send(self.xs, self.xr, 2, 1)
+
+    def own(self):
+        self.keep[0], self.keep[1] = self.mine(0)
+
+    def finish(self):
+        for made in (self.x1, self.y1, self.x2, self.y2):
+            made.wait_recv()
+        for made in self.sent:
+            made.wait_send()
+        self.sent = []
+
+    def total(self, h, i, step):
+        rows = pl.ds(pl.multiple_of(i * step, step), step)
+        first, second = (self.xr, self.yr) if h == 0 else (self.yr, self.xr)
+        return self.keep[h, rows, :] + first[1, rows, :].astype(F32) + second[2, rows, :].astype(F32)
+
+
+def reduce_scratch(rows, width):
+    half = rows // 2
+    return dict(
+        rs_keep=pltpu.VMEM((4, half, width), F32),
+        rs_out=pltpu.VMEM((4, rows, width), BF),
+        rs_in=pltpu.VMEM((4, rows, width), BF),
+        rs_xs=pltpu.VMEM((3, half, width), BF),
+        rs_ys=pltpu.VMEM((3, half, width), BF),
+        rs_xr=pltpu.VMEM((3, half, width), BF),
+        rs_yr=pltpu.VMEM((3, half, width), BF),
+    )
+
+
+def kernel_call(body, ins, outs, scratch, copies, local, far):
+    names = list(ins) + list(outs) + list(scratch)
+    near = pl.BlockSpec(memory_space=pltpu.VMEM)
+    away = pl.BlockSpec(memory_space=pl.ANY)
+    shapes = list(scratch.values())
+    if copies:
+        names += ["send", "recv", "local"]
+        shapes += [pltpu.SemaphoreType.DMA((n,)) for n in (copies, copies, local)]
+
+    def kernel(*refs):
+        body(types.SimpleNamespace(**dict(zip(names, refs))))
+
+    params = dict(vmem_limit_bytes=62 * 2**20)
+    if copies:
+        params.update(collective_id=0, has_side_effects=True)
+    results = pl.pallas_call(
+        kernel,
+        out_shape=list(outs.values()),
+        in_specs=[away if name in far else near for name in ins],
+        out_specs=[away if name in far else near for name in outs],
+        scratch_shapes=shapes,
+        compiler_params=pltpu.CompilerParams(**params),
+        name=body.__name__,
+    )(*ins.values())
+    return dict(zip(outs, results))
+
+
+def array(*shape, dtype=F32):
+    return jax.ShapeDtypeStruct(shape, dtype)
+
+
+def gelu_parts(v):
+    square = v * v
+    t = jnp.tanh(GELU_SCALE * v * (1.0 + GELU_CUBE * square))
+    half = 0.5 + 0.5 * t
+    slope = half + 0.5 * v * (1.0 - t * t) * (GELU_SCALE * (1.0 + 3.0 * GELU_CUBE * square))
+    return v * half, slope
+
+
+def decay_parts(sr, rate):
+    log_a = -DECAY_SCALE * sr * rate
+    a = jnp.exp(log_a)
+    y = 2.0 * log_a
+    series = 1.0 + y * (1 / 6) * (1.0 + y * (1 / 7))
+    for n in (5, 4, 3, 2):
+        series = 1.0 + y * (1 / n) * series
+    m2 = jnp.where(y > -0.35, -y * series, 1.0 - a * a)
+    return a, jnp.maximum(m2, 1e-36)
+
+
+def column_sum(value):
+    return jnp.sum(value.reshape(-1, 8, 128), axis=0)
+
+
+def scan_slabs(decay, value, reverse):
+    count = decay.shape[1] // 8
+    row = lax.broadcasted_iota(jnp.int32, (8, 128), 0)
+
+    def step(i, carry):
+        t = count - 1 - i if reverse else i
+        at = pl.ds(pl.multiple_of(t * 8, 8), 8)
+        done = []
+        for s in range(8):
+            pc, vc = carry[s]
+            p, own = decay[s, at, :], value[s, at, :]
+            v = p * own if reverse else own
+            for d in (1, 2, 4):
+                by = 8 - d if reverse else d
+                inside = row < 8 - d if reverse else row >= d
+                v = v + p * jnp.where(inside, pltpu.roll(v, by, 0), 0.0)
+                p = p * jnp.where(inside, pltpu.roll(p, by, 0), 1.0)
+            v = v + p * vc
+            p = p * pc
+            if reverse:
+                edge = row == 7
+                value[s, at, :] = own + jnp.where(edge, vc, pltpu.roll(v, 7, 0))
+                decay[s, at, :] = jnp.where(edge, pc, pltpu.roll(p, 7, 0))
+                last = slice(0, 1)
+            else:
+                value[s, at, :] = v
+                decay[s, at, :] = p
+                last = slice(7, 8)
+            done.append((jnp.broadcast_to(p[last], (8, 128)), jnp.broadcast_to(v[last], (8, 128))))
+        return tuple(done)
+
+    start = tuple((jnp.ones((8, 128), F32), jnp.zeros((8, 128), F32)) for _ in range(8))
+    return lax.fori_loop(0, count, step, start)
+
+
+def exchange_ends(r, net, ends, at):
+    for s in range(8):
+        r.tot[at, net.z, 0, s : s + 1, :] = ends[s][0][0:1, :]
+        r.tot[at, net.z, 1, s : s + 1, :] = ends[s][1][0:1, :]
+    mine = r.tot.at[at, net.z]
+    return [net.copy(mine, mine, net.line(net.up(k), net.c)) for k in (1, 2, 3)]
+
+
+def entering_states(r, net, copies, at, reverse):
+    for made in copies:
+        made.wait_recv()
+    state = jnp.zeros((8, 128), F32)
+    for i in range(4):
+        z = 3 - i if reverse else i
+        new = r.tot[at, z, 0] * state + r.tot[at, z, 1]
+        state = jnp.where((z > net.z) if reverse else (z < net.z), new, state)
+    r.inc[...] = state
+
+
+def tile_rows(i):
+    return pl.ds(pl.multiple_of(i * TILE, TILE), TILE)
+
+
+def layer(r):
+    r.do_all = r.x_all
+    r.dconv = r.gb
+    r.dgi = r.dgu
+    r.ug, r.ul = r.d_res.at[:, 0:384], r.d_res.at[:, 384:768]
+    r.ga = [r.hid.at[i, :, 0:256] for i in range(4)]
+    r.gb2 = [r.hid.at[4 + i, 0:128, 0:256] for i in range(4)]
+    net = Net(r)
+    p, z, c, o, q = net.p, net.z, net.c, net.o, net.q
+    sibling = net.plane(0, o)
+    mine = net.slot(0, c)
+    cols = r.wgu_out.shape[2]
+    piece = cols // 4
+    down = pl.ds(pl.multiple_of(p * piece, 16), piece)
+    quarter = pl.ds(pl.multiple_of(p * 48, 16), 48)
+    staged = []
+    for j in range(8):
+        lanes = pl.ds(j * cols, cols)
+        staged.append(net.local(r.wmg.at[:, lanes], r.hid.at[j, pl.ds(0, 128)]))
+        staged.append(net.local(r.wmu.at[:, lanes], r.hid.at[j, pl.ds(128, 128)]))
+    width = 3 * 128
+    first = pl.multiple_of(p * width, 128)
+    chip = pl.ds(first, width)
+    own_lanes = pl.ds(pl.multiple_of(c * width, 128), width)
+    wi_rows, wg_rows = pl.ds(128, 128), pl.ds(0, 128)
+    placed = [
+        net.local(r.wg.at[:, chip], r.wgi3.at[z, wg_rows, own_lanes]),
+        net.local(r.wi.at[:, chip], r.wgi3.at[z, wi_rows, own_lanes]),
+        net.local(r.wmd.at[down], r.wmd_all.at[z]),
+        net.local(r.wout.at[quarter], r.wq.at[z]),
+        net.local(r.wr.at[quarter], r.gq.at[z, :, pl.ds(0, 128)]),
+        net.local(r.wv.at[quarter], r.gq.at[z, :, pl.ds(128, 128)]),
+        net.local(r.g, r.g_all.at[mine]),
+    ]
+    r.lens_out[0:1, 0:5] = r.lens[...].astype(F32)
+    net.greet()
+    r.small_all[q] = r.small[...]
+    r.lens_all[p] = r.lens_out[...]
+    small = [net.copy(r.small, r.small_all.at[q], net.line(net.up(k), core)) for k in (1, 2, 3) for core in (c, o)]
+    small.append(net.copy(r.small, r.small_all.at[q], sibling))
+    lens = [net.copy(r.lens_out, r.lens_all.at[p], net.plane(k, c)) for k in (1, 2, 3)]
+    tokens = Gather(net, r.x, r.x_all)
+    tokens.start()
+    theirs = pl.ds(pl.multiple_of(c * width + o * 128, 128), 256)
+
+    def along(ref, sent=None):
+        return [net.copy(ref, ref, net.line(net.up(k), c), sent) for k in (1, 2, 3)]
+
+    handed = []
+
+    def heads_start(rows):
+        here = r.wgi3.at[z, rows, theirs]
+        return along(r.wgi3.at[z, rows, own_lanes], handed), [net.copy(here, here, sibling, handed)]
+
+    for made in placed:
+        made.wait()
+    heads_in, heads_in_over = heads_start(wi_rows)
+    gates_in = along(r.gq.at[z])
+
+    def hand_over(copies, rows, over):
+        for k in (1, 2, 3):
+            copies[k - 1].wait_recv()
+            here = r.wgi3.at[net.down(k), rows, theirs]
+            over.append(net.copy(here, here, sibling, handed))
+
+    def arrange(over, rows, lanes):
+        for made in over:
+            made.wait_recv()
+        for core in range(2):
+            cols_in = pl.ds(pl.multiple_of(core * width + c * 128, 128), 256)
+            for at in range(4):
+                to = slice((at * 2 + core) * 128, (at * 2 + core + 1) * 128)
+                r.w2[to, lanes] = r.wgi3[at, rows, cols_in]
+
+    def exchange(arrivals, src, dst):
+        for made in arrivals:
+            made.wait_recv()
+        dst[c, quarter, :] = src[p]
+        return [net.copy(src.at[net.near[k]], dst.at[c, quarter], net.plane(k, c)) for k in (1, 2, 3)]
+
+    def share(copies, dst):
+        for made in copies:
+            made.wait_recv()
+        return net.copy(dst.at[c], dst.at[c], sibling)
+
+    selects = []
+    k_at = lax.broadcasted_iota(jnp.int32, (cols, cols), 0)
+    j_at = lax.broadcasted_iota(jnp.int32, (cols, cols), 1)
+    for part in range(4):
+        inside = (j_at >= part * piece) & (j_at < (part + 1) * piece)
+        chosen = inside & (k_at == j_at + (p - part) * piece)
+        selects.append(jnp.where(chosen, 1.0, 0.0).astype(BF))
+    for made in staged:
+        made.wait()
+    for which in range(2):
+        rows = slice(which * 128, (which + 1) * 128)
+        for core in (0, 1):
+            picked = None
+            for part in range(4):
+                term = dot(r.hid[part * 2 + core, rows, :], selects[part])
+                picked = term if picked is None else picked + term
+            r.wgu_out[core, rows, :] = picked.astype(BF)
+    for made in small + lens:
+        made.wait_recv()
+    low, high = r.small_all[2 * p].astype(F32), r.small_all[2 * p + 1].astype(F32)
+    at_first = jnp.concatenate([low[:, :192], high[:, :64]], axis=1)
+    at_second = jnp.concatenate([low[:, 128:192], high[:, :192]], axis=1)
+    both = lax.select(c == 0, at_first, at_second)
+    for n in range(2):
+        r.chan[n] = both[:, n * 128 : (n + 1) * 128]
+        lam = -r.chan[n, 7:8, :]
+        e = jnp.exp(-jnp.abs(lam))
+        series = 1.0 - e * (6 / 7)
+        for k in (6, 5, 4, 3, 2):
+            series = 1.0 - e * ((k - 1) / k) * series
+        rate = jnp.maximum(lam, 0.0) + jnp.where(e < 0.05, e * series, jnp.log(1.0 + e))
+        r.chan[n, 7:8, :] = rate
+        r.chan[n, 8:9, :] = jax.nn.sigmoid(lam)
+    for i in range(8):
+        gains = r.small_all[i].astype(F32)[10:11, :]
+        r.gain[0:1, i * 128 : (i + 1) * 128] = gains[:, 0:128]
+        r.gain[1:2, i * 128 : (i + 1) * 128] = gains[:, 128:256]
+    gain = r.gain[0:1, :]
+    for b in range(4):
+        start = jnp.zeros((1, 128), F32)
+        for row in range(5):
+            r.starts_all[b, row : row + 1, :] = start
+            start = start + jnp.broadcast_to(r.lens_all[b, 0:1, row : row + 1], (1, 128))
+
+
+    def offset_rows(i):
+        b, tile = lax.div(i, 13), lax.rem(i, 13)
+        starts = r.starts_all[b]
+        at = lax.convert_element_type(z * 512 + tile * 40, F32)
+        at = at + lax.broadcasted_iota(jnp.int32, (40, 128), 0).astype(F32)
+        begun = jnp.zeros((40, 128), F32)
+        for row in range(1, 5):
+            start = starts[row : row + 1, :]
+            begun = jnp.where(at >= start, start, begun)
+        r.off[b, pl.ds(pl.multiple_of(tile * 40, 8), 40), :] = at - begun
+
+    loop(52, offset_rows)
+
+    def normalise(slot):
+        def body(i):
+            rows = pl.ds(pl.multiple_of(i * 32, 32), 32)
+            v = r.x_all[slot, rows, :].astype(F32)
+            s = lax.rsqrt(jnp.mean(v * v, axis=-1, keepdims=True) + NORM_EPS)
+            r.normed[slot, rows, :] = (v * s * gain).astype(BF)
+
+        loop(8, body)
+
+    r.x_all[mine] = r.x[...]
+    normalise(mine)
+    tokens.sibling(0)
+    normalise(net.slot(0, o))
+    tokens.forward()
+    out_in = along(r.wq.at[z])
+    heads_gate, heads_gate_over = heads_start(wg_rows)
+    hand_over(heads_in, wi_rows, heads_in_over)
+    tokens.middle()
+    gates_out = exchange(gates_in, r.gq, r.g3)
+    for k in (1, 2):
+        normalise(net.slot(k, c))
+    for k in (1, 2):
+        tokens.sibling(k)
+        normalise(net.slot(k, o))
+    arrange(heads_in_over, slice(128, 256), slice(256, 512))
+
+    def project_inner(slot):
+        b, half = lax.div(slot, 2), lax.rem(slot, 2)
+        at = pl.multiple_of(half * 256, 256)
+        inner = dot(r.normed[slot], r.w2[:, 256:512]).astype(BF).astype(F32)
+        for n in range(2):
+            r.inner[b * 2 + n, pl.ds(at + 8, 256), :] = inner[:, n * 128 : (n + 1) * 128]
+
+    def project_gate(slot):
+        b, half = lax.div(slot, 2), lax.rem(slot, 2)
+        at = pl.multiple_of(half * 256, 256)
+        gate = dot(r.normed[slot], r.w2[:, 0:256])
+        for n in range(2):
+            r.gp[b * 2 + n, pl.ds(at, 256), :] = gate[:, n * 128 : (n + 1) * 128]
+
+    for k in (0, 1, 2):
+        project_inner(net.slot(k, c))
+        project_inner(net.slot(k, o))
+    tokens.last()
+    normalise(net.slot(3, c))
+    project_inner(net.slot(3, c))
+    tokens.sibling(3)
+    normalise(net.slot(3, o))
+    project_inner(net.slot(3, o))
+    edge = net.reserve(1)
+
+    def edge_copy():
+        return net.describe(
+            r.inner.at[:, pl.ds(512, 8)], r.inner.at[:, pl.ds(0, 8)], net.line(net.up(1), c), edge, edge
+        )
+
+    @pl.when(z < 3)
+    def _():
+        edge_copy().start()
+
+    @pl.when(z == 0)
+    def _():
+        r.inner[:, 0:8, :] = jnp.zeros((8, 8, 128), F32)
+
+    gates_over = share(gates_out, r.g3)
+    stored = net.local(r.normed, r.normed_far)
+    tokens.release()
+    gates_over.wait_recv()
+    for i in range(4):
+        at = c * 128 + i * 64
+        value = r.g3[lax.div(at, 192), pl.ds(pl.multiple_of(lax.rem(at, 192), 64), 64), :]
+        r.wri[i // 2, (i % 2) * 64 : (i % 2 + 1) * 64, :] = value
+
+    @pl.when(z > 0)
+    def _():
+        edge_copy().wait_recv()
+
+
+    def conv_tile(i):
+        b, tile = lax.div(i, 8), lax.rem(i, 8)
+        rows = tile_rows(tile)
+        offset = r.off[b, rows, :]
+        for n in range(2):
+            s = b * 2 + n
+            window = r.inner[s, pl.ds(pl.multiple_of(tile * TILE, 8), TILE + 8), :]
+            chan = r.chan[n]
+            total = chan[4:5, :] + chan[0:1, :] * window[8:, :]
+            for k in (1, 2, 3):
+                total = total + chan[k : k + 1, :] * jnp.where(offset >= k, window[8 - k : TILE + 8 - k, :], 0.0)
+            r.conv[s, rows, :] = total.astype(BF)
+
+    loop(32, conv_tile)
+    feed = LineGather(
+        net,
+        [(r.wgu_out.at[core], core) for core in (c, o)],
+        lambda j: r.wgu_all.at[q],
+        lambda j, at: r.wgu_all.at[at * 2 + (c, o)[j]],
+    )
+    feed_down = LineGather(net, [(r.wmd.at[down], c)], lambda j: r.wmd_all.at[z], lambda j, at: r.wmd_all.at[at])
+    feed.start(2, (0,))
+    out_rows_in = exchange(out_in, r.wq, r.w3)
+    cots = Gather(net, r.g_all.at[mine], r.g_all)
+    cots.start()
+
+    def gate_products(i):
+        s, half = lax.div(i, 2), lax.rem(i, 2)
+        n = lax.rem(s, 2)
+        rows = pl.ds(pl.multiple_of(half * 256, 256), 256)
+        pre = dot(r.conv[s, rows, :], r.wri[n])
+        r.sr[s, rows, :] = pre[:, :128]
+        r.si[s, rows, :] = pre[:, 128:]
+
+    loop(16, gate_products)
+
+    def terms(b):
+        starts_b = r.starts_all[b]
+
+        def tile(i, sums):
+            rows = tile_rows(i)
+            offset = r.off[b, rows, :]
+            at = lax.convert_element_type(z * 512 + i * TILE, F32)
+            begun = at + lax.broadcasted_iota(jnp.int32, (TILE, 128), 0).astype(F32) - offset
+            restart = offset == 0.0
+            added = []
+            for n in range(2):
+                s = b * 2 + n
+                chan = r.chan[n]
+                sr = jax.nn.sigmoid(r.sr[s, rows, :] + chan[5:6, :])
+                si = jax.nn.sigmoid(r.si[s, rows, :] + chan[6:7, :])
+                r.sr[s, rows, :] = sr
+                r.si[s, rows, :] = si
+                a, m2 = decay_parts(sr, chan[7:8, :])
+                r.dec[s, rows, :] = jnp.where(restart, 0.0, a)
+                m = jnp.where(restart, 1.0, jnp.sqrt(m2))
+                r.drv[s, rows, :] = m * si * r.conv[s, rows, :].astype(F32)
+                for row in range(5):
+                    inside = jnp.where(begun == starts_b[row : row + 1, :], a, 0.0)
+                    added.append(sums[n * 5 + row] + column_sum(inside))
+            return tuple(added)
+
+        sums = lax.fori_loop(0, 512 // TILE, tile, tuple(jnp.zeros((8, 128), F32) for _ in range(10)))
+        for n in range(2):
+            rows = [jnp.sum(part, axis=0, keepdims=True) for part in sums[n * 5 : n * 5 + 5]]
+            r.rs_all[z, b * 2 + n] = jnp.concatenate(rows + [jnp.zeros((3, 128), F32)], axis=0)
+
+    loop(4, terms)
+    ends = scan_slabs(r.dec, r.drv, False)
+    ends = exchange_ends(r, net, ends, 0)
+    feed.start(2, (1,))
+    feed.start(1, (0, 1))
+    feed.start(3, (0, 1))
+    r.wgu_all[q] = r.wgu_out[c]
+    feed_over = net.copy(r.wgu_out.at[o], r.wgu_all.at[q], sibling)
+    hand_over(heads_gate, wg_rows, heads_gate_over)
+    cots.forward()
+    arrange(heads_gate_over, slice(0, 128), slice(0, 256))
+    for made in handed:
+        made.wait_send()
+    for k in (2, 1, 3):
+        feed_down.start(k, (0,))
+    for slot in range(8):
+        project_gate(slot)
+
+    def gelu_tile(i):
+        s, rows = lax.div(i, 8), tile_rows(lax.rem(i, 8))
+        v = r.gp[s, rows, :]
+        t = jnp.tanh(GELU_SCALE * v * (1.0 + GELU_CUBE * v * v))
+        r.gb[s, rows, :] = 0.5 * v * (1.0 + t)
+
+    loop(64, gelu_tile)
+    out_over = share(out_rows_in, r.w3)
+    entering_states(r, net, ends, 0, False)
+    row_sums = [net.copy(r.rs_all.at[z], r.rs_all.at[z], net.line(net.up(k), c)) for k in (1, 2, 3)]
+    out_over.wait_recv()
+
+    def own_rows(i):
+        at = c * 128 + i * 64
+        value = r.w3[lax.div(at, 192), pl.ds(pl.multiple_of(lax.rem(at, 192), 64), 64), :]
+        r.wo[pl.ds(pl.multiple_of(i * 64, 64), 64), :] = value
+
+    loop(4, own_rows)
+    for s in range(8):
+        r.states[s, 7:8, :] = r.inc[s : s + 1, :]
+
+    def mix_tile(i):
+        s, tile = lax.div(i, 8), lax.rem(i, 8)
+        b, n = lax.div(s, 2), lax.rem(s, 2)
+        rows = tile_rows(tile)
+        states = r.drv[s, rows, :] + r.dec[s, rows, :] * r.inc[pl.ds(s, 1), :]
+        r.states[s, pl.ds(pl.multiple_of(tile * TILE + 8, 8), TILE), :] = states
+        lanes = pl.ds(pl.multiple_of(n * 128, 128), 128)
+        r.mixed[b * 2 + lax.div(tile, 4), tile_rows(lax.rem(tile, 4)), lanes] = (states * r.gb[s, rows, :]).astype(BF)
+
+    loop(64, mix_tile)
+    stored.wait()
+    lane = lax.broadcasted_iota(jnp.int32, (1, 256), 1)
+    counted = jnp.where((lane >= 64 * c) & (lane < 192 + 64 * c), 1.0, 0.0)
+    counted_two = jnp.concatenate([counted, counted], axis=1)
+
+    def masked(value, mask):
+        return (value.astype(F32) * mask).astype(BF)
+
+    total = Reduce(
+        net, r, lambda k, core: dot(masked(r.mixed[net.slot(k, core)], counted), r.wo[...])
+    )
+    for k in (3, 1, 2, 0):
+        total.other(k)
+    total.far()
+    total.near()
+    cots.middle()
+    total.own()
+    cots.last()
+    for k in (0, 1, 2, 3):
+        cots.sibling(k)
+    cots.release()
+    total.relay()
+    feed_down.relay()
+    feed.relay()
+    def wmd():
+        return r.wmd_all[...].reshape(cols, -1)
+
+    total.finish()
+    gain2 = r.gain[1:2, :]
+    for h in range(2):
+
+        def residual_rows(i, h=h):
+            rows = pl.ds(pl.multiple_of(h * 128 + i * 32, 32), 32)
+            v = r.x[rows, :].astype(F32) + total.total(h, i, 32)
+            r.residual[rows, :] = v
+            s = lax.rsqrt(jnp.mean(v * v, axis=-1, keepdims=True) + NORM_EPS)
+            r.normed[mine, rows, :] = (v * s * gain2).astype(BF)
+
+        loop(4, residual_rows)
+
+    n2_all = r.normed
+    acts = Gather(net, n2_all.at[mine], n2_all)
+    acts.start()
+
+    def gate_up(which):
+        return r.wgu_all[:, which * 128 : (which + 1) * 128, :].reshape(-1, cols)
+
+    def d_normed2(k, core):
+        slot = net.slot(k, core)
+        return dot(r.dgu[slot, :, 0:cols], gate_up(0), NT) + dot(r.dgu[slot, :, cols:], gate_up(1), NT)
+
+    back = Reduce(net, r, d_normed2)
+
+    def part(k, core):
+        slot = net.slot(k, core)
+        h = n2_all[slot]
+        r.ug[...] = dot(h, gate_up(0))
+        r.ul[...] = dot(h, gate_up(1))
+
+        def body(i):
+            rows = pl.ds(pl.multiple_of(i * 32, 32), 32)
+            gelu, slope = gelu_parts(r.ug[rows, :])
+            ul, dh = r.ul[rows, :], r.dgu[slot, rows, 0:cols].astype(F32)
+            r.hid[slot, rows, :] = (gelu * ul).astype(BF)
+            r.dgu[slot, rows, 0:cols] = (dh * ul * slope).astype(BF)
+            r.dgu[slot, rows, cols:] = (dh * gelu).astype(BF)
+
+        loop(8, body)
+
+    feed_down.end()
+    for slot in range(8):
+        r.dgu[slot, :, 0:cols] = dot(r.g_all[slot], wmd(), NT).astype(BF)
+    feed_over.wait_recv()
+    feed.end()
+    part(0, c)
+    acts.sibling(0)
+    part(0, o)
+    back.other(0)
+    acts.forward()
+    acts.middle()
+    part(1, c)
+    part(2, c)
+    acts.sibling(1)
+    part(1, o)
+    back.other(1)
+    acts.sibling(2)
+    part(2, o)
+    back.other(2)
+    acts.last()
+    acts.sibling(3)
+    part(3, o)
+    back.other(3)
+    part(3, c)
+    back.far()
+    back.near()
+    back.relay()
+    back.own()
+    acts.release()
+    for i in range(4):
+        rows = n2_all[:, :, i * 256 : (i + 1) * 256].reshape(-1, 256)
+        r.gm[i] = dot(rows, r.dgu[...].reshape(-1, 2 * cols), TN).astype(BF)
+
+    def gm_in(k):
+        return r.wgi3.at[k - 1]
+
+    mlp_m = LineSum(net, lambda t: r.gm.at[t], gm_in)
+    mlp_m.start()
+    hid = r.hid[...].reshape(-1, cols)
+    for half in range(2):
+        lanes = slice(half * 512, half * 512 + 512)
+        value = dot(hid, r.g_all[:, :, lanes].reshape(-1, 512), TN).astype(BF)
+        for i in range(4):
+            r.gd[i, :, lanes] = value[i * piece : (i + 1) * piece, :]
+    mlp_d = LineSum(net, lambda t: r.gd.at[t], lambda k: r.gd_in.at[k - 1])
+    mlp_d.start()
+    back.finish()
+    sums = jnp.zeros((8, r.x.shape[1]), F32)
+    for h in range(2):
+
+        def residual_back(i, sums, h=h):
+            rows = pl.ds(pl.multiple_of(h * 128 + i * 32, 32), 32)
+            v = r.residual[rows, :]
+            dn = back.total(h, i, 32)
+            s = lax.rsqrt(jnp.mean(v * v, axis=-1, keepdims=True) + NORM_EPS)
+            u = dn * gain2
+            pulled = s * u - v * (s * s * s * jnp.mean(u * v, axis=-1, keepdims=True))
+            d_res = r.g_all[mine, rows, :].astype(F32) + pulled
+            r.d_res[rows, :] = d_res
+            r.do_all[mine, rows, :] = d_res.astype(BF)
+            return sums + jnp.sum((dn * v * s).reshape(4, 8, -1), axis=0)
+
+        sums = lax.fori_loop(0, 4, residual_back, sums)
+    r.gain2_sum[...] = sums
+
+    owners, returned = [], []
+
+    def to_owners(src, dst):
+        for k in (1, 2, 3):
+            for core in (c, o):
+                rows = pl.ds(pl.multiple_of(core * 128, 128), 128)
+                owners.append(net.copy(src.at[rows], dst.at[mine], net.plane(k, core)))
+        rows = pl.ds(pl.multiple_of(o * 128, 128), 128)
+        owners.append(net.copy(src.at[rows], dst.at[mine], sibling))
+        rows = pl.ds(pl.multiple_of(c * 128, 128), 128)
+        returned.append(net.local(src.at[rows], dst.at[mine]))
+
+    def to_chips(src, dst):
+        for k in (1, 2, 3):
+            owners.append(net.copy(src, dst.at[p], net.plane(k, c)))
+        returned.append(net.local(src, dst.at[p]))
+
+    fo_at = net.reserve(4)
+
+    def vector_copy(k):
+        return net.describe(r.vout.at[p], r.vout.at[p], net.plane(k, c), fo_at + k, fo_at)
+
+    def mlp_sums():
+        mlp_m.end(r.gm_sum)
+        to_owners(r.gm_sum, r.fm)
+
+    grads = Gather(net, r.do_all.at[mine], r.do_all)
+    grads.start()
+
+    def back_out(slot):
+        b, half = lax.div(slot, 2), lax.rem(slot, 2)
+        dm = dot(r.do_all[slot], r.wo[...], NT)
+        for n in range(2):
+            r.dconv[b * 2 + n, pl.ds(pl.multiple_of(half * 256, 256), 256), :] = dm[:, n * 128 : (n + 1) * 128]
+
+    back_out(mine)
+    grads.sibling(0)
+    back_out(net.slot(0, o))
+    out = Reduce(net, r, lambda k, core: dot(r.hid[net.slot(k, core)], wmd()))
+    for k in (3, 1, 2, 0):
+        out.other(k)
+    mlp_m.relay()
+    grads.forward()
+    out.far()
+    out.near()
+    out.own()
+    grads.middle()
+    for k in (1, 2):
+        back_out(net.slot(k, c))
+    for k in (1, 2):
+        grads.sibling(k)
+        back_out(net.slot(k, o))
+    grads.last()
+    back_out(net.slot(3, c))
+    grads.sibling(3)
+    back_out(net.slot(3, o))
+
+    def first_pass(i):
+        b, tile = lax.div(i, 8), lax.rem(i, 8)
+        rows = tile_rows(tile)
+        live = r.off[b, rows, :] != 0.0
+        for n in range(2):
+            s = b * 2 + n
+            gelu, slope = gelu_parts(r.gp[s, rows, :])
+            dm = r.dconv[s, rows, :]
+            states = r.states[s, pl.ds(pl.multiple_of(tile * TILE + 8, 8), TILE), :]
+            lanes = slice(n * 128, (n + 1) * 128)
+            r.dgi[b * 2 + lax.div(tile, 4), tile_rows(lax.rem(tile, 4)), lanes] = (dm * states * slope).astype(BF)
+            r.drv[s, rows, :] = dm * gelu
+            a = jnp.exp(-DECAY_SCALE * r.sr[s, rows, :] * r.chan[n, 7:8, :])
+            r.dec[s, rows, :] = jnp.where(live, a, 0.0)
+
+    loop(32, first_pass)
+    ends = scan_slabs(r.dec, r.drv, True)
+    ends = exchange_ends(r, net, ends, 1)
+    out.relay()
+    go_in, go_line_in = r.go_q, r.go_l
+    mixed = r.mixed[...].reshape(-1, 256)
+    for half in range(2):
+        lanes = slice(half * 512, half * 512 + 512)
+        r.go[:, lanes] = dot(mixed, r.do_all[:, :, lanes].reshape(-1, 512), TN).astype(BF)
+    grads.release()
+    fetched = net.local(r.normed_far, r.do_all)
+    go_rows = [pl.ds(pl.multiple_of(c * 64 + near * 48, 16), 48) for near in net.near]
+
+    def go_start(lanes):
+        return [net.copy(r.go.at[go_rows[k], lanes], go_in.at[p, :, lanes], net.plane(k, c)) for k in (1, 2, 3)]
+
+    go_out = go_start(pl.ds(0, 1024))
+    mlp_sums()
+    entering_states(r, net, ends, 1, True)
+    mlp_d.relay()
+    r.vec[...] = jnp.zeros((2, 8, 8, 128), F32)
+    dri = r.normed
+
+    def second_pass(s):
+        b, n = lax.div(s, 2), lax.rem(s, 2)
+        chan = r.chan[n]
+        enter = r.inc[pl.ds(s, 1), :]
+        lanes_r = pl.ds(pl.multiple_of(n * 256, 128), 128)
+        lanes_i = pl.ds(pl.multiple_of(n * 256 + 128, 128), 128)
+
+        def tile(i, sums):
+            rows = tile_rows(i)
+            live = r.off[b, rows, :] != 0.0
+            ds = r.drv[s, rows, :] + r.dec[s, rows, :] * enter
+            window = r.states[s, pl.ds(pl.multiple_of(i * TILE, 8), TILE + 8), :]
+            before = window[7 : TILE + 7, :]
+            sr, si = r.sr[s, rows, :], r.si[s, rows, :]
+            cv = r.conv[s, rows, :].astype(F32)
+            a, m2 = decay_parts(sr, chan[7:8, :])
+            inv = lax.rsqrt(m2)
+            m = jnp.where(live, m2 * inv, 1.0)
+            dsi = ds * si
+            d_log = jnp.where(live, a * (ds * before - dsi * cv * a * inv), 0.0)
+            lam_term = d_log * sr
+            d_r = (-DECAY_SCALE) * chan[7:8, :] * lam_term * (1.0 - sr)
+            dm_i = dsi * m
+            d_i = dm_i * cv * (1.0 - si)
+            d_r, d_i = d_r.astype(BF), d_i.astype(BF)
+            at = tile_rows(lax.rem(i, 4))
+            dri[b * 2 + lax.div(i, 4), at, lanes_r] = d_r
+            dri[b * 2 + lax.div(i, 4), at, lanes_i] = d_i
+            r.dconv[s, rows, :] = dm_i
+            return (
+                sums[0] + column_sum(d_r.astype(F32)),
+                sums[1] + column_sum(d_i.astype(F32)),
+                sums[2] + column_sum(lam_term),
+            )
+
+        zero = jnp.zeros((8, 128), F32)
+        sums = lax.fori_loop(0, 512 // TILE, tile, (zero, zero, zero))
+        for j in range(3):
+            r.vec[n, 5 + j] = r.vec[n, 5 + j] + sums[j]
+
+    loop(8, second_pass)
+
+    def gate_back(i):
+        s, half = lax.div(i, 2), lax.rem(i, 2)
+        b, n = lax.div(s, 2), lax.rem(s, 2)
+        rows = pl.ds(pl.multiple_of(half * 256, 256), 256)
+        lanes = pl.ds(pl.multiple_of(n * 256, 256), 256)
+        r.dconv[s, rows, :] = r.dconv[s, rows, :] + dot(dri[b * 2 + half, :, lanes], r.wri[n], NT)
+
+    loop(16, gate_back)
+    edge_back = net.reserve(1)
+
+    def edge_back_copy():
+        return net.describe(
+            r.dconv.at[:, pl.ds(0, 8)], r.dconv.at[:, pl.ds(512, 8)], net.line(net.down(1), c), edge_back, edge_back
+        )
+
+    @pl.when(z > 0)
+    def _():
+        edge_back_copy().start()
+
+    @pl.when(z == 3)
+    def _():
+        r.dconv[:, 512:520, :] = jnp.zeros((8, 8, 128), F32)
+
+    for n in range(2):
+        total_ri = None
+        for b in range(4):
+            for half in range(2):
+                term = dot(
+                    r.conv[b * 2 + n, half * 256 : (half + 1) * 256, :],
+                    dri[b * 2 + half, :, n * 256 : (n + 1) * 256],
+                    TN,
+                )
+                total_ri = term if total_ri is None else total_ri + term
+        r.go[n * 128 : (n + 1) * 128, 1024:1280] = total_ri.astype(BF)
+    go_out += go_start(pl.ds(1024, 256))
+
+    @pl.when(z < 3)
+    def _():
+        edge_back_copy().wait_recv()
+
+
+    def conv_back(s):
+        b, n = lax.div(s, 2), lax.rem(s, 2)
+        chan = r.chan[n]
+        lanes = pl.ds(pl.multiple_of(256 + n * 128, 128), 128)
+
+        def tile(i, sums):
+            offset = r.off[b, pl.ds(pl.multiple_of(i * TILE, 8), TILE + 8), :]
+            window = r.dconv[s, pl.ds(pl.multiple_of(i * TILE, 8), TILE + 8), :]
+            inner = r.inner[s, pl.ds(pl.multiple_of(i * TILE, 8), TILE + 8), :]
+            value = chan[0:1, :] * window[:TILE, :]
+            added = [sums[0] + column_sum(window[:TILE, :] * inner[8:, :])]
+            for k in (1, 2, 3):
+                held = jnp.where(offset >= k, window, 0.0)
+                value = value + chan[k : k + 1, :] * held[k : TILE + k, :]
+                added.append(sums[k] + column_sum(held[:TILE, :] * inner[8 - k : TILE + 8 - k, :]))
+            added.append(sums[4] + column_sum(window[:TILE, :]))
+            r.dgi[b * 2 + lax.div(i, 4), tile_rows(lax.rem(i, 4)), lanes] = value.astype(BF)
+            return tuple(added)
+
+        sums = lax.fori_loop(0, 512 // TILE, tile, tuple(jnp.zeros((8, 128), F32) for _ in range(5)))
+        for j in range(5):
+            r.vec[n, j] = r.vec[n, j] + sums[j]
+
+    loop(8, conv_back)
+    out.finish()
+    for h in range(2):
+
+        def out_rows(i, h=h):
+            rows = pl.ds(pl.multiple_of(h * 128 + i * 32, 32), 32)
+            value = (r.residual[rows, :] + out.total(h, i, 32)).astype(BF)
+            for j in range(4):
+                r.dgu[j, rows, 512:768] = value[:, j * 256 : (j + 1) * 256]
+
+        loop(4, out_rows)
+    for j in range(4):
+        returned.append(net.local(r.dgu.at[j, :, pl.ds(512, 256)], r.block_out.at[:, pl.ds(j * 256, 256)]))
+    for partner in (sibling, net.plane(1, c), net.plane(2, c)):
+        pl.semaphore_signal(r.free, inc=1, device_id=partner, device_id_type=pl.DeviceIdType.MESH)
+    for n in range(2):
+        sums = [jnp.sum(r.vec[n, j], axis=0, keepdims=True) for j in range(8)]
+        sums[7] = sums[7] * (DECAY_SCALE * r.chan[n, 8:9, :])
+        r.vsum[z, :, n * 128 : (n + 1) * 128] = jnp.concatenate(sums, axis=0)
+    vec = [net.copy(r.vsum.at[z], r.vsum.at[z], net.line(net.up(k), c)) for k in (1, 2, 3)]
+    fetched.wait()
+    flat = r.dgi[:, :, 0:512].reshape(-1, 512)
+    for i in range(4):
+        value = dot(r.do_all[:, :, i * 256 : (i + 1) * 256].reshape(-1, 256), flat, TN)
+        for j in range(2):
+            n0, n1 = value[:, j * 256 : j * 256 + 128], value[:, j * 256 + 128 : j * 256 + 256]
+            r.ga[i][:, j * 128 : (j + 1) * 128] = lax.select(c == 0, n0, n1).astype(BF)
+            shared = lax.select(c == 0, n1, n0)
+            r.gb2[i][:, j * 128 : (j + 1) * 128] = lax.select(c == 0, shared[0:128], shared[128:256]).astype(BF)
+
+    def ga_in(k):
+        return r.g_all.at[7, :, pl.ds((k - 1) * 256, 256)]
+
+    def gb_in(k):
+        return r.g_all.at[3 + k, pl.ds(128, 128), pl.ds(0, 256)]
+
+    sum_a = LineSum(net, lambda t: r.hid.at[t, :, 0:256], ga_in)
+    sum_b = LineSum(net, lambda t: r.hid.at[4 + t, 0:128, 0:256], gb_in)
+    sum_a.start()
+    sum_b.start()
+    first_back = Reduce(
+        net,
+        r,
+        lambda k, core: dot(masked(r.dgi[net.slot(k, core), :, 0:512], counted_two), r.w2[...], NT),
+    )
+    pl.semaphore_wait(r.free, 3)
+    for k in (3, 1, 2, 0):
+        first_back.other(k)
+    first_back.far()
+    first_back.near()
+    go_in[p] = r.go[go_rows[0], :]
+    for made in go_out:
+        made.wait_recv()
+    go_line = LineSum(net, lambda t: go_in.at[t], lambda k: go_line_in.at[k - 1])
+    go_line.start()
+    first_back.relay()
+    mlp_d.end(r.gd_sum)
+    to_chips(r.gd_sum, r.fd)
+    first_back.own()
+    sum_a.relay()
+    sum_b.relay()
+    go_line.relay()
+    first_back.finish()
+    sums = jnp.zeros((8, r.x.shape[1]), F32)
+    for h in range(2):
+
+        def input_rows(i, sums, h=h):
+            rows = pl.ds(pl.multiple_of(h * 128 + i * 32, 32), 32)
+            v = r.x[rows, :].astype(F32)
+            dn = first_back.total(h, i, 32)
+            s = lax.rsqrt(jnp.mean(v * v, axis=-1, keepdims=True) + NORM_EPS)
+            u = dn * r.gain[0:1, :]
+            r.d_res[rows, :] = r.d_res[rows, :] + (
+                s * u - v * (s * s * s * jnp.mean(u * v, axis=-1, keepdims=True))
+            )
+            return sums + jnp.sum((dn * v * s).reshape(4, 8, -1), axis=0)
+
+        sums = lax.fori_loop(0, 4, input_rows, sums)
+    returned.append(net.local(r.d_res, r.d_in))
+    gains = jnp.concatenate(
+        [
+            jnp.sum(sums, axis=0, keepdims=True),
+            jnp.sum(r.gain2_sum[...], axis=0, keepdims=True),
+            jnp.zeros((6, sums.shape[1]), F32),
+        ],
+        axis=0,
+    )
+    for i in range(8):
+        r.gsum[i] = gains[:, i * 128 : (i + 1) * 128]
+    r.gline[q] = r.gsum[q]
+    gain_line = [
+        net.copy(r.gsum.at[net.up(k) * 2 + core], r.gline.at[q], net.line(net.up(k), core))
+        for k in (1, 2, 3)
+        for core in (c, o)
+    ]
+    gain_line.append(net.copy(r.gsum.at[z * 2 + o], r.gline.at[q], sibling))
+    for made in row_sums:
+        made.wait_recv()
+    r.rows_sum[...] = r.rs_all[0] + r.rs_all[1] + r.rs_all[2] + r.rs_all[3]
+    for k in (1, 2, 3):
+        for core in (c, o):
+            owners.append(net.copy(r.rows_sum.at[pl.ds(net.near[k] * 2, 2)], r.fr.at[mine], net.plane(k, core)))
+    owners.append(net.copy(r.rows_sum.at[pl.ds(p * 2, 2)], r.fr.at[mine], sibling))
+    returned.append(net.local(r.rows_sum.at[pl.ds(p * 2, 2)], r.fr.at[mine]))
+    for made in vec:
+        made.wait_recv()
+    r.vout[p] = r.vsum[0] + r.vsum[1] + r.vsum[2] + r.vsum[3]
+
+    @pl.when(z == p)
+    def _():
+        for k in (1, 2, 3):
+            vector_copy(k).start()
+
+    sum_a.end(r.ga_sum)
+    to_owners(r.ga_sum, r.fa)
+    sum_b.end(r.gb2_sum)
+    to_chips(r.gb2_sum, r.fb)
+    go_line.end(r.go_sum)
+    to_chips(r.go_sum, r.fo)
+    for made in gain_line:
+        made.wait_recv()
+    sums = r.gline[0]
+    for i in range(1, 8):
+        sums = sums + r.gline[i]
+    r.gplane[p] = sums
+    gain_plane = [net.copy(r.gplane.at[p], r.gplane.at[p], net.plane(k, c)) for k in (1, 2, 3)]
+
+    @pl.when(z != p)
+    def _():
+        vector_copy(1).wait_recv()
+
+    @pl.when(z == p)
+    def _():
+        for k in (1, 2, 3):
+            vector_copy(k).wait_send()
+
+    for made in owners + gain_plane:
+        made.wait_recv()
+    r.gain_out[...] = r.gplane[0] + r.gplane[1] + r.gplane[2] + r.gplane[3]
+    r.vec_out[...] = r.vout[z]
+    for made in returned:
+        made.wait()
+    @pl.when(z < 3)
+    def _():
+        edge_copy().wait_send()
+
+    @pl.when(z > 0)
+    def _():
+        edge_back_copy().wait_send()
+
+    feed.drain()
+    feed_down.drain()
+    for made in (mlp_m, mlp_d, go_line, sum_a, sum_b):
+        made.drain()
+    net.drain()
+
+
+def assemble(r):
+    c = lax.rem(lax.axis_index("seq"), 2)
+    for chip in range(4):
+        for j, out in enumerate((r.o_gate, r.o_in)):
+            lanes = slice(j * 128, (j + 1) * 128)
+            at = chip * 384
+            out[:, at : at + 128] = r.fa[chip * 2, :, lanes].astype(F32)
+            out[:, at + 128 : at + 256] = r.fb[chip, :, lanes].astype(F32)
+            out[:, at + 256 : at + 384] = r.fa[chip * 2 + 1, :, lanes].astype(F32)
+    cols = r.fm.shape[2] // 2
+    piece = cols // 4
+    for j, out in enumerate((r.o_mgate, r.o_mup)):
+        for part in range(4):
+            for core in range(2):
+                at = (part * 2 + core) * cols
+                lanes = slice(j * cols + part * piece, j * cols + (part + 1) * piece)
+                out[:, at : at + cols] = jnp.concatenate(
+                    [r.fm[chip * 2 + core, :, lanes].astype(F32) for chip in range(4)], axis=1
+                )
+    for chip in range(4):
+        r.o_mdown[chip * piece : (chip + 1) * piece, :] = r.fd[chip].astype(F32)
+    for chip in range(4):
+        rows = slice(chip * 48, (chip + 1) * 48)
+        r.o_out[rows, :] = r.fo[chip, :, 0:1024].astype(F32)
+        r.o_r[rows, :] = r.fo[chip, :, 1024:1152].astype(F32)
+        r.o_i[rows, :] = r.fo[chip, :, 1152:1280].astype(F32)
+    vec = r.vec_in[...]
+    vec = lax.select(c == 0, vec[:, 0:192], vec[:, 64:256])
+    r.o_cw[...] = vec[0:4]
+    for j, out in enumerate((r.o_cb, r.o_rb, r.o_ib, r.o_lam)):
+        out[...] = vec[4 + j : 5 + j]
+    r.o_ngain[...] = r.gains[0:1, :]
+    r.o_mgain[...] = r.gains[1:2, :]
+    counts = [jnp.broadcast_to(r.lens[0:1, row : row + 1].astype(F32), (1, 128)) for row in range(5)]
+    for chip in range(4):
+        for half, (slot, n) in enumerate(((chip * 2, 0), (chip * 2, 1), (chip * 2 + 1, 1))):
+            at = chip * 384 + half * 128
+            for row in range(5):
+                r.o_mean[row, :, at : at + 128] = r.fr[slot, n, row : row + 1, :] / counts[row]
 
 
 def shifted(value, axis, by):
@@ -306,6 +1641,179 @@
     )
 
 
+def pack(conv_w, conv_b, b_rgate, b_igate, lam, norm_gain, mlp_gain):
+    row = lax.broadcasted_iota(jnp.int32, (16, 256), 0)
+    lane = lax.broadcasted_iota(jnp.int32, (16, 256), 1)
+    small = jnp.pad(conv_w, ((0, 12), (0, 64)))
+    for at, value in ((4, conv_b), (5, b_rgate), (6, b_igate), (7, lam)):
+        spread = jnp.broadcast_to(jnp.pad(value, (0, 64)), (16, 256))
+        small = jnp.where(row == at, spread, small)
+    for first, value in ((0, norm_gain), (128, mlp_gain)):
+        spread = jnp.broadcast_to(jnp.pad(value, (first, 128 - first)), (16, 256))
+        small = jnp.where((row == 10) & (lane // 128 == first // 128), spread, small)
+    return small
+
+
+def planes(
+    inputs,
+    out_grad,
+    row_lengths,
+    norm_gain,
+    w_gate,
+    w_in,
+    conv_w,
+    conv_b,
+    w_rgate,
+    b_rgate,
+    w_igate,
+    b_igate,
+    lam,
+    w_out,
+    mlp_gain,
+    w_mlp_gate,
+    w_mlp_up,
+    w_mlp_down,
+):
+    small = pack(conv_w, conv_b, b_rgate, b_igate, lam, norm_gain, mlp_gain)
+    vmem = pltpu.VMEM
+    done = kernel_call(
+        layer,
+        dict(
+            x=inputs[0], small=small, lens=row_lengths, g=out_grad[0], wg=w_gate, wi=w_in, wr=w_rgate, wv=w_igate, wout=w_out,
+            wmg=w_mlp_gate, wmu=w_mlp_up, wmd=w_mlp_down,
+        ),
+        dict(
+            block_out=array(256, 1024, dtype=BF),
+            d_in=array(256, 1024),
+            fm=array(8, 128, 768, dtype=BF),
+            fd=array(4, 96, 1024, dtype=BF),
+            fa=array(8, 128, 256, dtype=BF),
+            fb=array(4, 128, 256, dtype=BF),
+            fo=array(4, 48, 1280, dtype=BF),
+            fr=array(8, 2, 8, 128),
+            vec_out=array(8, 256),
+            gain_out=array(8, 128),
+            normed_far=array(8, 256, 1024, dtype=BF),
+        ),
+        dict(
+            x_all=vmem((8, 256, 1024), BF),
+            normed=vmem((8, 256, 1024), BF),
+            g_all=vmem((8, 256, 1024), BF),
+            small_all=vmem((8, 16, 256), BF),
+            lens_out=vmem((8, 128), F32),
+            lens_all=vmem((4, 8, 128), F32),
+            off=vmem((4, 520, 128), F32),
+            starts_all=vmem((4, 8, 128), F32),
+            chan=vmem((2, 16, 128), F32),
+            gain=vmem((8, 1024), F32),
+            wgi3=vmem((4, 256, 768), BF),
+            w2=vmem((1024, 512), BF),
+            gq=vmem((4, 48, 256), BF),
+            g3=vmem((2, 192, 256), BF),
+            wq=vmem((4, 48, 1024), BF),
+            wri=vmem((2, 128, 256), BF),
+            w3=vmem((2, 192, 1024), BF),
+            wo=vmem((256, 1024), BF),
+            wgu_out=vmem((2, 256, 384), BF),
+            wgu_all=vmem((8, 256, 384), BF),
+            wmd_all=vmem((4, 96, 1024), BF),
+            gp=vmem((8, 512, 128), F32),
+            gb=vmem((8, 520, 128), F32),
+            inner=vmem((8, 520, 128), F32),
+            conv=vmem((8, 512, 128), BF),
+            sr=vmem((8, 512, 128), F32),
+            si=vmem((8, 512, 128), F32),
+            dec=vmem((8, 512, 128), F32),
+            drv=vmem((8, 512, 128), F32),
+            states=vmem((8, 520, 128), F32),
+            mixed=vmem((8, 256, 256), BF),
+            tot=vmem((2, 4, 2, 8, 128), F32),
+            inc=vmem((8, 128), F32),
+            rs_all=vmem((4, 8, 8, 128), F32),
+            rows_sum=vmem((8, 8, 128), F32),
+            residual=vmem((256, 1024), F32),
+            d_res=vmem((256, 1024), F32),
+            hid=vmem((8, 256, 384), BF),
+            dgu=vmem((8, 256, 768), BF),
+            gm=vmem((4, 256, 768), BF),
+            gm_sum=vmem((256, 768), BF),
+            gd=vmem((4, 96, 1024), BF),
+            gd_in=vmem((3, 96, 1024), BF),
+            gd_sum=vmem((96, 1024), BF),
+            go=vmem((256, 1280), BF),
+            go_q=vmem((4, 48, 1280), BF),
+            go_l=vmem((3, 48, 1280), BF),
+            go_sum=vmem((48, 1280), BF),
+            ga_sum=vmem((256, 256), BF),
+            gb2_sum=vmem((128, 256), BF),
+            gain2_sum=vmem((8, 1024), F32),
+            vec=vmem((2, 8, 8, 128), F32),
+            vsum=vmem((4, 8, 256), F32),
+            vout=vmem((4, 8, 256), F32),
+            gsum=vmem((8, 8, 128), F32),
+            gline=vmem((8, 8, 128), F32),
+            gplane=vmem((4, 8, 128), F32),
+            free=pltpu.SemaphoreType.REGULAR,
+            **reduce_scratch(256, 1024),
+        ),
+        210,
+        36,
+        (
+            "g", "wg", "wi", "wr", "wv", "wout", "wmg", "wmu", "wmd", "d_in", "block_out", "fm", "fd", "fa", "fb", "fo",
+            "fr", "normed_far",
+        ),
+    )
+    out = kernel_call(
+        assemble,
+        dict(
+            {name: done[name] for name in ("fm", "fd", "fa", "fb", "fo", "fr")},
+            vec_in=done["vec_out"], gains=done["gain_out"], lens=row_lengths,
+        ),
+        dict(
+            o_gate=array(128, 1536),
+            o_in=array(128, 1536),
+            o_mgate=array(128, 3072),
+            o_mup=array(128, 3072),
+            o_mdown=array(384, 1024),
+            o_out=array(192, 1024),
+            o_r=array(192, 128),
+            o_i=array(192, 128),
+            o_cw=array(4, 192),
+            o_cb=array(1, 192),
+            o_rb=array(1, 192),
+            o_ib=array(1, 192),
+            o_lam=array(1, 192),
+            o_ngain=array(1, 128),
+            o_mgain=array(1, 128),
+            o_mean=array(5, 1, 1536),
+        ),
+        {},
+        0,
+        0,
+        (),
+    )
+    return (
+        done["block_out"][None],
+        done["d_in"][None],
+        out["o_ngain"][0],
+        out["o_gate"],
+        out["o_in"],
+        out["o_cw"],
+        out["o_cb"][0],
+        out["o_r"],
+        out["o_rb"][0],
+        out["o_i"],
+        out["o_ib"][0],
+        out["o_lam"][0],
+        out["o_out"],
+        out["o_mgain"][0],
+        out["o_mgate"],
+        out["o_mup"],
+        out["o_mdown"],
+        jnp.transpose(out["o_mean"], (1, 0, 2)),
+    )
+
+
 def solution(mesh):
     in_specs = (
         P("batch", "seq", None),
@@ -347,4 +1855,6 @@
         P("seq", None),
         P("batch", None, None),
     )
-    return jax.shard_map(shards, mesh=mesh, in_specs=in_specs, out_specs=out_specs, check_vma=False)
+    in_planes = mesh.shape["batch"] == 4 and mesh.shape["seq"] == 8
+    body = planes if in_planes else shards
+    return jax.shard_map(body, mesh=mesh, in_specs=in_specs, out_specs=out_specs, check_vma=False)

time: 1630 us -> 248 us (0.15); the launches traced: 1610 us -> 245 us
  waiting for transfers between devices: 728 us -> 0 us
  local copies, waits for them, and re-layouts: 402 us -> 5.74 us
  Pallas kernels: 0 us -> 237 us
  other arithmetic: 175 us -> 1.4 us
  blocking collectives: 169 us -> 0 us
  matrix products: 108 us -> 0 us
  between operations: 17.8 us -> 1.16 us
    reduce_scatter x8 -> x0, waiting for transfers between devices: 595 us -> none  [the longest x1 128 us: shards(): lax.psum_scatter(grad_mgate, 'seq', scatter_dimension=0, tiled=True)]
    pallas_call x0 -> x2, Pallas kernels: none -> 237 us  [kernel_call(): pl.pallas_call(kernel, out_shape=list(outs.values()), in_specs=[away if n...]
    slice x112 -> x0, local copies, waits for them, and re-layouts: 223 us -> none  [the longest x57 131 us: shards(): lax.associative_scan(link, (next_decay, direct), axis=0, reverse=True)]
    psum x2 -> x0, waiting for transfers between devices: 127 us -> none  [the longest x1 90.2 us: shards(): lax.psum(shares[1].astype(jnp.bfloat16), 'batch').astype(jnp.float32)]
    all_gather x9 -> x0, blocking collectives: 123 us -> none  [the longest x4 56.9 us: entering(): everything = jax.tree.map(lambda part: lax.all_gather(part, axis), value)]
    dot_general x25 -> x0, matrix products: 108 us -> none  [the longest x1 9.87 us: shards(): jnp.einsum('td,fd->tf', grad_top, gathered[14], preferred_element_type=jn...]
    pad x56 -> x6, local copies, waits for them, and re-layouts: 111 us -> 3.96 us  [the longest x4 2.64 us: pack(): spread = jnp.broadcast_to(jnp.pad(value, (0, 64)), (16, 256))]
    add x46 -> x0, other arithmetic: 60.9 us -> none  [the longest x16 22 us: shards(): lax.associative_scan(link, (next_decay, direct), axis=0, reverse=True)]
  transfers between devices with their start and end apart: 19 -> 0, of which waited for: 10 -> 0; matrix products, arithmetic and copies ran while one was open for 23% -> 0% of each run, Pallas kernels for 0% -> 0%
where the time goes in v2:
time: 248 us; the launch traced here: 245 us
  Pallas kernels  237 us (96%)
  local copies, waits for them, and re-layouts  5.74 us (2%)
    pallas_call x2, Pallas kernels, kernel_call(): pl.pallas_call(kernel, out_shape=list(outs.values()), in_specs=[away if n...  237 us

profile of v2, /device:TPU:19, one launch (start us, length us, event | category | flops | bytes accessed | tf_op | source)
XLA Modules:
  0.0 245.1 jit_solution(13286752386105144881)
XLA Ops:
  0.7 0.7 pad.26
  1.3 0.7 pad.30
  2.0 0.7 pad.29
  2.6 0.7 pad.28
  3.3 0.7 pad.27
  4.0 0.7 pad.25
  4.7 1.4 fusion.1.refs_1_
  6.0 230.9 %layer.1 = (bf16[256,1024]{1,0:T(8,128)(2,1)}, f32[256,1024]{1,0:T(8,128)}, bf16[8,128,768]{2,1,0:T(8,128)(2,1)}, bf16[4,96,1024]{2,1,0:T(8,128)(2,1)}, bf16[8,1...) custom-call(bf16[256,1024]{1,0:T(8,128)(2,1)} %bitcast.12, ...), custom_call_target="tpu_custom_call" | custom-call | tf_op jit(solution)/shard_map/layer/pallas_call | solution.py:378
  237.0 0.0 copy-start.1
  237.0 0.0 copy-start
  237.0 5.9 %assemble.1 = (f32[128,1536]{1,0:T(8,128)}, f32[128,1536]{1,0:T(8,128)}, f32[128,3072]{1,0:T(8,128)}, f32[128,3072]{1,0:T(8,128)}, f32[384,1024]{1,0:T(8,128)}, ...) custom-call(bf16[8,128,768]{2,1,0:T(8,128)(2,1)} %get-tuple-element., ...), custom_call_target="tpu_custom_call" | custom-call | tf_op jit(solution)/shard_map/assemble/pallas_call | solution.py:378
  242.9 0.0 copy-done.1
  242.9 0.8 copy.38
  243.7 0.0 copy-done
  243.7 1.0 copy.39
  (5 shorter events, 0.0 us)
Async XLA Ops:
  237.0 5.9 %copy-start.1 = (bf16[256,1024]{1,0:T(8,128)(2,1)S(1)}, bf16[256,1024]{1,0:T(8,128)(2,1)}, u32[]{:S(2)}) copy-start(bf16[256,1024]{1,0:T(8,128)(2,1)} %get-tuple-element.44) | copy-start | bytes 1572868
  237.0 6.7 %copy-start = (f32[256,1024]{1,0:T(8,128)S(1)}, f32[256,1024]{1,0:T(8,128)}, u32[]{:S(2)}) copy-start(f32[256,1024]{1,0:T(8,128)} %get-tuple-element.45) | copy-start | bytes 3145732

commit v3 on v2

--- a/solution.py
+++ b/solution.py
@@ -84,8 +84,8 @@
             device_id_type=pl.DeviceIdType.MESH,
         )
 
-    def copy(self, src, dst, device, sent=None):
-        at = self.reserve(1)
+    def copy(self, src, dst, device, sent=None, at=None):
+        at = self.reserve(1) if at is None else at
         made = self.describe(src, dst, device, at, at)
         made.start()
         (self.pending if sent is None else sent).append(made)
@@ -105,9 +105,10 @@
 
 
 class Gather:
-    def __init__(self, net, own, everything):
+    def __init__(self, net, own, everything, at=None):
         self.net, self.own, self.all = net, own, everything
         self.sent = []
+        self.at = net.reserve(10) if at is None else at
         self.half = everything.shape[1] // 2
 
     def part(self, slot, h):
@@ -118,25 +119,25 @@
         mine = net.slot(0, net.c)
         low, high = self.own.at[pl.ds(0, self.half)], self.own.at[pl.ds(self.half, self.half)]
         self.s = []
-        self.x0 = net.copy(low, self.part(mine, 0), net.plane(1, net.c), self.sent)
-        self.y1 = net.copy(high, self.part(mine, 1), net.plane(2, net.c), self.sent)
-        self.x1 = net.copy(high, self.part(mine, 1), net.plane(1, net.c), self.sent)
-        self.y0 = net.copy(low, self.part(mine, 0), net.plane(2, net.c), self.sent)
-        self.s.append(net.copy(self.own, self.all.at[mine], net.plane(0, net.o), self.sent))
+        self.x0 = net.copy(low, self.part(mine, 0), net.plane(1, net.c), self.sent, self.at + 0)
+        self.y1 = net.copy(high, self.part(mine, 1), net.plane(2, net.c), self.sent, self.at + 1)
+        self.x1 = net.copy(high, self.part(mine, 1), net.plane(1, net.c), self.sent, self.at + 2)
+        self.y0 = net.copy(low, self.part(mine, 0), net.plane(2, net.c), self.sent, self.at + 3)
+        self.s.append(net.copy(self.own, self.all.at[mine], net.plane(0, net.o), self.sent, self.at + 4))
 
     def forward(self):
         net = self.net
         self.x0.wait_recv()
         mine = self.part(net.slot(1, net.c), 0)
-        self.d0 = net.copy(mine, mine, net.plane(2, net.c), self.sent)
+        self.d0 = net.copy(mine, mine, net.plane(2, net.c), self.sent, self.at + 5)
         self.y1.wait_recv()
         mine = self.part(net.slot(2, net.c), 1)
-        self.d1 = net.copy(mine, mine, net.plane(1, net.c), self.sent)
+        self.d1 = net.copy(mine, mine, net.plane(1, net.c), self.sent, self.at + 6)
 
     def across(self, k):
         net = self.net
         mine = self.all.at[net.slot(k, net.c)]
-        self.s.append(net.copy(mine, mine, net.plane(0, net.o), self.sent))
+        self.s.append(net.copy(mine, mine, net.plane(0, net.o), self.sent, self.at + 6 + k))
 
     def middle(self):
         self.x1.wait_recv()
@@ -284,8 +285,9 @@
 
 
 class Reduce:
-    def __init__(self, net, r, value):
+    def __init__(self, net, r, value, at=None):
         self.net, self.value = net, value
+        self.at = net.reserve(10) if at is None else at
         self.keep, self.out, self.into = r.rs_keep, r.rs_out, r.rs_in
         self.xs, self.ys, self.xr, self.yr = r.rs_xs, r.rs_ys, r.rs_xr, r.rs_yr
         self.half = self.keep.shape[1]
@@ -295,7 +297,7 @@
     def other(self, k):
         net = self.net
         self.out[k] = self.value(k, net.o).astype(BF)
-        self.cross[k] = net.copy(self.out.at[k], self.into.at[k], net.plane(0, net.o), self.sent)
+        self.cross[k] = net.copy(self.out.at[k], self.into.at[k], net.plane(0, net.o), self.sent, self.at + k)
 
     def mine(self, k):
         self.cross[k].wait_recv()
@@ -304,7 +306,8 @@
 
     def send(self, src, dst, j, k):
         net = self.net
-        return net.copy(src.at[j], dst.at[j], net.plane(k, net.c), self.sent)
+        at = self.at + 4 + j + (0 if src is self.xs else 3)
+        return net.copy(src.at[j], dst.at[j], net.plane(k, net.c), self.sent, at)
 
     def far(self):
         low, high = self.mine(3)
@@ -366,8 +369,11 @@
     away = pl.BlockSpec(memory_space=pl.ANY)
     shapes = list(scratch.values())
     if copies:
-        names += ["send", "recv", "local"]
-        shapes += [pltpu.SemaphoreType.DMA((n,)) for n in (copies, copies, local)]
+        names += ["send", "recv"]
+        shapes += [pltpu.SemaphoreType.DMA((copies,))] * 2
+    if local:
+        names.append("local")
+        shapes.append(pltpu.SemaphoreType.DMA((local,)))
 
     def kernel(*refs):
         body(types.SimpleNamespace(**dict(zip(names, refs))))
@@ -507,6 +513,13 @@
         net.local(r.g, r.g_all.at[mine]),
     ]
     r.lens_out[0:1, 0:5] = r.lens[...].astype(F32)
+    r.small_rows[...] = jnp.zeros((16, 256), F32)
+    r.small_rows[0:4, 0:192] = r.cw[...].astype(F32)
+    for at, ref in ((4, r.cb), (5, r.br), (6, r.bi), (7, r.lam)):
+        r.small_rows[at : at + 1, 0:192] = ref[...].astype(F32).reshape(1, 192)
+    for at, ref in ((0, r.ngain), (128, r.mgain)):
+        r.small_rows[10:11, at : at + 128] = ref[...].astype(F32).reshape(1, 128)
+    r.small[...] = r.small_rows[...].astype(BF)
     net.greet()
     r.small_all[q] = r.small[...]
     r.lens_all[p] = r.lens_out[...]
@@ -633,7 +646,6 @@
     heads_gate, heads_gate_over = heads_start(wg_rows)
     hand_over(heads_in, wi_rows, heads_in_over)
     tokens.middle()
-    gates_out = exchange(gates_in, r.gq, r.g3)
     for k in (1, 2):
         normalise(net.slot(k, c))
     for k in (1, 2):
@@ -658,6 +670,7 @@
     for k in (0, 1, 2):
         project_inner(net.slot(k, c))
         project_inner(net.slot(k, o))
+    gates_out = exchange(gates_in, r.gq, r.g3)
     tokens.last()
     normalise(net.slot(3, c))
     project_inner(net.slot(3, c))
@@ -850,7 +863,7 @@
         loop(4, residual_rows)
 
     n2_all = r.normed
-    acts = Gather(net, n2_all.at[mine], n2_all)
+    acts = Gather(net, n2_all.at[mine], n2_all, tokens.at)
     acts.start()
 
     def gate_up(which):
@@ -860,7 +873,7 @@
         slot = net.slot(k, core)
         return dot(r.dgu[slot, :, 0:cols], gate_up(0), NT) + dot(r.dgu[slot, :, cols:], gate_up(1), NT)
 
-    back = Reduce(net, r, d_normed2)
+    back = Reduce(net, r, d_normed2, total.at)
 
     def part(k, core):
         slot = net.slot(k, core)
@@ -969,7 +982,7 @@
         mlp_m.end(r.gm_sum)
         to_owners(r.gm_sum, r.fm)
 
-    grads = Gather(net, r.do_all.at[mine], r.do_all)
+    grads = Gather(net, r.do_all.at[mine], r.do_all, cots.at)
     grads.start()
 
     def back_out(slot):
@@ -981,7 +994,7 @@
     back_out(mine)
     grads.sibling(0)
     back_out(net.slot(0, o))
-    out = Reduce(net, r, lambda k, core: dot(r.hid[net.slot(k, core)], wmd()))
+    out = Reduce(net, r, lambda k, core: dot(r.hid[net.slot(k, core)], wmd()), total.at)
     for k in (3, 1, 2, 0):
         out.other(k)
     mlp_m.relay()
@@ -1188,6 +1201,7 @@
         net,
         r,
         lambda k, core: dot(masked(r.dgi[net.slot(k, core), :, 0:512], counted_two), r.w2[...], NT),
+        total.at,
     )
     pl.semaphore_wait(r.free, 3)
     for k in (3, 1, 2, 0):
@@ -1303,30 +1317,18 @@
 
 def assemble(r):
     c = lax.rem(lax.axis_index("seq"), 2)
-    for chip in range(4):
-        for j, out in enumerate((r.o_gate, r.o_in)):
-            lanes = slice(j * 128, (j + 1) * 128)
-            at = chip * 384
-            out[:, at : at + 128] = r.fa[chip * 2, :, lanes].astype(F32)
-            out[:, at + 128 : at + 256] = r.fb[chip, :, lanes].astype(F32)
-            out[:, at + 256 : at + 384] = r.fa[chip * 2 + 1, :, lanes].astype(F32)
-    cols = r.fm.shape[2] // 2
-    piece = cols // 4
-    for j, out in enumerate((r.o_mgate, r.o_mup)):
-        for part in range(4):
-            for core in range(2):
-                at = (part * 2 + core) * cols
-                lanes = slice(j * cols + part * piece, j * cols + (part + 1) * piece)
-                out[:, at : at + cols] = jnp.concatenate(
-                    [r.fm[chip * 2 + core, :, lanes].astype(F32) for chip in range(4)], axis=1
-                )
-    for chip in range(4):
-        r.o_mdown[chip * piece : (chip + 1) * piece, :] = r.fd[chip].astype(F32)
-    for chip in range(4):
-        rows = slice(chip * 48, (chip + 1) * 48)
-        r.o_out[rows, :] = r.fo[chip, :, 0:1024].astype(F32)
-        r.o_r[rows, :] = r.fo[chip, :, 1024:1152].astype(F32)
-        r.o_i[rows, :] = r.fo[chip, :, 1152:1280].astype(F32)
+    count = 0
+    stores = []
+
+    def start(src, dst):
+        nonlocal count
+        made = pltpu.make_async_copy(src, dst, r.local.at[count])
+        count += 1
+        made.start()
+        return made
+
+    loads = [start(*pair) for pair in ((r.fm, r.vm), (r.fa, r.va), (r.fb, r.vb), (r.fd, r.vd), (r.fo, r.vo))]
+    passed = [start(r.d_in, r.v_din), start(r.block_out, r.v_block)]
     vec = r.vec_in[...]
     vec = lax.select(c == 0, vec[:, 0:192], vec[:, 64:256])
     r.o_cw[...] = vec[0:4]
@@ -1340,6 +1342,45 @@
             at = chip * 384 + half * 128
             for row in range(5):
                 r.o_mean[row, :, at : at + 128] = r.fr[slot, n, row : row + 1, :] / counts[row]
+    cols = r.fm.shape[2] // 2
+    piece = cols // 4
+    loads[0].wait()
+    for j, (stage, out) in enumerate(((r.s_mgate, r.o_mgate), (r.s_mup, r.o_mup))):
+        for part in range(4):
+            for core in range(2):
+                at = (part * 2 + core) * cols
+                lanes = slice(j * cols + part * piece, j * cols + (part + 1) * piece)
+                stage[:, at : at + cols] = jnp.concatenate(
+                    [r.vm[chip * 2 + core, :, lanes].astype(F32) for chip in range(4)], axis=1
+                )
+            here = pl.ds(part * 2 * cols, 2 * cols)
+            stores.append(start(stage.at[:, here], out.at[:, here]))
+    for made, src, dst in zip(passed, (r.v_din, r.v_block), (r.o_din, r.o_block)):
+        made.wait()
+        stores.append(start(src, dst))
+    loads[1].wait()
+    loads[2].wait()
+    for j, (stage, out) in enumerate(((r.s_gate, r.o_gate), (r.s_in, r.o_in))):
+        lanes = slice(j * 128, (j + 1) * 128)
+        for chip in range(4):
+            at = chip * 384
+            stage[:, at : at + 128] = r.va[chip * 2, :, lanes].astype(F32)
+            stage[:, at + 128 : at + 256] = r.vb[chip, :, lanes].astype(F32)
+            stage[:, at + 256 : at + 384] = r.va[chip * 2 + 1, :, lanes].astype(F32)
+        stores.append(start(stage, out))
+    loads[3].wait()
+    for chip in range(4):
+        r.s_down[chip * piece : (chip + 1) * piece, :] = r.vd[chip].astype(F32)
+    stores.append(start(r.s_down, r.o_mdown))
+    loads[4].wait()
+    for chip in range(4):
+        rows = slice(chip * 48, (chip + 1) * 48)
+        r.s_out[rows, :] = r.vo[chip, :, 0:1024].astype(F32)
+        r.o_r[rows, :] = r.vo[chip, :, 1024:1152].astype(F32)
+        r.o_i[rows, :] = r.vo[chip, :, 1152:1280].astype(F32)
+    stores.append(start(r.s_out, r.o_out))
+    for made in stores:
+        made.wait()
 
 
 def shifted(value, axis, by):
@@ -1641,19 +1682,6 @@
     )
 
 
-def pack(conv_w, conv_b, b_rgate, b_igate, lam, norm_gain, mlp_gain):
-    row = lax.broadcasted_iota(jnp.int32, (16, 256), 0)
-    lane = lax.broadcasted_iota(jnp.int32, (16, 256), 1)
-    small = jnp.pad(conv_w, ((0, 12), (0, 64)))
-    for at, value in ((4, conv_b), (5, b_rgate), (6, b_igate), (7, lam)):
-        spread = jnp.broadcast_to(jnp.pad(value, (0, 64)), (16, 256))
-        small = jnp.where(row == at, spread, small)
-    for first, value in ((0, norm_gain), (128, mlp_gain)):
-        spread = jnp.broadcast_to(jnp.pad(value, (first, 128 - first)), (16, 256))
-        small = jnp.where((row == 10) & (lane // 128 == first // 128), spread, small)
-    return small
-
-
 def planes(
     inputs,
     out_grad,
@@ -1674,12 +1702,12 @@
     w_mlp_up,
     w_mlp_down,
 ):
-    small = pack(conv_w, conv_b, b_rgate, b_igate, lam, norm_gain, mlp_gain)
     vmem = pltpu.VMEM
     done = kernel_call(
         layer,
         dict(
-            x=inputs[0], small=small, lens=row_lengths, g=out_grad[0], wg=w_gate, wi=w_in, wr=w_rgate, wv=w_igate, wout=w_out,
+            x=inputs[0], cw=conv_w, cb=conv_b, br=b_rgate, bi=b_igate, lam=lam, ngain=norm_gain, mgain=mlp_gain,
+            lens=row_lengths, g=out_grad[0], wg=w_gate, wi=w_in, wr=w_rgate, wv=w_igate, wout=w_out,
             wmg=w_mlp_gate, wmu=w_mlp_up, wmd=w_mlp_down,
         ),
         dict(
@@ -1699,6 +1727,8 @@
             x_all=vmem((8, 256, 1024), BF),
             normed=vmem((8, 256, 1024), BF),
             g_all=vmem((8, 256, 1024), BF),
+            small_rows=vmem((16, 256), F32),
+            small=vmem((16, 256), BF),
             small_all=vmem((8, 16, 256), BF),
             lens_out=vmem((8, 128), F32),
             lens_all=vmem((4, 8, 128), F32),
@@ -1756,7 +1786,7 @@
             free=pltpu.SemaphoreType.REGULAR,
             **reduce_scratch(256, 1024),
         ),
-        210,
+        160,
         36,
         (
             "g", "wg", "wi", "wr", "wv", "wout", "wmg", "wmu", "wmd", "d_in", "block_out", "fm", "fd", "fa", "fb", "fo",
@@ -1766,10 +1796,12 @@
     out = kernel_call(
         assemble,
         dict(
-            {name: done[name] for name in ("fm", "fd", "fa", "fb", "fo", "fr")},
+            {name: done[name] for name in ("d_in", "block_out", "fm", "fd", "fa", "fb", "fo", "fr")},
             vec_in=done["vec_out"], gains=done["gain_out"], lens=row_lengths,
         ),
         dict(
+            o_din=array(256, 1024),
+            o_block=array(256, 1024, dtype=BF),
             o_gate=array(128, 1536),
             o_in=array(128, 1536),
             o_mgate=array(128, 3072),
@@ -1787,14 +1819,31 @@
             o_mgain=array(1, 128),
             o_mean=array(5, 1, 1536),
         ),
-        {},
+        dict(
+            v_din=vmem((256, 1024), F32),
+            v_block=vmem((256, 1024), BF),
+            vm=vmem((8, 128, 768), BF),
+            va=vmem((8, 128, 256), BF),
+            vb=vmem((4, 128, 256), BF),
+            vd=vmem((4, 96, 1024), BF),
+            vo=vmem((4, 48, 1280), BF),
+            s_mgate=vmem((128, 3072), F32),
+            s_mup=vmem((128, 3072), F32),
+            s_gate=vmem((128, 1536), F32),
+            s_in=vmem((128, 1536), F32),
+            s_down=vmem((384, 1024), F32),
+            s_out=vmem((192, 1024), F32),
+        ),
         0,
-        0,
-        (),
+        21,
+        (
+            "d_in", "block_out", "fm", "fd", "fa", "fb", "fo", "o_din", "o_block", "o_gate", "o_in", "o_mgate", "o_mup",
+            "o_mdown", "o_out",
+        ),
     )
     return (
-        done["block_out"][None],
-        done["d_in"][None],
+        out["o_block"][None],
+        out["o_din"][None],
         out["o_ngain"][0],
         out["o_gate"],
         out["o_in"],

time: 248 us -> 240 us (0.968)
  local copies, waits for them, and re-layouts: 5.74 us -> 0 us
    pad x6 -> x0, local copies, waits for them, and re-layouts: 3.96 us -> none  [the longest x4 2.64 us: pack(): spread = jnp.broadcast_to(jnp.pad(value, (0, 64)), (16, 256))]
where the time goes in v3:
time: 240 us; the launch traced here: 237 us
  Pallas kernels  236 us (98%)
    pallas_call x2, Pallas kernels, kernel_call(): pl.pallas_call(kernel, out_shape=list(outs.values()), in_specs=[away if n...  236 us

profile of v3, /device:TPU:19, one launch (start us, length us, event | category | flops | bytes accessed | tf_op | source)
XLA Modules:
  0.0 237.2 jit_solution(18275038524641257151)
XLA Ops:
  0.7 229.4 %layer.1 = (bf16[256,1024]{1,0:T(8,128)(2,1)}, f32[256,1024]{1,0:T(8,128)}, bf16[8,128,768]{2,1,0:T(8,128)(2,1)}, bf16[4,96,1024]{2,1,0:T(8,128)(2,1)}, bf16[8,1...) custom-call(bf16[256,1024]{1,0:T(8,128)(2,1)} %bitcast.11, ...), custom_call_target="tpu_custom_call" | custom-call | tf_op jit(solution)/shard_map/layer/pallas_call | solution.py:384
  230.1 6.7 %assemble.1 = (f32[256,1024]{1,0:T(8,128)}, bf16[256,1024]{1,0:T(8,128)(2,1)}, f32[128,1536]{1,0:T(8,128)}, f32[128,1536]{1,0:T(8,128)}, f32[128,3072]{1,0:T(8,1...) custom-call(f32[256,1024]{1,0:T(8,128)} %get-tuple-element.46.refs_0, ...), custom_call_target="tpu_custom_call" | custom-call | tf_op jit(solution)/shard_map/assemble/pallas_call | solution.py:384

commit v4 on v3

--- a/solution.py
+++ b/solution.py
@@ -157,6 +157,56 @@
         for made in self.sent:
             made.wait_send()
         self.sent = []
+
+
+class Owners:
+    def __init__(self, net, own, everything, extra=None):
+        self.net, self.own, self.all, self.extra = net, own, everything, extra
+        self.half = everything.shape[1] // 2
+        self.s = [None] * 4
+
+    def part(self, k, h):
+        return self.all.at[self.net.near[k], pl.ds(h * self.half, self.half)]
+
+    def across(self, k, block):
+        if self.extra is not None:
+            net = self.net
+            rows = pl.ds(pl.multiple_of(net.o * self.half, 16), self.half)
+            self.s[k] = net.copy(block.at[rows], self.extra.at[net.near[k]], net.plane(0, net.o))
+
+    def start(self):
+        net = self.net
+        low, high = self.own.at[pl.ds(0, self.half)], self.own.at[pl.ds(self.half, self.half)]
+        self.x0 = net.copy(low, self.part(0, 0), net.plane(1, net.c))
+        self.y1 = net.copy(high, self.part(0, 1), net.plane(2, net.c))
+        self.x1 = net.copy(high, self.part(0, 1), net.plane(1, net.c))
+        self.y0 = net.copy(low, self.part(0, 0), net.plane(2, net.c))
+        self.across(0, self.own)
+        self.kept = net.local(self.own, self.all.at[net.p])
+
+    def forward(self):
+        net = self.net
+        self.x0.wait_recv()
+        self.d0 = net.copy(self.part(1, 0), self.part(1, 0), net.plane(2, net.c))
+        self.y1.wait_recv()
+        self.d1 = net.copy(self.part(2, 1), self.part(2, 1), net.plane(1, net.c))
+
+    def middle(self):
+        self.x1.wait_recv()
+        self.across(1, self.all.at[self.net.near[1]])
+        self.y0.wait_recv()
+        self.across(2, self.all.at[self.net.near[2]])
+
+    def last(self):
+        self.d0.wait_recv()
+        self.d1.wait_recv()
+        self.across(3, self.all.at[self.net.near[3]])
+
+    def end(self):
+        if self.extra is not None:
+            for made in self.s:
+                made.wait_recv()
+        self.kept.wait()
 
 
 class LineGather:
@@ -530,23 +580,27 @@
     tokens.start()
     theirs = pl.ds(pl.multiple_of(c * width + o * 128, 128), 256)
 
-    def along(ref, sent=None):
-        return [net.copy(ref, ref, net.line(net.up(k), c), sent) for k in (1, 2, 3)]
+    def along(place):
+        made = LineGather(net, [(place(z), c)], lambda j: place(z), lambda j, at: place(at))
+        for k in (2, 1, 3):
+            made.start(k, (0,))
+        return made
 
     handed = []
 
     def heads_start(rows):
         here = r.wgi3.at[z, rows, theirs]
-        return along(r.wgi3.at[z, rows, own_lanes], handed), [net.copy(here, here, sibling, handed)]
+        made = along(lambda at: r.wgi3.at[at, rows, own_lanes])
+        return made, [net.copy(here, here, sibling, handed)]
 
     for made in placed:
         made.wait()
     heads_in, heads_in_over = heads_start(wi_rows)
-    gates_in = along(r.gq.at[z])
-
-    def hand_over(copies, rows, over):
+    gates_in = along(lambda at: r.gq.at[at])
+
+    def hand_over(arrivals, rows, over):
+        arrivals.end()
         for k in (1, 2, 3):
-            copies[k - 1].wait_recv()
             here = r.wgi3.at[net.down(k), rows, theirs]
             over.append(net.copy(here, here, sibling, handed))
 
@@ -560,8 +614,7 @@
                 r.w2[to, lanes] = r.wgi3[at, rows, cols_in]
 
     def exchange(arrivals, src, dst):
-        for made in arrivals:
-            made.wait_recv()
+        arrivals.end()
         dst[c, quarter, :] = src[p]
         return [net.copy(src.at[net.near[k]], dst.at[c, quarter], net.plane(k, c)) for k in (1, 2, 3)]
 
@@ -642,10 +695,19 @@
     tokens.sibling(0)
     normalise(net.slot(0, o))
     tokens.forward()
-    out_in = along(r.wq.at[z])
-    heads_gate, heads_gate_over = heads_start(wg_rows)
+    heads_in.relay()
+    gates_in.relay()
+    out_in = along(lambda at: r.wq.at[at])
+    feed = LineGather(
+        net,
+        [(r.wgu_out.at[core], core) for core in (c, o)],
+        lambda j: r.wgu_all.at[q],
+        lambda j, at: r.wgu_all.at[at * 2 + (c, o)[j]],
+    )
+    feed_down = LineGather(net, [(r.wmd.at[down], c)], lambda j: r.wmd_all.at[z], lambda j, at: r.wmd_all.at[at])
     hand_over(heads_in, wi_rows, heads_in_over)
     tokens.middle()
+    gates_out = exchange(gates_in, r.gq, r.g3)
     for k in (1, 2):
         normalise(net.slot(k, c))
     for k in (1, 2):
@@ -667,10 +729,10 @@
         for n in range(2):
             r.gp[b * 2 + n, pl.ds(at, 256), :] = gate[:, n * 128 : (n + 1) * 128]
 
+    out_in.relay()
     for k in (0, 1, 2):
         project_inner(net.slot(k, c))
         project_inner(net.slot(k, o))
-    gates_out = exchange(gates_in, r.gq, r.g3)
     tokens.last()
     normalise(net.slot(3, c))
     project_inner(net.slot(3, c))
@@ -694,12 +756,15 @@
 
     gates_over = share(gates_out, r.g3)
     stored = net.local(r.normed, r.normed_far)
+    cots = Gather(net, r.g_all.at[mine], r.g_all)
+    cots.start()
     tokens.release()
     gates_over.wait_recv()
     for i in range(4):
         at = c * 128 + i * 64
         value = r.g3[lax.div(at, 192), pl.ds(pl.multiple_of(lax.rem(at, 192), 64), 64), :]
         r.wri[i // 2, (i % 2) * 64 : (i % 2 + 1) * 64, :] = value
+    heads_gate, heads_gate_over = heads_start(wg_rows)
 
     @pl.when(z > 0)
     def _():
@@ -720,17 +785,8 @@
             r.conv[s, rows, :] = total.astype(BF)
 
     loop(32, conv_tile)
-    feed = LineGather(
-        net,
-        [(r.wgu_out.at[core], core) for core in (c, o)],
-        lambda j: r.wgu_all.at[q],
-        lambda j, at: r.wgu_all.at[at * 2 + (c, o)[j]],
-    )
-    feed_down = LineGather(net, [(r.wmd.at[down], c)], lambda j: r.wmd_all.at[z], lambda j, at: r.wmd_all.at[at])
     feed.start(2, (0,))
     out_rows_in = exchange(out_in, r.wq, r.w3)
-    cots = Gather(net, r.g_all.at[mine], r.g_all)
-    cots.start()
 
     def gate_products(i):
         s, half = lax.div(i, 2), lax.rem(i, 2)
@@ -741,6 +797,7 @@
         r.si[s, rows, :] = pre[:, 128:]
 
     loop(16, gate_products)
+    heads_gate.relay()
 
     def terms(b):
         starts_b = r.starts_all[b]
@@ -761,7 +818,7 @@
                 r.si[s, rows, :] = si
                 a, m2 = decay_parts(sr, chan[7:8, :])
                 r.dec[s, rows, :] = jnp.where(restart, 0.0, a)
-                m = jnp.where(restart, 1.0, jnp.sqrt(m2))
+                m = jnp.where(restart, 1.0, m2 * lax.rsqrt(m2))
                 r.drv[s, rows, :] = m * si * r.conv[s, rows, :].astype(F32)
                 for row in range(5):
                     inside = jnp.where(begun == starts_b[row : row + 1, :], a, 0.0)
@@ -774,6 +831,7 @@
             r.rs_all[z, b * 2 + n] = jnp.concatenate(rows + [jnp.zeros((3, 128), F32)], axis=0)
 
     loop(4, terms)
+    cots.forward()
     ends = scan_slabs(r.dec, r.drv, False)
     ends = exchange_ends(r, net, ends, 0)
     feed.start(2, (1,))
@@ -782,10 +840,11 @@
     r.wgu_all[q] = r.wgu_out[c]
     feed_over = net.copy(r.wgu_out.at[o], r.wgu_all.at[q], sibling)
     hand_over(heads_gate, wg_rows, heads_gate_over)
-    cots.forward()
     arrange(heads_gate_over, slice(0, 128), slice(0, 256))
     for made in handed:
         made.wait_send()
+    heads_in.drain()
+    heads_gate.drain()
     for k in (2, 1, 3):
         feed_down.start(k, (0,))
     for slot in range(8):
@@ -910,13 +969,13 @@
     acts.sibling(2)
     part(2, o)
     back.other(2)
+    back.near()
     acts.last()
     acts.sibling(3)
     part(3, o)
     back.other(3)
     part(3, c)
     back.far()
-    back.near()
     back.relay()
     back.own()
     acts.release()
@@ -936,7 +995,6 @@
         for i in range(4):
             r.gd[i, :, lanes] = value[i * piece : (i + 1) * piece, :]
     mlp_d = LineSum(net, lambda t: r.gd.at[t], lambda k: r.gd_in.at[k - 1])
-    mlp_d.start()
     back.finish()
     sums = jnp.zeros((8, r.x.shape[1]), F32)
     for h in range(2):
@@ -958,16 +1016,6 @@
 
     owners, returned = [], []
 
-    def to_owners(src, dst):
-        for k in (1, 2, 3):
-            for core in (c, o):
-                rows = pl.ds(pl.multiple_of(core * 128, 128), 128)
-                owners.append(net.copy(src.at[rows], dst.at[mine], net.plane(k, core)))
-        rows = pl.ds(pl.multiple_of(o * 128, 128), 128)
-        owners.append(net.copy(src.at[rows], dst.at[mine], sibling))
-        rows = pl.ds(pl.multiple_of(c * 128, 128), 128)
-        returned.append(net.local(src.at[rows], dst.at[mine]))
-
     def to_chips(src, dst):
         for k in (1, 2, 3):
             owners.append(net.copy(src, dst.at[p], net.plane(k, c)))
@@ -978,9 +1026,14 @@
     def vector_copy(k):
         return net.describe(r.vout.at[p], r.vout.at[p], net.plane(k, c), fo_at + k, fo_at)
 
+    owners_m = Owners(net, r.gm_sum, r.fm, r.fm_x)
+    owners_d = Owners(net, r.gd_sum, r.fd)
+    owners_a = Owners(net, r.ga_sum, r.fa, r.fa_x)
+    owners_b = Owners(net, r.gb2_sum, r.fb)
+
     def mlp_sums():
         mlp_m.end(r.gm_sum)
-        to_owners(r.gm_sum, r.fm)
+        owners_m.start()
 
     grads = Gather(net, r.do_all.at[mine], r.do_all, cots.at)
     grads.start()
@@ -997,12 +1050,12 @@
     out = Reduce(net, r, lambda k, core: dot(r.hid[net.slot(k, core)], wmd()), total.at)
     for k in (3, 1, 2, 0):
         out.other(k)
-    mlp_m.relay()
     grads.forward()
     out.far()
     out.near()
     out.own()
     grads.middle()
+    mlp_m.relay()
     for k in (1, 2):
         back_out(net.slot(k, c))
     for k in (1, 2):
@@ -1047,7 +1100,6 @@
     go_out = go_start(pl.ds(0, 1024))
     mlp_sums()
     entering_states(r, net, ends, 1, True)
-    mlp_d.relay()
     r.vec[...] = jnp.zeros((2, 8, 8, 128), F32)
     dri = r.normed
 
@@ -1112,6 +1164,8 @@
     def _():
         edge_back_copy().start()
 
+    mlp_d.start()
+
     @pl.when(z == 3)
     def _():
         r.dconv[:, 512:520, :] = jnp.zeros((8, 8, 128), F32)
@@ -1197,6 +1251,8 @@
     sum_b = LineSum(net, lambda t: r.hid.at[4 + t, 0:128, 0:256], gb_in)
     sum_a.start()
     sum_b.start()
+    mlp_d.relay()
+    owners_m.forward()
     first_back = Reduce(
         net,
         r,
@@ -1215,8 +1271,9 @@
     go_line.start()
     first_back.relay()
     mlp_d.end(r.gd_sum)
-    to_chips(r.gd_sum, r.fd)
+    owners_d.start()
     first_back.own()
+    owners_m.middle()
     sum_a.relay()
     sum_b.relay()
     go_line.relay()
@@ -1272,11 +1329,15 @@
             vector_copy(k).start()
 
     sum_a.end(r.ga_sum)
-    to_owners(r.ga_sum, r.fa)
+    owners_a.start()
     sum_b.end(r.gb2_sum)
-    to_chips(r.gb2_sum, r.fb)
+    owners_b.start()
     go_line.end(r.go_sum)
     to_chips(r.go_sum, r.fo)
+    owners_d.forward()
+    owners_m.last()
+    owners_a.forward()
+    owners_b.forward()
     for made in gain_line:
         made.wait_recv()
     sums = r.gline[0]
@@ -1294,6 +1355,13 @@
         for k in (1, 2, 3):
             vector_copy(k).wait_send()
 
+    owners_d.middle()
+    owners_a.middle()
+    owners_b.middle()
+    for each in (owners_d, owners_a, owners_b):
+        each.last()
+    for each in (owners_m, owners_d, owners_a, owners_b):
+        each.end()
     for made in owners + gain_plane:
         made.wait_recv()
     r.gain_out[...] = r.gplane[0] + r.gplane[1] + r.gplane[2] + r.gplane[3]
@@ -1308,6 +1376,8 @@
     def _():
         edge_back_copy().wait_send()
 
+    gates_in.drain()
+    out_in.drain()
     feed.drain()
     feed_down.drain()
     for made in (mlp_m, mlp_d, go_line, sum_a, sum_b):
@@ -1327,7 +1397,18 @@
         made.start()
         return made
 
-    loads = [start(*pair) for pair in ((r.fm, r.vm), (r.fa, r.va), (r.fb, r.vb), (r.fd, r.vd), (r.fo, r.vo))]
+    mine = pl.ds(pl.multiple_of(c * 128, 128), 128)
+    loads = [
+        [start(r.fm.at[:, mine], r.vm.at[c]), start(r.fm_x, r.vm.at[1 - c])],
+        [start(r.fa.at[:, mine], r.va.at[c]), start(r.fa_x, r.va.at[1 - c]), start(r.fb, r.vb)],
+        [start(r.fd, r.vd)],
+        [start(r.fo, r.vo)],
+    ]
+
+    def loaded(which):
+        for made in loads[which]:
+            made.wait()
+
     passed = [start(r.d_in, r.v_din), start(r.block_out, r.v_block)]
     vec = r.vec_in[...]
     vec = lax.select(c == 0, vec[:, 0:192], vec[:, 64:256])
@@ -1344,35 +1425,34 @@
                 r.o_mean[row, :, at : at + 128] = r.fr[slot, n, row : row + 1, :] / counts[row]
     cols = r.fm.shape[2] // 2
     piece = cols // 4
-    loads[0].wait()
+    loaded(0)
     for j, (stage, out) in enumerate(((r.s_mgate, r.o_mgate), (r.s_mup, r.o_mup))):
         for part in range(4):
             for core in range(2):
                 at = (part * 2 + core) * cols
                 lanes = slice(j * cols + part * piece, j * cols + (part + 1) * piece)
                 stage[:, at : at + cols] = jnp.concatenate(
-                    [r.vm[chip * 2 + core, :, lanes].astype(F32) for chip in range(4)], axis=1
+                    [r.vm[core, chip, :, lanes].astype(F32) for chip in range(4)], axis=1
                 )
             here = pl.ds(part * 2 * cols, 2 * cols)
             stores.append(start(stage.at[:, here], out.at[:, here]))
     for made, src, dst in zip(passed, (r.v_din, r.v_block), (r.o_din, r.o_block)):
         made.wait()
         stores.append(start(src, dst))
-    loads[1].wait()
-    loads[2].wait()
+    loaded(1)
     for j, (stage, out) in enumerate(((r.s_gate, r.o_gate), (r.s_in, r.o_in))):
         lanes = slice(j * 128, (j + 1) * 128)
         for chip in range(4):
             at = chip * 384
-            stage[:, at : at + 128] = r.va[chip * 2, :, lanes].astype(F32)
+            stage[:, at : at + 128] = r.va[0, chip, :, lanes].astype(F32)
             stage[:, at + 128 : at + 256] = r.vb[chip, :, lanes].astype(F32)
-            stage[:, at + 256 : at + 384] = r.va[chip * 2 + 1, :, lanes].astype(F32)
+            stage[:, at + 256 : at + 384] = r.va[1, chip, :, lanes].astype(F32)
         stores.append(start(stage, out))
-    loads[3].wait()
+    loaded(2)
     for chip in range(4):
         r.s_down[chip * piece : (chip + 1) * piece, :] = r.vd[chip].astype(F32)
     stores.append(start(r.s_down, r.o_mdown))
-    loads[4].wait()
+    loaded(3)
     for chip in range(4):
         rows = slice(chip * 48, (chip + 1) * 48)
         r.s_out[rows, :] = r.vo[chip, :, 0:1024].astype(F32)
@@ -1713,9 +1793,11 @@
         dict(
             block_out=array(256, 1024, dtype=BF),
             d_in=array(256, 1024),
-            fm=array(8, 128, 768, dtype=BF),
+            fm=array(4, 256, 768, dtype=BF),
+            fm_x=array(4, 128, 768, dtype=BF),
             fd=array(4, 96, 1024, dtype=BF),
-            fa=array(8, 128, 256, dtype=BF),
+            fa=array(4, 256, 256, dtype=BF),
+            fa_x=array(4, 128, 256, dtype=BF),
             fb=array(4, 128, 256, dtype=BF),
             fo=array(4, 48, 1280, dtype=BF),
             fr=array(8, 2, 8, 128),
@@ -1786,17 +1868,17 @@
             free=pltpu.SemaphoreType.REGULAR,
             **reduce_scratch(256, 1024),
         ),
-        160,
+        176,
         36,
         (
-            "g", "wg", "wi", "wr", "wv", "wout", "wmg", "wmu", "wmd", "d_in", "block_out", "fm", "fd", "fa", "fb", "fo",
+            "g", "wg", "wi", "wr", "wv", "wout", "wmg", "wmu", "wmd", "d_in", "block_out", "fm", "fm_x", "fd", "fa", "fa_x", "fb", "fo",
             "fr", "normed_far",
         ),
     )
     out = kernel_call(
         assemble,
         dict(
-            {name: done[name] for name in ("d_in", "block_out", "fm", "fd", "fa", "fb", "fo", "fr")},
+            {name: done[name] for name in ("d_in", "block_out", "fm", "fm_x", "fd", "fa", "fa_x", "fb", "fo", "fr")},
             vec_in=done["vec_out"], gains=done["gain_out"], lens=row_lengths,
         ),
         dict(
@@ -1822,8 +1904,8 @@
         dict(
             v_din=vmem((256, 1024), F32),
             v_block=vmem((256, 1024), BF),
-            vm=vmem((8, 128, 768), BF),
-            va=vmem((8, 128, 256), BF),
+            vm=vmem((2, 4, 128, 768), BF),
+            va=vmem((2, 4, 128, 256), BF),
             vb=vmem((4, 128, 256), BF),
             vd=vmem((4, 96, 1024), BF),
             vo=vmem((4, 48, 1280), BF),
@@ -1835,9 +1917,9 @@
             s_out=vmem((192, 1024), F32),
         ),
         0,
-        21,
+        23,
         (
-            "d_in", "block_out", "fm", "fd", "fa", "fb", "fo", "o_din", "o_block", "o_gate", "o_in", "o_mgate", "o_mup",
+            "d_in", "block_out", "fm", "fm_x", "fd", "fa", "fa_x", "fb", "fo", "o_din", "o_block", "o_gate", "o_in", "o_mgate", "o_mup",
             "o_mdown", "o_out",
         ),
     )

time: 240 us -> 225 us (0.938)
  Pallas kernels: 236 us -> 220 us
    pallas_call x2, Pallas kernels: 236 us -> 220 us  [kernel_call(): pl.pallas_call(kernel, out_shape=list(outs.values()), in_specs=[away if n...]
where the time goes in v4:
time: 225 us; the launch traced here: 221 us
  Pallas kernels  220 us (98%)
    pallas_call x2, Pallas kernels, kernel_call(): pl.pallas_call(kernel, out_shape=list(outs.values()), in_specs=[away if n...  220 us

profile of v4, /device:TPU:19, one launch (start us, length us, event | category | flops | bytes accessed | tf_op | source)
XLA Modules:
  0.0 221.3 jit_solution(12534430610145402153)
XLA Ops:
  0.7 213.5 %layer.1 = (bf16[256,1024]{1,0:T(8,128)(2,1)}, f32[256,1024]{1,0:T(8,128)}, bf16[4,256,768]{2,1,0:T(8,128)(2,1)}, bf16[4,128,768]{2,1,0:T(8,128)(2,1)}, bf16[4,9...) custom-call(bf16[256,1024]{1,0:T(8,128)(2,1)} %bitcast.11, ...), custom_call_target="tpu_custom_call" | custom-call | tf_op jit(solution)/shard_map/layer/pallas_call | solution.py:434
  214.1 6.7 %assemble.1 = (f32[256,1024]{1,0:T(8,128)}, bf16[256,1024]{1,0:T(8,128)(2,1)}, f32[128,1536]{1,0:T(8,128)}, f32[128,1536]{1,0:T(8,128)}, f32[128,3072]{1,0:T(8,1...) custom-call(f32[256,1024]{1,0:T(8,128)} %get-tuple-element.48.refs_0, ...), custom_call_target="tpu_custom_call" | custom-call | tf_op jit(solution)/shard_map/assemble/pallas_call | solution.py:434

commit v5 on v4

--- a/solution.py
+++ b/solution.py
@@ -108,41 +108,48 @@
     def __init__(self, net, own, everything, at=None):
         self.net, self.own, self.all = net, own, everything
         self.sent = []
-        self.at = net.reserve(10) if at is None else at
+        self.at = net.reserve(14) if at is None else at
         self.half = everything.shape[1] // 2
-
-    def part(self, slot, h):
+        self.x0, self.y1, self.x1, self.y0 = [], [], [], []
+
+    def half_of(self, slot, h):
         return self.all.at[slot, pl.ds(h * self.half, self.half)]
 
-    def start(self):
+    def send(self, src, dst, device, at):
+        return self.net.copy(src, dst, device, self.sent, self.at + at)
+
+    def start(self, part):
         net = self.net
         mine = net.slot(0, net.c)
-        low, high = self.own.at[pl.ds(0, self.half)], self.own.at[pl.ds(self.half, self.half)]
-        self.s = []
-        self.x0 = net.copy(low, self.part(mine, 0), net.plane(1, net.c), self.sent, self.at + 0)
-        self.y1 = net.copy(high, self.part(mine, 1), net.plane(2, net.c), self.sent, self.at + 1)
-        self.x1 = net.copy(high, self.part(mine, 1), net.plane(1, net.c), self.sent, self.at + 2)
-        self.y0 = net.copy(low, self.part(mine, 0), net.plane(2, net.c), self.sent, self.at + 3)
-        self.s.append(net.copy(self.own, self.all.at[mine], net.plane(0, net.o), self.sent, self.at + 4))
+        size = self.half // 2
+        low, high = pl.ds(part * size, size), pl.ds(self.half + part * size, size)
+        for made, rows, k, at in ((self.x0, low, 1, 0), (self.y1, high, 2, 2), (self.x1, high, 1, 4), (self.y0, low, 2, 6)):
+            made.append(self.send(self.own.at[rows], self.all.at[mine, rows], net.plane(k, net.c), at + part))
+        if part == 1:
+            self.s = [self.send(self.own, self.all.at[mine], net.plane(0, net.o), 8)]
 
     def forward(self):
         net = self.net
-        self.x0.wait_recv()
-        mine = self.part(net.slot(1, net.c), 0)
-        self.d0 = net.copy(mine, mine, net.plane(2, net.c), self.sent, self.at + 5)
-        self.y1.wait_recv()
-        mine = self.part(net.slot(2, net.c), 1)
-        self.d1 = net.copy(mine, mine, net.plane(1, net.c), self.sent, self.at + 6)
+        for made in self.x0:
+            made.wait_recv()
+        block = self.half_of(net.slot(1, net.c), 0)
+        self.d0 = self.send(block, block, net.plane(2, net.c), 9)
+        for made in self.y1:
+            made.wait_recv()
+        block = self.half_of(net.slot(2, net.c), 1)
+        self.d1 = self.send(block, block, net.plane(1, net.c), 10)
 
     def across(self, k):
         net = self.net
-        mine = self.all.at[net.slot(k, net.c)]
-        self.s.append(net.copy(mine, mine, net.plane(0, net.o), self.sent, self.at + 6 + k))
+        block = self.all.at[net.slot(k, net.c)]
+        self.s.append(self.send(block, block, net.plane(0, net.o), 10 + k))
 
     def middle(self):
-        self.x1.wait_recv()
+        for made in self.x1:
+            made.wait_recv()
         self.across(1)
-        self.y0.wait_recv()
+        for made in self.y0:
+            made.wait_recv()
         self.across(2)
 
     def last(self):
@@ -160,8 +167,9 @@
 
 
 class Owners:
-    def __init__(self, net, own, everything, extra=None):
+    def __init__(self, net, own, everything, extra=None, at=None):
         self.net, self.own, self.all, self.extra = net, own, everything, extra
+        self.at = net.reserve(6 if extra is None else 10) if at is None else at
         self.half = everything.shape[1] // 2
         self.s = [None] * 4
 
@@ -172,24 +180,24 @@
         if self.extra is not None:
             net = self.net
             rows = pl.ds(pl.multiple_of(net.o * self.half, 16), self.half)
-            self.s[k] = net.copy(block.at[rows], self.extra.at[net.near[k]], net.plane(0, net.o))
+            self.s[k] = net.copy(block.at[rows], self.extra.at[net.near[k]], net.plane(0, net.o), None, self.at + 6 + k)
 
     def start(self):
         net = self.net
         low, high = self.own.at[pl.ds(0, self.half)], self.own.at[pl.ds(self.half, self.half)]
-        self.x0 = net.copy(low, self.part(0, 0), net.plane(1, net.c))
-        self.y1 = net.copy(high, self.part(0, 1), net.plane(2, net.c))
-        self.x1 = net.copy(high, self.part(0, 1), net.plane(1, net.c))
-        self.y0 = net.copy(low, self.part(0, 0), net.plane(2, net.c))
+        self.x0 = net.copy(low, self.part(0, 0), net.plane(1, net.c), None, self.at + 0)
+        self.y1 = net.copy(high, self.part(0, 1), net.plane(2, net.c), None, self.at + 1)
+        self.x1 = net.copy(high, self.part(0, 1), net.plane(1, net.c), None, self.at + 2)
+        self.y0 = net.copy(low, self.part(0, 0), net.plane(2, net.c), None, self.at + 3)
         self.across(0, self.own)
         self.kept = net.local(self.own, self.all.at[net.p])
 
     def forward(self):
         net = self.net
         self.x0.wait_recv()
-        self.d0 = net.copy(self.part(1, 0), self.part(1, 0), net.plane(2, net.c))
+        self.d0 = net.copy(self.part(1, 0), self.part(1, 0), net.plane(2, net.c), None, self.at + 4)
         self.y1.wait_recv()
-        self.d1 = net.copy(self.part(2, 1), self.part(2, 1), net.plane(1, net.c))
+        self.d1 = net.copy(self.part(2, 1), self.part(2, 1), net.plane(1, net.c), None, self.at + 5)
 
     def middle(self):
         self.x1.wait_recv()
@@ -337,7 +345,7 @@
 class Reduce:
     def __init__(self, net, r, value, at=None):
         self.net, self.value = net, value
-        self.at = net.reserve(10) if at is None else at
+        self.at = net.reserve(12) if at is None else at
         self.keep, self.out, self.into = r.rs_keep, r.rs_out, r.rs_in
         self.xs, self.ys, self.xr, self.yr = r.rs_xs, r.rs_ys, r.rs_xr, r.rs_yr
         self.half = self.keep.shape[1]
@@ -354,10 +362,14 @@
         value = self.value(k, self.net.c) + self.into[k].astype(F32)
         return value[: self.half], value[self.half :]
 
-    def send(self, src, dst, j, k):
+    def send(self, src, dst, j, k, part=None):
         net = self.net
-        at = self.at + 4 + j + (0 if src is self.xs else 3)
-        return net.copy(src.at[j], dst.at[j], net.plane(k, net.c), self.sent, at)
+        at = self.at + 4 + j + (part or 0) + (0 if src is self.xs else 4)
+        src, dst = src.at[j], dst.at[j]
+        if part is not None:
+            rows = pl.ds(part * self.half // 2, self.half // 2)
+            src, dst = src.at[rows], dst.at[rows]
+        return net.copy(src, dst, net.plane(k, net.c), self.sent, at)
 
     def far(self):
         low, high = self.mine(3)
@@ -377,22 +389,32 @@
         self.keep[3] = low
 
     def relay(self):
-        self.x0.wait_recv()
-        self.ys[2] = (self.keep[3] + self.xr[0].astype(F32)).astype(BF)
-        self.y2 = self.send(self.ys, self.yr, 2, 2)
-        self.y0.wait_recv()
-        self.xs[2] = (self.keep[2] + self.yr[0].astype(F32)).astype(BF)
-        self.x2 = self.send(self.xs, self.xr, 2, 1)
+        size = self.half // 2
+        self.x2, self.y2 = [], []
+        for part in (0, 1):
+            rows = slice(part * size, (part + 1) * size)
+            if part == 0:
+                self.x0.wait_recv()
+            self.ys[2, rows, :] = (self.keep[3, rows, :] + self.xr[0, rows, :].astype(F32)).astype(BF)
+            self.y2.append(self.send(self.ys, self.yr, 2, 2, part))
+            if part == 0:
+                self.y0.wait_recv()
+            self.xs[2, rows, :] = (self.keep[2, rows, :] + self.yr[0, rows, :].astype(F32)).astype(BF)
+            self.x2.append(self.send(self.xs, self.xr, 2, 1, part))
 
     def own(self):
         self.keep[0], self.keep[1] = self.mine(0)
 
-    def finish(self):
-        for made in (self.x1, self.y1, self.x2, self.y2):
-            made.wait_recv()
-        for made in self.sent:
-            made.wait_send()
-        self.sent = []
+    def finish(self, part):
+        if part == 0:
+            self.x1.wait_recv()
+            self.y1.wait_recv()
+        self.x2[part].wait_recv()
+        self.y2[part].wait_recv()
+        if part == 1:
+            for made in self.sent:
+                made.wait_send()
+            self.sent = []
 
     def total(self, h, i, step):
         rows = pl.ds(pl.multiple_of(i * step, step), step)
@@ -577,7 +599,8 @@
     small.append(net.copy(r.small, r.small_all.at[q], sibling))
     lens = [net.copy(r.lens_out, r.lens_all.at[p], net.plane(k, c)) for k in (1, 2, 3)]
     tokens = Gather(net, r.x, r.x_all)
-    tokens.start()
+    tokens.start(0)
+    tokens.start(1)
     theirs = pl.ds(pl.multiple_of(c * width + o * 128, 128), 256)
 
     def along(place):
@@ -705,14 +728,14 @@
         lambda j, at: r.wgu_all.at[at * 2 + (c, o)[j]],
     )
     feed_down = LineGather(net, [(r.wmd.at[down], c)], lambda j: r.wmd_all.at[z], lambda j, at: r.wmd_all.at[at])
-    hand_over(heads_in, wi_rows, heads_in_over)
     tokens.middle()
-    gates_out = exchange(gates_in, r.gq, r.g3)
     for k in (1, 2):
         normalise(net.slot(k, c))
+    hand_over(heads_in, wi_rows, heads_in_over)
     for k in (1, 2):
         tokens.sibling(k)
         normalise(net.slot(k, o))
+    gates_out = exchange(gates_in, r.gq, r.g3)
     arrange(heads_in_over, slice(128, 256), slice(256, 512))
 
     def project_inner(slot):
@@ -757,7 +780,8 @@
     gates_over = share(gates_out, r.g3)
     stored = net.local(r.normed, r.normed_far)
     cots = Gather(net, r.g_all.at[mine], r.g_all)
-    cots.start()
+    cots.start(0)
+    cots.start(1)
     tokens.release()
     gates_over.wait_recv()
     for i in range(4):
@@ -785,7 +809,6 @@
             r.conv[s, rows, :] = total.astype(BF)
 
     loop(32, conv_tile)
-    feed.start(2, (0,))
     out_rows_in = exchange(out_in, r.wq, r.w3)
 
     def gate_products(i):
@@ -798,6 +821,7 @@
 
     loop(16, gate_products)
     heads_gate.relay()
+    feed.start(2, (0,))
 
     def terms(b):
         starts_b = r.starts_all[b]
@@ -908,22 +932,23 @@
     def wmd():
         return r.wmd_all[...].reshape(cols, -1)
 
-    total.finish()
     gain2 = r.gain[1:2, :]
-    for h in range(2):
-
-        def residual_rows(i, h=h):
-            rows = pl.ds(pl.multiple_of(h * 128 + i * 32, 32), 32)
-            v = r.x[rows, :].astype(F32) + total.total(h, i, 32)
-            r.residual[rows, :] = v
-            s = lax.rsqrt(jnp.mean(v * v, axis=-1, keepdims=True) + NORM_EPS)
-            r.normed[mine, rows, :] = (v * s * gain2).astype(BF)
-
-        loop(4, residual_rows)
-
     n2_all = r.normed
     acts = Gather(net, n2_all.at[mine], n2_all, tokens.at)
-    acts.start()
+    for part in range(2):
+        total.finish(part)
+        for h in range(2):
+
+            def residual_rows(i, h=h, part=part):
+                i = part * 2 + i
+                rows = pl.ds(pl.multiple_of(h * 128 + i * 32, 32), 32)
+                v = r.x[rows, :].astype(F32) + total.total(h, i, 32)
+                r.residual[rows, :] = v
+                s = lax.rsqrt(jnp.mean(v * v, axis=-1, keepdims=True) + NORM_EPS)
+                r.normed[mine, rows, :] = (v * s * gain2).astype(BF)
+
+            loop(2, residual_rows)
+        acts.start(part)
 
     def gate_up(which):
         return r.wgu_all[:, which * 128 : (which + 1) * 128, :].reshape(-1, cols)
@@ -995,23 +1020,27 @@
         for i in range(4):
             r.gd[i, :, lanes] = value[i * piece : (i + 1) * piece, :]
     mlp_d = LineSum(net, lambda t: r.gd.at[t], lambda k: r.gd_in.at[k - 1])
-    back.finish()
     sums = jnp.zeros((8, r.x.shape[1]), F32)
-    for h in range(2):
-
-        def residual_back(i, sums, h=h):
-            rows = pl.ds(pl.multiple_of(h * 128 + i * 32, 32), 32)
-            v = r.residual[rows, :]
-            dn = back.total(h, i, 32)
-            s = lax.rsqrt(jnp.mean(v * v, axis=-1, keepdims=True) + NORM_EPS)
-            u = dn * gain2
-            pulled = s * u - v * (s * s * s * jnp.mean(u * v, axis=-1, keepdims=True))
-            d_res = r.g_all[mine, rows, :].astype(F32) + pulled
-            r.d_res[rows, :] = d_res
-            r.do_all[mine, rows, :] = d_res.astype(BF)
-            return sums + jnp.sum((dn * v * s).reshape(4, 8, -1), axis=0)
-
-        sums = lax.fori_loop(0, 4, residual_back, sums)
+    grads = Gather(net, r.do_all.at[mine], r.do_all, cots.at)
+    for part in range(2):
+        back.finish(part)
+        for h in range(2):
+
+            def residual_back(i, sums, h=h, part=part):
+                i = part * 2 + i
+                rows = pl.ds(pl.multiple_of(h * 128 + i * 32, 32), 32)
+                v = r.residual[rows, :]
+                dn = back.total(h, i, 32)
+                s = lax.rsqrt(jnp.mean(v * v, axis=-1, keepdims=True) + NORM_EPS)
+                u = dn * gain2
+                pulled = s * u - v * (s * s * s * jnp.mean(u * v, axis=-1, keepdims=True))
+                d_res = r.g_all[mine, rows, :].astype(F32) + pulled
+                r.d_res[rows, :] = d_res
+                r.do_all[mine, rows, :] = d_res.astype(BF)
+                return sums + jnp.sum((dn * v * s).reshape(4, 8, -1), axis=0)
+
+            sums = lax.fori_loop(0, 2, residual_back, sums)
+        grads.start(part)
     r.gain2_sum[...] = sums
 
     owners, returned = [], []
@@ -1026,17 +1055,14 @@
     def vector_copy(k):
         return net.describe(r.vout.at[p], r.vout.at[p], net.plane(k, c), fo_at + k, fo_at)
 
-    owners_m = Owners(net, r.gm_sum, r.fm, r.fm_x)
+    owners_m = Owners(net, r.gm_sum, r.fm, r.fm_x, tokens.at)
     owners_d = Owners(net, r.gd_sum, r.fd)
-    owners_a = Owners(net, r.ga_sum, r.fa, r.fa_x)
+    owners_a = Owners(net, r.ga_sum, r.fa, r.fa_x, cots.at)
     owners_b = Owners(net, r.gb2_sum, r.fb)
 
     def mlp_sums():
         mlp_m.end(r.gm_sum)
         owners_m.start()
-
-    grads = Gather(net, r.do_all.at[mine], r.do_all, cots.at)
-    grads.start()
 
     def back_out(slot):
         b, half = lax.div(slot, 2), lax.rem(slot, 2)
@@ -1212,7 +1238,8 @@
             r.vec[n, j] = r.vec[n, j] + sums[j]
 
     loop(8, conv_back)
-    out.finish()
+    out.finish(0)
+    out.finish(1)
     for h in range(2):
 
         def out_rows(i, h=h):
@@ -1277,7 +1304,8 @@
     sum_a.relay()
     sum_b.relay()
     go_line.relay()
-    first_back.finish()
+    first_back.finish(0)
+    first_back.finish(1)
     sums = jnp.zeros((8, r.x.shape[1]), F32)
     for h in range(2):
 
@@ -1868,7 +1896,7 @@
             free=pltpu.SemaphoreType.REGULAR,
             **reduce_scratch(256, 1024),
         ),
-        176,
+        166,
         36,
         (
             "g", "wg", "wi", "wr", "wv", "wout", "wmg", "wmu", "wmd", "d_in", "block_out", "fm", "fm_x", "fd", "fa", "fa_x", "fb", "fo",

time: 225 us -> 220 us (0.978)
  Pallas kernels: 220 us -> 214 us
    pallas_call x2, Pallas kernels: 220 us -> 214 us  [kernel_call(): pl.pallas_call(kernel, out_shape=list(outs.values()), in_specs=[away if n...]
where the time goes in v5:
time: 220 us; the launch traced here: 216 us
  Pallas kernels  214 us (97%)
    pallas_call x2, Pallas kernels, kernel_call(): pl.pallas_call(kernel, out_shape=list(outs.values()), in_specs=[away if n...  214 us

profile of v5, /device:TPU:19, one launch (start us, length us, event | category | flops | bytes accessed | tf_op | source)
XLA Modules:
  0.0 215.6 jit_solution(18226668301848958266)
XLA Ops:
  0.7 207.8 %layer.1 = (bf16[256,1024]{1,0:T(8,128)(2,1)}, f32[256,1024]{1,0:T(8,128)}, bf16[4,256,768]{2,1,0:T(8,128)(2,1)}, bf16[4,128,768]{2,1,0:T(8,128)(2,1)}, bf16[4,9...) custom-call(bf16[256,1024]{1,0:T(8,128)(2,1)} %bitcast.11, ...), custom_call_target="tpu_custom_call" | custom-call | tf_op jit(solution)/shard_map/layer/pallas_call | solution.py:456
  208.5 6.7 %assemble.1 = (f32[256,1024]{1,0:T(8,128)}, bf16[256,1024]{1,0:T(8,128)(2,1)}, f32[128,1536]{1,0:T(8,128)}, f32[128,1536]{1,0:T(8,128)}, f32[128,3072]{1,0:T(8,1...) custom-call(f32[256,1024]{1,0:T(8,128)} %get-tuple-element.48.refs_0, ...), custom_call_target="tpu_custom_call" | custom-call | tf_op jit(solution)/shard_map/assemble/pallas_call | solution.py:456

commit v6 on v5

--- a/solution.py
+++ b/solution.py
@@ -287,9 +287,9 @@
 
 
 class LineSum:
-    def __init__(self, net, block, slot):
+    def __init__(self, net, block, slot, at=None):
         self.net, self.block, self.slot = net, block, slot
-        self.at = net.reserve(3)
+        self.at = net.reserve(3) if at is None else at
 
     def made(self, k):
         net = self.net
@@ -456,8 +456,8 @@
     results = pl.pallas_call(
         kernel,
         out_shape=list(outs.values()),
-        in_specs=[away if name in far else near for name in ins],
-        out_specs=[away if name in far else near for name in outs],
+        in_specs=[away if far is None or name in far else near for name in ins],
+        out_specs=[away if far is None or name in far else near for name in outs],
         scratch_shapes=shapes,
         compiler_params=pltpu.CompilerParams(**params),
         name=body.__name__,
@@ -554,17 +554,18 @@
     r.do_all = r.x_all
     r.dconv = r.gb
     r.dgi = r.dgu
-    r.ug, r.ul = r.d_res.at[:, 0:384], r.d_res.at[:, 384:768]
+    r.up = r.d_res.at[:, 0:768]
     r.ga = [r.hid.at[i, :, 0:256] for i in range(4)]
     r.gb2 = [r.hid.at[4 + i, 0:128, 0:256] for i in range(4)]
     net = Net(r)
     p, z, c, o, q = net.p, net.z, net.c, net.o, net.q
     sibling = net.plane(0, o)
     mine = net.slot(0, c)
-    cols = r.wgu_out.shape[2]
+    cols = r.wgu_out.shape[2] // 2
     piece = cols // 4
     down = pl.ds(pl.multiple_of(p * piece, 16), piece)
     quarter = pl.ds(pl.multiple_of(p * 48, 16), 48)
+    x_here = net.local(r.x_in, r.x)
     staged = []
     for j in range(8):
         lanes = pl.ds(j * cols, cols)
@@ -598,6 +599,7 @@
     small = [net.copy(r.small, r.small_all.at[q], net.line(net.up(k), core)) for k in (1, 2, 3) for core in (c, o)]
     small.append(net.copy(r.small, r.small_all.at[q], sibling))
     lens = [net.copy(r.lens_out, r.lens_all.at[p], net.plane(k, c)) for k in (1, 2, 3)]
+    x_here.wait()
     tokens = Gather(net, r.x, r.x_all)
     tokens.start(0)
     tokens.start(1)
@@ -662,7 +664,7 @@
             for part in range(4):
                 term = dot(r.hid[part * 2 + core, rows, :], selects[part])
                 picked = term if picked is None else picked + term
-            r.wgu_out[core, rows, :] = picked.astype(BF)
+            r.wgu_out[core, :, which * cols : (which + 1) * cols] = picked.astype(BF)
     for made in small + lens:
         made.wait_recv()
     low, high = r.small_all[2 * p].astype(F32), r.small_all[2 * p + 1].astype(F32)
@@ -869,6 +871,8 @@
         made.wait_send()
     heads_in.drain()
     heads_gate.drain()
+    gates_in.drain()
+    out_in.drain()
     for k in (2, 1, 3):
         feed_down.start(k, (0,))
     for slot in range(8):
@@ -950,25 +954,23 @@
             loop(2, residual_rows)
         acts.start(part)
 
-    def gate_up(which):
-        return r.wgu_all[:, which * 128 : (which + 1) * 128, :].reshape(-1, cols)
+    def gate_up():
+        return r.wgu_all[...].reshape(-1, 2 * cols)
 
     def d_normed2(k, core):
-        slot = net.slot(k, core)
-        return dot(r.dgu[slot, :, 0:cols], gate_up(0), NT) + dot(r.dgu[slot, :, cols:], gate_up(1), NT)
+        return dot(r.dgu[net.slot(k, core)], gate_up(), NT)
 
     back = Reduce(net, r, d_normed2, total.at)
 
     def part(k, core):
         slot = net.slot(k, core)
         h = n2_all[slot]
-        r.ug[...] = dot(h, gate_up(0))
-        r.ul[...] = dot(h, gate_up(1))
+        r.up[...] = dot(h, gate_up())
 
         def body(i):
             rows = pl.ds(pl.multiple_of(i * 32, 32), 32)
-            gelu, slope = gelu_parts(r.ug[rows, :])
-            ul, dh = r.ul[rows, :], r.dgu[slot, rows, 0:cols].astype(F32)
+            gelu, slope = gelu_parts(r.up[rows, 0:cols])
+            ul, dh = r.up[rows, cols:], r.dgu[slot, rows, 0:cols].astype(F32)
             r.hid[slot, rows, :] = (gelu * ul).astype(BF)
             r.dgu[slot, rows, 0:cols] = (dh * ul * slope).astype(BF)
             r.dgu[slot, rows, cols:] = (dh * gelu).astype(BF)
@@ -1019,7 +1021,7 @@
         value = dot(hid, r.g_all[:, :, lanes].reshape(-1, 512), TN).astype(BF)
         for i in range(4):
             r.gd[i, :, lanes] = value[i * piece : (i + 1) * piece, :]
-    mlp_d = LineSum(net, lambda t: r.gd.at[t], lambda k: r.gd_in.at[k - 1])
+    mlp_d = LineSum(net, lambda t: r.gd.at[t], lambda k: r.gd_in.at[k - 1], out_in.at)
     sums = jnp.zeros((8, r.x.shape[1]), F32)
     grads = Gather(net, r.do_all.at[mine], r.do_all, cots.at)
     for part in range(2):
@@ -1124,7 +1126,6 @@
         return [net.copy(r.go.at[go_rows[k], lanes], go_in.at[p, :, lanes], net.plane(k, c)) for k in (1, 2, 3)]
 
     go_out = go_start(pl.ds(0, 1024))
-    mlp_sums()
     entering_states(r, net, ends, 1, True)
     r.vec[...] = jnp.zeros((2, 8, 8, 128), F32)
     dri = r.normed
@@ -1170,6 +1171,7 @@
             r.vec[n, 5 + j] = r.vec[n, 5 + j] + sums[j]
 
     loop(8, second_pass)
+    mlp_sums()
 
     def gate_back(i):
         s, half = lax.div(i, 2), lax.rem(i, 2)
@@ -1274,8 +1276,8 @@
     def gb_in(k):
         return r.g_all.at[3 + k, pl.ds(128, 128), pl.ds(0, 256)]
 
-    sum_a = LineSum(net, lambda t: r.hid.at[t, :, 0:256], ga_in)
-    sum_b = LineSum(net, lambda t: r.hid.at[4 + t, 0:128, 0:256], gb_in)
+    sum_a = LineSum(net, lambda t: r.hid.at[t, :, 0:256], ga_in, heads_in.at)
+    sum_b = LineSum(net, lambda t: r.hid.at[4 + t, 0:128, 0:256], gb_in, heads_gate.at)
     sum_a.start()
     sum_b.start()
     mlp_d.relay()
@@ -1294,7 +1296,7 @@
     go_in[p] = r.go[go_rows[0], :]
     for made in go_out:
         made.wait_recv()
-    go_line = LineSum(net, lambda t: go_in.at[t], lambda k: go_line_in.at[k - 1])
+    go_line = LineSum(net, lambda t: go_in.at[t], lambda k: go_line_in.at[k - 1], gates_in.at)
     go_line.start()
     first_back.relay()
     mlp_d.end(r.gd_sum)
@@ -1404,8 +1406,6 @@
     def _():
         edge_back_copy().wait_send()
 
-    gates_in.drain()
-    out_in.drain()
     feed.drain()
     feed_down.drain()
     for made in (mlp_m, mlp_d, go_line, sum_a, sum_b):
@@ -1437,20 +1437,8 @@
         for made in loads[which]:
             made.wait()
 
+    little = [start(r.vec_in, r.v_vec), start(r.gains, r.v_gains), start(r.fr, r.v_fr), start(r.lens, r.v_lens)]
     passed = [start(r.d_in, r.v_din), start(r.block_out, r.v_block)]
-    vec = r.vec_in[...]
-    vec = lax.select(c == 0, vec[:, 0:192], vec[:, 64:256])
-    r.o_cw[...] = vec[0:4]
-    for j, out in enumerate((r.o_cb, r.o_rb, r.o_ib, r.o_lam)):
-        out[...] = vec[4 + j : 5 + j]
-    r.o_ngain[...] = r.gains[0:1, :]
-    r.o_mgain[...] = r.gains[1:2, :]
-    counts = [jnp.broadcast_to(r.lens[0:1, row : row + 1].astype(F32), (1, 128)) for row in range(5)]
-    for chip in range(4):
-        for half, (slot, n) in enumerate(((chip * 2, 0), (chip * 2, 1), (chip * 2 + 1, 1))):
-            at = chip * 384 + half * 128
-            for row in range(5):
-                r.o_mean[row, :, at : at + 128] = r.fr[slot, n, row : row + 1, :] / counts[row]
     cols = r.fm.shape[2] // 2
     piece = cols // 4
     loaded(0)
@@ -1480,13 +1468,33 @@
     for chip in range(4):
         r.s_down[chip * piece : (chip + 1) * piece, :] = r.vd[chip].astype(F32)
     stores.append(start(r.s_down, r.o_mdown))
+    for made in little:
+        made.wait()
+    vec = r.v_vec[...]
+    vec = lax.select(c == 0, vec[:, 0:192], vec[:, 64:256])
+    r.s_cw[...] = vec[0:4]
+    stores.append(start(r.s_cw, r.o_cw))
+    for j, (stage, out) in enumerate(((r.s_cb, r.o_cb), (r.s_rb, r.o_rb), (r.s_ib, r.o_ib), (r.s_lam, r.o_lam))):
+        stage[...] = vec[4 + j : 5 + j]
+        stores.append(start(stage, out))
+    for j, (stage, out) in enumerate(((r.s_ngain, r.o_ngain), (r.s_mgain, r.o_mgain))):
+        stage[...] = r.v_gains[j : j + 1, :]
+        stores.append(start(stage, out))
+    counts = [jnp.broadcast_to(r.v_lens[0:1, row : row + 1].astype(F32), (1, 128)) for row in range(5)]
+    for chip in range(4):
+        for half, (slot, n) in enumerate(((chip * 2, 0), (chip * 2, 1), (chip * 2 + 1, 1))):
+            at = chip * 384 + half * 128
+            for row in range(5):
+                r.s_mean[row, :, at : at + 128] = r.v_fr[slot, n, row : row + 1, :] / counts[row]
+    stores.append(start(r.s_mean, r.o_mean))
     loaded(3)
     for chip in range(4):
         rows = slice(chip * 48, (chip + 1) * 48)
         r.s_out[rows, :] = r.vo[chip, :, 0:1024].astype(F32)
-        r.o_r[rows, :] = r.vo[chip, :, 1024:1152].astype(F32)
-        r.o_i[rows, :] = r.vo[chip, :, 1152:1280].astype(F32)
-    stores.append(start(r.s_out, r.o_out))
+        r.s_r[rows, :] = r.vo[chip, :, 1024:1152].astype(F32)
+        r.s_i[rows, :] = r.vo[chip, :, 1152:1280].astype(F32)
+    for stage, out in ((r.s_out, r.o_out), (r.s_r, r.o_r), (r.s_i, r.o_i)):
+        stores.append(start(stage, out))
     for made in stores:
         made.wait()
 
@@ -1814,7 +1822,7 @@
     done = kernel_call(
         layer,
         dict(
-            x=inputs[0], cw=conv_w, cb=conv_b, br=b_rgate, bi=b_igate, lam=lam, ngain=norm_gain, mgain=mlp_gain,
+            x_in=inputs[0], cw=conv_w, cb=conv_b, br=b_rgate, bi=b_igate, lam=lam, ngain=norm_gain, mgain=mlp_gain,
             lens=row_lengths, g=out_grad[0], wg=w_gate, wi=w_in, wr=w_rgate, wv=w_igate, wout=w_out,
             wmg=w_mlp_gate, wmu=w_mlp_up, wmd=w_mlp_down,
         ),
@@ -1834,6 +1842,7 @@
             normed_far=array(8, 256, 1024, dtype=BF),
         ),
         dict(
+            x=vmem((256, 1024), BF),
             x_all=vmem((8, 256, 1024), BF),
             normed=vmem((8, 256, 1024), BF),
             g_all=vmem((8, 256, 1024), BF),
@@ -1854,8 +1863,8 @@
             wri=vmem((2, 128, 256), BF),
             w3=vmem((2, 192, 1024), BF),
             wo=vmem((256, 1024), BF),
-            wgu_out=vmem((2, 256, 384), BF),
-            wgu_all=vmem((8, 256, 384), BF),
+            wgu_out=vmem((2, 128, 768), BF),
+            wgu_all=vmem((8, 128, 768), BF),
             wmd_all=vmem((4, 96, 1024), BF),
             gp=vmem((8, 512, 128), F32),
             gb=vmem((8, 520, 128), F32),
@@ -1896,10 +1905,10 @@
             free=pltpu.SemaphoreType.REGULAR,
             **reduce_scratch(256, 1024),
         ),
-        166,
-        36,
+        154,
+        37,
         (
-            "g", "wg", "wi", "wr", "wv", "wout", "wmg", "wmu", "wmd", "d_in", "block_out", "fm", "fm_x", "fd", "fa", "fa_x", "fb", "fo",
+            "x_in", "g", "wg", "wi", "wr", "wv", "wout", "wmg", "wmu", "wmd", "d_in", "block_out", "fm", "fm_x", "fd", "fa", "fa_x", "fb", "fo",
             "fr", "normed_far",
         ),
     )
@@ -1943,13 +1952,24 @@
             s_in=vmem((128, 1536), F32),
             s_down=vmem((384, 1024), F32),
             s_out=vmem((192, 1024), F32),
+            s_r=vmem((192, 128), F32),
+            s_i=vmem((192, 128), F32),
+            s_cw=vmem((4, 192), F32),
+            s_cb=vmem((1, 192), F32),
+            s_rb=vmem((1, 192), F32),
+            s_ib=vmem((1, 192), F32),
+            s_lam=vmem((1, 192), F32),
+            s_ngain=vmem((1, 128), F32),
+            s_mgain=vmem((1, 128), F32),
+            s_mean=vmem((5, 1, 1536), F32),
+            v_vec=vmem((8, 256), F32),
+            v_gains=vmem((8, 128), F32),
+            v_fr=vmem((8, 2, 8, 128), F32),
+            v_lens=vmem((1, 5), jnp.int32),
         ),
         0,
-        23,
-        (
-            "d_in", "block_out", "fm", "fm_x", "fd", "fa", "fa_x", "fb", "fo", "o_din", "o_block", "o_gate", "o_in", "o_mgate", "o_mup",
-            "o_mdown", "o_out",
-        ),
+        37,
+        None,
     )
     return (
         out["o_block"][None],

time: 220 us -> 214 us (0.973); the launches traced: 216 us -> 213 us
  no operation moved by 1% of the time
where the time goes in v6:
time: 214 us; the launch traced here: 213 us
  Pallas kernels  212 us (99%)
    pallas_call x2, Pallas kernels, kernel_call(): pl.pallas_call(kernel, out_shape=list(outs.values()), in_specs=[away if f...  212 us

profile of v6, /device:TPU:19, one launch (start us, length us, event | category | flops | bytes accessed | tf_op | source)
XLA Modules:
  0.0 213.2 jit_solution(8828801061451931659)
XLA Ops:
  0.7 207.0 %layer.1 = (bf16[256,1024]{1,0:T(8,128)(2,1)}, f32[256,1024]{1,0:T(8,128)}, bf16[4,256,768]{2,1,0:T(8,128)(2,1)}, bf16[4,128,768]{2,1,0:T(8,128)(2,1)}, bf16[4,9...) custom-call(bf16[256,1024]{1,0:T(8,128)(2,1)} %bitcast.11, ...), custom_call_target="tpu_custom_call" | custom-call | tf_op jit(solution)/shard_map/layer/pallas_call | solution.py:456
  207.7 5.3 %assemble.1 = (f32[256,1024]{1,0:T(8,128)}, bf16[256,1024]{1,0:T(8,128)(2,1)}, f32[128,1536]{1,0:T(8,128)}, f32[128,1536]{1,0:T(8,128)}, f32[128,3072]{1,0:T(8,1...) custom-call(f32[256,1024]{1,0:T(8,128)} %get-tuple-element.48.refs_0, ...), custom_call_target="tpu_custom_call" | custom-call | tf_op jit(solution)/shard_map/assemble/pallas_call | solution.py:456

commit v7 on v6

--- a/solution.py
+++ b/solution.py
@@ -167,14 +167,15 @@
 
 
 class Owners:
-    def __init__(self, net, own, everything, extra=None, at=None):
+    def __init__(self, net, own, everything, extra=None, at=None, cut=None):
         self.net, self.own, self.all, self.extra = net, own, everything, extra
         self.at = net.reserve(6 if extra is None else 10) if at is None else at
-        self.half = everything.shape[1] // 2
+        self.half = everything.shape[1] // 2 if cut is None else cut
+        self.rows = (pl.ds(0, self.half), pl.ds(self.half, everything.shape[1] - self.half))
         self.s = [None] * 4
 
     def part(self, k, h):
-        return self.all.at[self.net.near[k], pl.ds(h * self.half, self.half)]
+        return self.all.at[self.net.near[k], self.rows[h]]
 
     def across(self, k, block):
         if self.extra is not None:
@@ -184,7 +185,7 @@
 
     def start(self):
         net = self.net
-        low, high = self.own.at[pl.ds(0, self.half)], self.own.at[pl.ds(self.half, self.half)]
+        low, high = self.own.at[self.rows[0]], self.own.at[self.rows[1]]
         self.x0 = net.copy(low, self.part(0, 0), net.plane(1, net.c), None, self.at + 0)
         self.y1 = net.copy(high, self.part(0, 1), net.plane(2, net.c), None, self.at + 1)
         self.x1 = net.copy(high, self.part(0, 1), net.plane(1, net.c), None, self.at + 2)
@@ -594,10 +595,9 @@
         r.small_rows[10:11, at : at + 128] = ref[...].astype(F32).reshape(1, 128)
     r.small[...] = r.small_rows[...].astype(BF)
     net.greet()
-    r.small_all[q] = r.small[...]
+    r.small_all[c, z] = r.small[...]
     r.lens_all[p] = r.lens_out[...]
-    small = [net.copy(r.small, r.small_all.at[q], net.line(net.up(k), core)) for k in (1, 2, 3) for core in (c, o)]
-    small.append(net.copy(r.small, r.small_all.at[q], sibling))
+    small = [net.copy(r.small, r.small_all.at[c, z], net.line(net.up(k), c)) for k in (1, 2, 3)]
     lens = [net.copy(r.lens_out, r.lens_all.at[p], net.plane(k, c)) for k in (1, 2, 3)]
     x_here.wait()
     tokens = Gather(net, r.x, r.x_all)
@@ -648,6 +648,9 @@
             made.wait_recv()
         return net.copy(dst.at[c], dst.at[c], sibling)
 
+    for made in small:
+        made.wait_recv()
+    small_over = net.copy(r.small_all.at[c], r.small_all.at[c], sibling)
     selects = []
     k_at = lax.broadcasted_iota(jnp.int32, (cols, cols), 0)
     j_at = lax.broadcasted_iota(jnp.int32, (cols, cols), 1)
@@ -665,9 +668,10 @@
                 term = dot(r.hid[part * 2 + core, rows, :], selects[part])
                 picked = term if picked is None else picked + term
             r.wgu_out[core, :, which * cols : (which + 1) * cols] = picked.astype(BF)
-    for made in small + lens:
+    for made in lens:
         made.wait_recv()
-    low, high = r.small_all[2 * p].astype(F32), r.small_all[2 * p + 1].astype(F32)
+    small_over.wait_recv()
+    low, high = r.small_all[0, p].astype(F32), r.small_all[1, p].astype(F32)
     at_first = jnp.concatenate([low[:, :192], high[:, :64]], axis=1)
     at_second = jnp.concatenate([low[:, 128:192], high[:, :192]], axis=1)
     both = lax.select(c == 0, at_first, at_second)
@@ -682,7 +686,7 @@
         r.chan[n, 7:8, :] = rate
         r.chan[n, 8:9, :] = jax.nn.sigmoid(lam)
     for i in range(8):
-        gains = r.small_all[i].astype(F32)[10:11, :]
+        gains = r.small_all[i % 2, i // 2].astype(F32)[10:11, :]
         r.gain[0:1, i * 128 : (i + 1) * 128] = gains[:, 0:128]
         r.gain[1:2, i * 128 : (i + 1) * 128] = gains[:, 128:256]
     gain = r.gain[0:1, :]
@@ -860,9 +864,8 @@
     cots.forward()
     ends = scan_slabs(r.dec, r.drv, False)
     ends = exchange_ends(r, net, ends, 0)
-    feed.start(2, (1,))
-    feed.start(1, (0, 1))
-    feed.start(3, (0, 1))
+    for k in (2, 1, 3):
+        feed_down.start(k, (0,))
     r.wgu_all[q] = r.wgu_out[c]
     feed_over = net.copy(r.wgu_out.at[o], r.wgu_all.at[q], sibling)
     hand_over(heads_gate, wg_rows, heads_gate_over)
@@ -873,8 +876,9 @@
     heads_gate.drain()
     gates_in.drain()
     out_in.drain()
-    for k in (2, 1, 3):
-        feed_down.start(k, (0,))
+    feed.start(2, (1,))
+    feed.start(1, (0, 1))
+    feed.start(3, (0, 1))
     for slot in range(8):
         project_gate(slot)
 
@@ -954,6 +958,7 @@
             loop(2, residual_rows)
         acts.start(part)
 
+    owners, returned = [], []
     def gate_up():
         return r.wgu_all[...].reshape(-1, 2 * cols)
 
@@ -996,6 +1001,14 @@
     acts.sibling(2)
     part(2, o)
     back.other(2)
+    for made in row_sums:
+        made.wait_recv()
+    r.rows_sum[...] = r.rs_all[0] + r.rs_all[1] + r.rs_all[2] + r.rs_all[3]
+    for k in (1, 2, 3):
+        for core in (c, o):
+            owners.append(net.copy(r.rows_sum.at[pl.ds(net.near[k] * 2, 2)], r.fr.at[mine], net.plane(k, core)))
+    owners.append(net.copy(r.rows_sum.at[pl.ds(p * 2, 2)], r.fr.at[mine], sibling))
+    returned.append(net.local(r.rows_sum.at[pl.ds(p * 2, 2)], r.fr.at[mine]))
     back.near()
     acts.last()
     acts.sibling(3)
@@ -1045,12 +1058,6 @@
         grads.start(part)
     r.gain2_sum[...] = sums
 
-    owners, returned = [], []
-
-    def to_chips(src, dst):
-        for k in (1, 2, 3):
-            owners.append(net.copy(src, dst.at[p], net.plane(k, c)))
-        returned.append(net.local(src, dst.at[p]))
 
     fo_at = net.reserve(4)
 
@@ -1061,6 +1068,7 @@
     owners_d = Owners(net, r.gd_sum, r.fd)
     owners_a = Owners(net, r.ga_sum, r.fa, r.fa_x, cots.at)
     owners_b = Owners(net, r.gb2_sum, r.fb)
+    owners_o = Owners(net, r.go_sum, r.fo, cut=32)
 
     def mlp_sums():
         mlp_m.end(r.gm_sum)
@@ -1341,14 +1349,6 @@
         for core in (c, o)
     ]
     gain_line.append(net.copy(r.gsum.at[z * 2 + o], r.gline.at[q], sibling))
-    for made in row_sums:
-        made.wait_recv()
-    r.rows_sum[...] = r.rs_all[0] + r.rs_all[1] + r.rs_all[2] + r.rs_all[3]
-    for k in (1, 2, 3):
-        for core in (c, o):
-            owners.append(net.copy(r.rows_sum.at[pl.ds(net.near[k] * 2, 2)], r.fr.at[mine], net.plane(k, core)))
-    owners.append(net.copy(r.rows_sum.at[pl.ds(p * 2, 2)], r.fr.at[mine], sibling))
-    returned.append(net.local(r.rows_sum.at[pl.ds(p * 2, 2)], r.fr.at[mine]))
     for made in vec:
         made.wait_recv()
     r.vout[p] = r.vsum[0] + r.vsum[1] + r.vsum[2] + r.vsum[3]
@@ -1363,11 +1363,12 @@
     sum_b.end(r.gb2_sum)
     owners_b.start()
     go_line.end(r.go_sum)
-    to_chips(r.go_sum, r.fo)
+    owners_o.start()
     owners_d.forward()
     owners_m.last()
     owners_a.forward()
     owners_b.forward()
+    owners_o.forward()
     for made in gain_line:
         made.wait_recv()
     sums = r.gline[0]
@@ -1388,9 +1389,10 @@
     owners_d.middle()
     owners_a.middle()
     owners_b.middle()
-    for each in (owners_d, owners_a, owners_b):
+    owners_o.middle()
+    for each in (owners_d, owners_a, owners_b, owners_o):
         each.last()
-    for each in (owners_m, owners_d, owners_a, owners_b):
+    for each in (owners_m, owners_d, owners_a, owners_b, owners_o):
         each.end()
     for made in owners + gain_plane:
         made.wait_recv()
@@ -1848,7 +1850,7 @@
             g_all=vmem((8, 256, 1024), BF),
             small_rows=vmem((16, 256), F32),
             small=vmem((16, 256), BF),
-            small_all=vmem((8, 16, 256), BF),
+            small_all=vmem((2, 4, 16, 256), BF),
             lens_out=vmem((8, 128), F32),
             lens_all=vmem((4, 8, 128), F32),
             off=vmem((4, 520, 128), F32),

time: 214 us -> 212 us (level)
    pallas_call x2, Pallas kernels: 212 us -> 210 us  [kernel_call(): pl.pallas_call(kernel, out_shape=list(outs.values()), in_specs=[away if f...]
where the time goes in v7:
time: 212 us; the launch traced here: 210 us
  Pallas kernels  210 us (99%)
    pallas_call x2, Pallas kernels, kernel_call(): pl.pallas_call(kernel, out_shape=list(outs.values()), in_specs=[away if f...  210 us

profile of v7, /device:TPU:19, one launch (start us, length us, event | category | flops | bytes accessed | tf_op | source)
XLA Modules:
  0.0 210.5 jit_solution(10836253349731237177)
XLA Ops:
  0.7 204.3 %layer.1 = (bf16[256,1024]{1,0:T(8,128)(2,1)}, f32[256,1024]{1,0:T(8,128)}, bf16[4,256,768]{2,1,0:T(8,128)(2,1)}, bf16[4,128,768]{2,1,0:T(8,128)(2,1)}, bf16[4,9...) custom-call(bf16[256,1024]{1,0:T(8,128)(2,1)} %bitcast.11, ...), custom_call_target="tpu_custom_call" | custom-call | tf_op jit(solution)/shard_map/layer/pallas_call | solution.py:457
  205.0 5.3 %assemble.1 = (f32[256,1024]{1,0:T(8,128)}, bf16[256,1024]{1,0:T(8,128)(2,1)}, f32[128,1536]{1,0:T(8,128)}, f32[128,1536]{1,0:T(8,128)}, f32[128,3072]{1,0:T(8,1...) custom-call(f32[256,1024]{1,0:T(8,128)} %get-tuple-element.48.refs_0, ...), custom_call_target="tpu_custom_call" | custom-call | tf_op jit(solution)/shard_map/assemble/pallas_call | solution.py:457

commit v8 on v7

--- a/solution.py
+++ b/solution.py
@@ -534,6 +534,30 @@
         r.tot[at, net.z, 1, s : s + 1, :] = ends[s][1][0:1, :]
     mine = r.tot.at[at, net.z]
     return [net.copy(mine, mine, net.line(net.up(k), net.c)) for k in (1, 2, 3)]
+
+
+class Onward:
+    def __init__(self, r, net, ends):
+        self.r, self.net = r, net
+        self.at = net.reserve(3)
+        for s in range(8):
+            r.tot[0, net.z, 0, s : s + 1, :] = ends[s][0][0:1, :]
+            r.tot[0, net.z, 1, s : s + 1, :] = ends[s][1][0:1, :]
+        for k in (1, 2, 3):
+            pl.when(net.z + k <= 3)(lambda k=k: self.made(k).start())
+
+    def made(self, k):
+        net = self.net
+        mine = self.r.tot.at[0, net.z]
+        return net.describe(mine, mine, net.line(net.up(k), net.c), self.at + k - 1, self.at + k - 1)
+
+    def wait_recv(self):
+        for k in (1, 2, 3):
+            pl.when(self.net.z >= k)(lambda k=k: self.made(k).wait_recv())
+
+    def drain(self):
+        for k in (1, 2, 3):
+            pl.when(self.net.z + k <= 3)(lambda k=k: self.made(k).wait_send())
 
 
 def entering_states(r, net, copies, at, reverse):
@@ -594,6 +618,7 @@
     for at, ref in ((0, r.ngain), (128, r.mgain)):
         r.small_rows[10:11, at : at + 128] = ref[...].astype(F32).reshape(1, 128)
     r.small[...] = r.small_rows[...].astype(BF)
+    r.tot[0] = jnp.zeros(r.tot.shape[1:], F32)
     net.greet()
     r.small_all[c, z] = r.small[...]
     r.lens_all[p] = r.lens_out[...]
@@ -863,7 +888,7 @@
     loop(4, terms)
     cots.forward()
     ends = scan_slabs(r.dec, r.drv, False)
-    ends = exchange_ends(r, net, ends, 0)
+    onward = Onward(r, net, ends)
     for k in (2, 1, 3):
         feed_down.start(k, (0,))
     r.wgu_all[q] = r.wgu_out[c]
@@ -890,7 +915,7 @@
 
     loop(64, gelu_tile)
     out_over = share(out_rows_in, r.w3)
-    entering_states(r, net, ends, 0, False)
+    entering_states(r, net, [onward], 0, False)
     row_sums = [net.copy(r.rs_all.at[z], r.rs_all.at[z], net.line(net.up(k), c)) for k in (1, 2, 3)]
     out_over.wait_recv()
 
@@ -1408,6 +1433,7 @@
     def _():
         edge_back_copy().wait_send()
 
+    onward.drain()
     feed.drain()
     feed_down.drain()
     for made in (mlp_m, mlp_d, go_line, sum_a, sum_b):

time: 212 us -> 212 us (level)
  no operation moved by 1% of the time
where the time goes in v8:
time: 212 us; the launch traced here: 210 us
  Pallas kernels  209 us (99%)
    pallas_call x2, Pallas kernels, kernel_call(): pl.pallas_call(kernel, out_shape=list(outs.values()), in_specs=[away if f...  209 us

profile of v8, /device:TPU:19, one launch (start us, length us, event | category | flops | bytes accessed | tf_op | source)
XLA Modules:
  0.0 210.3 jit_solution(4006422296318622998)
XLA Ops:
  0.7 204.1 %layer.1 = (bf16[256,1024]{1,0:T(8,128)(2,1)}, f32[256,1024]{1,0:T(8,128)}, bf16[4,256,768]{2,1,0:T(8,128)(2,1)}, bf16[4,128,768]{2,1,0:T(8,128)(2,1)}, bf16[4,9...) custom-call(bf16[256,1024]{1,0:T(8,128)(2,1)} %bitcast.11, ...), custom_call_target="tpu_custom_call" | custom-call | tf_op jit(solution)/shard_map/layer/pallas_call | solution.py:457
  204.8 5.3 %assemble.1 = (f32[256,1024]{1,0:T(8,128)}, bf16[256,1024]{1,0:T(8,128)(2,1)}, f32[128,1536]{1,0:T(8,128)}, f32[128,1536]{1,0:T(8,128)}, f32[128,3072]{1,0:T(8,1...) custom-call(f32[256,1024]{1,0:T(8,128)} %get-tuple-element.48.refs_0, ...), custom_call_target="tpu_custom_call" | custom-call | tf_op jit(solution)/shard_map/assemble/pallas_call | solution.py:457
